TPU v7x, 128 devices: a whole 4x4x4 slice. The times are simulated.
128 devices in a mesh: dp: 2 (over core), ep: 64 (over z, y, x).
Axes of the slice: x: 4, y: 4, z: 4, core: 2. Of those that a mesh axis runs over, the one named last changes fastest.
Arguments:
- kv_cache: bfloat16 [4096, 36864], P(('dp', 'ep')), may hold values from -6 to 6
- lengths: int32 [4096], P(('dp', 'ep')), may hold values from 1 to 62, as said below
- move_list: int32 [4096, 2], P(('dp', 'ep')), may hold values from 0 to 63, as said below
- queries: bfloat16 [2, 4096, 36864], P(None, ('dp', 'ep')), may hold values from -125 to 125
- new_kv: bfloat16 [2, 4096, 576], P(None, ('dp', 'ep')), may hold values from -6 to 6
- hidden: bfloat16 [2, 4096, 3584], P(None, ('dp', 'ep')), may hold values from -6 to 6
- expert_ids: int32 [2, 4096, 8], P(None, ('dp', 'ep')), may hold values from 0 to 63, all different within a row; in each aligned block of 32 rows (0 to 31, 32 to 63, ..., all dimensions but the last counted through in order) at most 8 rows name the same one
- gate_weights: float32 [2, 4096, 8], P(None, ('dp', 'ep')), may hold values from 0.2 to 1
- expert_gate: bfloat16 [64, 3584, 1024], P('ep', None, 'dp'), may hold values from -0.09375 to 0.09375
- expert_up: bfloat16 [64, 3584, 1024], P('ep', None, 'dp'), may hold values from -0.09375 to 0.09375
- expert_down: bfloat16 [64, 1024, 3584], P('ep', 'dp'), may hold values from -0.1875 to 0.1875
Outputs:
- context: bfloat16 [2, 4096, 32768], P(None, ('dp', 'ep'))
- expert_mix: bfloat16 [2, 4096, 3584], P(None, ('dp', 'ep'))
Inputs may be any that keep to these rules, and one draw needn't show every extreme that they name: `lengths`: each slot's count of cached positions; room is left for the 2 new tokens. `move_list`: destinations lie in the same dp index as the source. Each device sends its 32 requests and receives exactly 32, into distinct slots; between two devices move either none or exactly 1 request. `expert_ids`: in each step, among the 32 tokens of one device no expert is named more than 8 times; a token names 8 different experts.
All inputs are finite; a program needn't handle non-finite values.
Results may differ from a plain program's by a relative error of at most 0.0058.
Values may be sent and summed in bfloat16 or wider, within the bound.
No kernel may reach another device: no remote copies, remote signals or barrier semaphores. Data moves between devices by JAX's collectives and lax.ppermute only.
A program may use at most 192 MiB of HBM per device.

v0:
```python
import jax
import jax.numpy as jnp
from jax import lax
from jax.experimental import pallas as pl
from jax.experimental.pallas import tpu as pltpu
from jax.sharding import PartitionSpec as P

D = 3584
H = 64
LAT = 512
TOPK = 8
STEPS = 2
CTX = 64
KVW = 576
HALF = CTX // 2
GROUP = 16
TOGETHER = 8
WIDE = 640
SIDE = 4
Z, Y, X = SIDE * SIDE, SIDE, 1
MAIN = 2432
MINOR = D - MAIN
MARK = 128
SLOTS = 32
CAPE = 8
ROWS = STEPS * SLOTS
PICKS = STEPS * CAPE
LINE = SIDE * ROWS
PLANE = SIDE * SIDE
CHIPS = SIDE**3
ORDERS = (((Z, Y, X), (Y, X, Z)), ((X, Z, Y), (X, Z, Y)))
TARGETS = (0, 1, -1, 2)
KEYS = GROUP * (CTX + STEPS)


score_scale = 192.0 ** (-0.5)


def attend_kernel(landing_ref, got_ref, len_ref, new_ref, query_ref, out_ref, even_ref, odd_ref, value_ref, bias_ref):
    pairs = GROUP * HALF

    def lanes(rows):
        return lax.broadcasted_iota(jnp.int32, (rows, WIDE), 1)

    def place(keys, rows, at):
        even_ref[pl.ds(at, rows), :] = keys.astype(jnp.bfloat16)
        odd_ref[pl.ds(at, rows), :] = pltpu.roll(keys, WIDE - KVW, 1).astype(jnp.bfloat16)
        value_ref[pl.ds(at, rows), :] = keys[:, :LAT].astype(jnp.bfloat16)

    def one(slot, carry):
        source = landing_ref[slot]
        block = got_ref[source]
        first = jnp.where(lanes(HALF) < KVW, block[:, :WIDE].astype(jnp.float32), 0.0)
        at = pl.multiple_of(slot * HALF, HALF)
        place(first, HALF, at)
        second = block[:, LAT:].astype(jnp.float32)
        second = jnp.where(lanes(HALF) < WIDE - KVW, 0.0, second)
        place(pltpu.roll(second, KVW, 1), HALF, pl.multiple_of(pairs + at, HALF))
        return carry

    lax.fori_loop(0, GROUP, one, 0)
    for step in range(STEPS):
        rows = new_ref[step].astype(jnp.float32)
        rows = jnp.concatenate([rows, jnp.zeros((GROUP, WIDE - KVW), jnp.float32)], axis=1)
        place(rows, GROUP, 2 * pairs + step * GROUP)

    column = lax.broadcasted_iota(jnp.int32, (GROUP, KEYS), 1)
    row = lax.broadcasted_iota(jnp.int32, (GROUP, KEYS), 0)
    cached = column < 2 * pairs
    half = (column >= pairs).astype(jnp.int32)
    within = column - half * pairs
    position = 2 * (within % HALF) + half
    recent = column - 2 * pairs
    owner = jnp.where(cached, within // HALF, recent % GROUP)
    live = cached & (position < len_ref[...])
    for step in range(STEPS):
        allowed = (live | (~cached & (recent < (step + 1) * GROUP))) & (owner == row)
        bias_ref[pl.ds(step * GROUP, GROUP), :] = jnp.where(allowed, 0.0, -jnp.inf)

    def heads(index, carry):
        bias = jnp.concatenate([bias_ref[...]] * TOGETHER, axis=0)
        for odd in range(2):
            slabs = []
            for k in range(TOGETHER):
                start = pl.multiple_of((index * TOGETHER + k) * 2 * KVW + odd * LAT, 128)
                for step in range(STEPS):
                    slabs.append(query_ref[step, :, pl.ds(start, WIDE)])
            keys = odd_ref[...] if odd else even_ref[...]
            score = lax.dot_general(
                jnp.concatenate(slabs, axis=0),
                keys,
                (((1,), (1,)), ((), ())),
                preferred_element_type=jnp.float32,
            )
            score = score * score_scale + bias
            weight = jnp.exp(score - jnp.max(score, axis=1, keepdims=True))
            prob = weight * (1.0 / jnp.sum(weight, axis=1, keepdims=True))
            mixed = jnp.dot(
                prob.astype(jnp.bfloat16), value_ref[...], preferred_element_type=jnp.float32
            ).astype(jnp.bfloat16)
            for k in range(TOGETHER):
                start = pl.multiple_of(((index * TOGETHER + k) * 2 + odd) * LAT, LAT)
                for step in range(STEPS):
                    at = (k * STEPS + step) * GROUP
                    out_ref[step, :, pl.ds(start, LAT)] = mixed[at : at + GROUP]
        return carry

    lax.fori_loop(0, H // (2 * TOGETHER), heads, 0)


def attend(queries, new_kv, got, landing, placed_len, earlier):
    slots = queries.shape[1]
    group = 0 if earlier is None else 1
    specs = [
        pl.BlockSpec(memory_space=pltpu.SMEM),
        pl.BlockSpec(memory_space=pltpu.VMEM),
        pl.BlockSpec((GROUP, 1), lambda g: (group, 0)),
        pl.BlockSpec((STEPS, GROUP, KVW), lambda g: (0, group, 0)),
        pl.BlockSpec((STEPS, GROUP, H * KVW), lambda g: (0, group, 0)),
    ]
    operands = [landing[group * GROUP :][:GROUP], got, placed_len[:, None], new_kv, queries]
    kernel = attend_kernel
    if earlier is not None:
        specs.append(pl.BlockSpec(memory_space=pl.ANY))
        operands.append(earlier)

        def kernel(*refs):
            attend_kernel(*refs[:5], *refs[6:])

    return pl.pallas_call(
        kernel,
        grid=(1,),
        out_shape=jax.ShapeDtypeStruct((STEPS, slots, H * LAT), jnp.bfloat16),
        in_specs=specs,
        out_specs=pl.BlockSpec((STEPS, GROUP, H * LAT), lambda g: (0, group, 0)),
        scratch_shapes=[
            pltpu.VMEM((KEYS, WIDE), jnp.bfloat16),
            pltpu.VMEM((KEYS, WIDE), jnp.bfloat16),
            pltpu.VMEM((KEYS, LAT), jnp.bfloat16),
            pltpu.VMEM((STEPS * GROUP, KEYS), jnp.float32),
        ],
        input_output_aliases={} if earlier is None else {5: 0},
        compiler_params=pltpu.CompilerParams(vmem_limit_bytes=32 * 2**20),
        cost_estimate=pl.CostEstimate(
            flops=2 * STEPS * GROUP * H * KEYS * (WIDE + LAT),
            bytes_accessed=2 * STEPS * GROUP * H * (KVW + LAT),
            transcendentals=STEPS * GROUP * H * KEYS,
        ),
    )(*operands)


def expert_rows(token_rows, row_weight, halves):
    total = None
    for gate_mat, up_mat, down_mat in halves:
        gate_pre = jnp.dot(token_rows, gate_mat, preferred_element_type=jnp.float32)
        up_pre = jnp.dot(token_rows, up_mat, preferred_element_type=jnp.float32)
        inner = (jax.nn.silu(gate_pre) * up_pre).astype(jnp.bfloat16)
        part = jnp.dot(inner, down_mat, preferred_element_type=jnp.float32)
        total = part if total is None else total + part
    return (total * row_weight).astype(jnp.bfloat16)


def hop(value, strides, delta):
    pairs = []
    for core, stride in enumerate(strides):
        for chip in range(CHIPS):
            place = chip // stride % SIDE
            there = chip + ((place + delta) % SIDE - place) * stride
            pairs.append((core * CHIPS + chip, core * CHIPS + there))
    return lax.ppermute(value, ("dp", "ep"), pairs)


def chip_at(stride, delta, start):
    place = start // stride % SIDE
    return start + ((place + delta) % SIDE - place) * stride


def pick_matrix(targets_ref, ids):
    hits = [
        jnp.sum((ids == targets_ref[j].astype(jnp.float32)).astype(jnp.float32), axis=0, keepdims=True)
        for j in range(SIDE)
    ]
    before = lax.broadcasted_iota(jnp.int32, (LINE, LINE), 0)
    after = lax.broadcasted_iota(jnp.int32, (LINE, LINE), 1)
    earlier = ((before // SLOTS == after // SLOTS) & (before < after)).astype(jnp.bfloat16)
    stacked = jnp.concatenate(hits + hits, axis=0).astype(jnp.bfloat16)
    ranks = jnp.dot(stacked, earlier, preferred_element_type=jnp.float32)
    base = (lax.broadcasted_iota(jnp.int32, (1, LINE), 1) // SLOTS * CAPE).astype(jnp.float32)
    rows = lax.broadcasted_iota(jnp.int32, (SIDE * PICKS, LINE), 0).astype(jnp.float32)
    picks = []
    for j in range(SIDE):
        place = jnp.where(hits[j] > 0.0, base + ranks[j : j + 1], -1.0)
        picks.append((rows == place).astype(jnp.float32))
    return jnp.concatenate(picks, axis=0).astype(jnp.bfloat16)


def select_kernel(targets_ref, *refs):
    pieces, outs, ids_ref = refs[:SIDE], refs[SIDE : 2 * SIDE], refs[2 * SIDE]
    width = pieces[0].shape[1]
    for line in range(SIDE):
        piece = pieces[line][...]
        ids = piece[:, width - MARK :].astype(jnp.float32).T[:TOPK]
        ids_ref[line] = ids
        picks = pick_matrix(targets_ref, ids)
        rows = jnp.dot(picks, piece, preferred_element_type=jnp.float32).astype(jnp.bfloat16)
        rows = rows.reshape(SIDE, SIDE, PICKS, width)
        for j in range(SIDE):
            outs[j][pl.ds(line * SIDE, SIDE)] = rows[j]


def select(targets, pieces):
    width = pieces[0].shape[1]
    vmem = pl.BlockSpec(memory_space=pltpu.VMEM)
    return pl.pallas_call(
        select_kernel,
        out_shape=[jax.ShapeDtypeStruct((PLANE, PICKS, width), jnp.bfloat16)] * SIDE
        + [jax.ShapeDtypeStruct((SIDE, TOPK, LINE), jnp.float32)],
        in_specs=[pl.BlockSpec(memory_space=pltpu.SMEM)] + [vmem] * SIDE,
        out_specs=[vmem] * (SIDE + 1),
        compiler_params=pltpu.CompilerParams(vmem_limit_bytes=32 * 2**20),
        cost_estimate=pl.CostEstimate(
            flops=2 * SIDE * LINE * LINE * width, bytes_accessed=4 * SIDE * LINE * width, transcendentals=0
        ),
    )(targets, *pieces)


def combine_kernel(targets_ref, ids_ref, *refs):
    width = refs[0].shape[2]
    for line in range(SIDE):
        picks = pick_matrix(targets_ref, ids_ref[line])
        blocks = [ref[pl.ds(line * SIDE, SIDE)] for ref in refs[:SIDE]]
        rows = jnp.concatenate([b.reshape(SIDE * PICKS, width) for b in blocks], axis=0)
        total = lax.dot_general(
            picks, rows, (((0,), (0,)), ((), ())), preferred_element_type=jnp.float32
        )
        refs[SIDE + line][...] = total.astype(jnp.bfloat16)


def combine(targets, ids, blocks):
    width = blocks[0].shape[2]
    vmem = pl.BlockSpec(memory_space=pltpu.VMEM)
    return pl.pallas_call(
        combine_kernel,
        out_shape=[jax.ShapeDtypeStruct((LINE, width), jnp.bfloat16)] * SIDE,
        in_specs=[pl.BlockSpec(memory_space=pltpu.SMEM)] + [vmem] * (1 + SIDE),
        out_specs=[vmem] * SIDE,
        compiler_params=pltpu.CompilerParams(vmem_limit_bytes=32 * 2**20),
        cost_estimate=pl.CostEstimate(
            flops=2 * SIDE * LINE * LINE * width, bytes_accessed=4 * SIDE * LINE * width, transcendentals=0
        ),
    )(targets, ids, *blocks)


def together(*trees):
    return lax.optimization_barrier(trees)


def stage_axes():
    return [[tuple(by_core[n] for by_core in orders) for orders in ORDERS] for n in range(3)]


def exchange(blocks, strides, deltas):
    return [hop(block, strides, delta) for block, delta in zip(blocks, deltas)]


def send_rows(columns, targets):
    first, second, third = stage_axes()
    both = range(len(columns))
    rings = [exchange([columns[i]] * 3, first[i], (1, -1, 2)) for i in both]
    columns, rings = together(columns, rings)
    lines = [jnp.concatenate([columns[i]] + rings[i], axis=0) for i in both]
    rings = [exchange([lines[i]] * 3, second[i], (1, -1, 2)) for i in both]
    lines, rings = together(lines, rings)
    picked = [select(targets[i], [lines[i]] + rings[i]) for i in both]
    rings = [exchange(picked[i][1:SIDE], third[i], TARGETS[1:]) for i in both]
    return [[picked[i][0]] + rings[i] for i in both], [p[SIDE] for p in picked]


def return_rows(outward, targets, ids, contexts):
    first, second, third = stage_axes()
    both = range(len(outward))
    rings = [exchange(outward[i][1:], third[i], (-1, 1, 2)) for i in both]
    context = contexts(None)
    rings, context = together(rings, context)
    lines = [combine(targets[i], ids[i], [outward[i][0]] + rings[i]) for i in both]
    rings = [exchange(lines[i][1:], second[i], (-1, 1, 2)) for i in both]
    context = contexts(context)
    rings, context = together(rings, context)
    sums = []
    for i in both:
        line = add(lines[i][0], *rings[i])
        blocks = [line[k * ROWS : (k + 1) * ROWS] for k in range(SIDE)]
        sums.append([blocks[0]] + exchange(blocks[1:], first[i], (-1, 1, 2)))
    sums, = together(sums)
    return [add(*terms) for terms in sums], context


def add(*terms):
    return sum(t.astype(jnp.float32) for t in terms).astype(jnp.bfloat16)


def join_kernel(order_ref, *refs):
    main, minor, (rows_ref, mark_ref) = refs[:SIDE], refs[SIDE : 2 * SIDE], refs[2 * SIDE :]

    def one(group, carry):
        for j in range(SIDE):
            number = j * PLANE + group
            rows_ref[number, :, pl.ds(0, MAIN)] = main[j][group, :, pl.ds(0, MAIN)]
            mark_ref[number] = main[j][group, :, pl.ds(MAIN, MARK)]
            rows_ref[order_ref[number], :, pl.ds(MAIN, MINOR)] = minor[j][group, :, pl.ds(0, MINOR)]
        return carry

    lax.fori_loop(0, PLANE, one, 0)


def join_rows(order, main, minor):
    vmem = pl.BlockSpec(memory_space=pltpu.VMEM)
    return pl.pallas_call(
        join_kernel,
        out_shape=[
            jax.ShapeDtypeStruct((CHIPS, PICKS, D), jnp.bfloat16),
            jax.ShapeDtypeStruct((CHIPS, PICKS, MARK), jnp.bfloat16),
        ],
        in_specs=[pl.BlockSpec(memory_space=pltpu.SMEM)] + [vmem] * (2 * SIDE),
        out_specs=[vmem] * 2,
        compiler_params=pltpu.CompilerParams(vmem_limit_bytes=32 * 2**20),
        cost_estimate=pl.CostEstimate(
            flops=0, bytes_accessed=4 * CHIPS * PICKS * D, transcendentals=0
        ),
    )(order, *main, *minor)


def split_kernel(order_ref, rows_ref, *refs):
    main, minor = refs[:SIDE], refs[SIDE:]

    def one(group, carry):
        for j in range(SIDE):
            number = j * PLANE + group
            main[j][group] = rows_ref[number, :, pl.ds(0, MAIN)]
            minor[j][group] = rows_ref[order_ref[number], :, pl.ds(MAIN, MINOR)]
        return carry

    lax.fori_loop(0, PLANE, one, 0)


def split_rows(order, rows):
    vmem = pl.BlockSpec(memory_space=pltpu.VMEM)
    shapes = [(PLANE, PICKS, width) for width in (MAIN, MINOR) for _ in range(SIDE)]
    outs = pl.pallas_call(
        split_kernel,
        out_shape=[jax.ShapeDtypeStruct(shape, jnp.bfloat16) for shape in shapes],
        in_specs=[pl.BlockSpec(memory_space=pltpu.SMEM), vmem],
        out_specs=[vmem] * (2 * SIDE),
        compiler_params=pltpu.CompilerParams(vmem_limit_bytes=32 * 2**20),
        cost_estimate=pl.CostEstimate(
            flops=0, bytes_accessed=4 * CHIPS * PICKS * D, transcendentals=0
        ),
    )(order, rows)
    return outs[:SIDE], outs[SIDE:]


def three_parts(weights):
    high = lax.reduce_precision(weights, 8, 7)
    rest = weights - high
    mid = lax.reduce_precision(rest, 8, 7)
    return [part.astype(jnp.bfloat16) for part in (high, mid, rest - mid)]


def pack_kernel(from_ref, slot_ref, len_ref, cache_ref, out_ref):
    row = lax.broadcasted_iota(jnp.int32, (HALF, 128), 0)
    lane = lax.broadcasted_iota(jnp.int32, (HALF, 128), 1)

    def one(chip, carry):
        block = cache_ref[from_ref[chip]]
        out_ref[chip] = block
        mark = jnp.where(lane == 0, slot_ref[chip], len_ref[chip]).astype(jnp.float32)
        head = jnp.where((row == HALF - 1) & (lane < 2), mark, block[:, :128].astype(jnp.float32))
        out_ref[chip, :, pl.ds(0, 128)] = head.astype(jnp.bfloat16)
        return carry

    lax.fori_loop(0, out_ref.shape[0], one, 0)


def pack_cache(send_from, sent_slot, sent_len, cache):
    chips = send_from.shape[0]
    small = pl.BlockSpec(memory_space=pltpu.SMEM)
    return pl.pallas_call(
        pack_kernel,
        out_shape=jax.ShapeDtypeStruct((chips,) + cache.shape[1:], jnp.bfloat16),
        in_specs=[small, small, small, pl.BlockSpec(memory_space=pltpu.VMEM)],
        out_specs=pl.BlockSpec(memory_space=pltpu.VMEM),
        compiler_params=pltpu.CompilerParams(vmem_limit_bytes=24 * 2**20),
        cost_estimate=pl.CostEstimate(
            flops=0, bytes_accessed=2 * (chips + cache.shape[0]) * CTX * KVW, transcendentals=0
        ),
    )(send_from, sent_slot, sent_len, cache)


def on_device(
    kv_cache,
    lengths,
    move_list,
    queries,
    new_kv,
    hidden,
    expert_ids,
    gate_weights,
    expert_gate,
    expert_up,
    expert_down,
):
    ep_count = lax.axis_size("ep")
    slot_count = lengths.shape[0]
    own = (expert_gate[0], expert_up[0], expert_down[0])
    expert_range = jnp.arange(ep_count, dtype=jnp.int32)
    me = lax.axis_index("ep")
    core = lax.axis_index("dp")

    marks = [expert_ids.astype(jnp.bfloat16)] + three_parts(gate_weights)
    marks = jnp.concatenate(marks, axis=2).reshape(ROWS, 4 * TOPK)
    marks = jnp.pad(marks, ((0, 0), (0, MARK - 4 * TOPK)))
    rows = hidden.reshape(ROWS, D)
    columns = [
        jnp.concatenate([block, marks], axis=1) for block in (rows[:, :MAIN], rows[:, MAIN:])
    ]
    targets = []
    for orders in ORDERS:
        stride = jnp.where(core == 0, orders[0][2], orders[1][2])
        targets.append(
            jnp.stack([chip_at(stride, delta, me) for delta in TARGETS]).astype(jnp.int32)
        )
    arrived, ids = send_rows(columns, targets)

    slot_range = jnp.arange(slot_count, dtype=jnp.int32)
    send_hit = expert_range[:, None] == move_list[:, 0][None, :]
    send_from = jnp.sum(jnp.where(send_hit, slot_range[None, :], 0), axis=1)
    sent_slot = jnp.sum(jnp.where(send_hit, move_list[:, 1][None, :] + 1, 0), axis=1) - 1
    sent_len = jnp.sum(jnp.where(send_hit, lengths[None, :], 0), axis=1)
    packed_cache = pack_cache(
        send_from, sent_slot, sent_len, kv_cache.reshape(slot_count, HALF, 2 * KVW)
    )
    packed_cache, arrived, own = together(packed_cache, arrived, own)
    other = tuple(lax.ppermute(w, "dp", [(0, 1), (1, 0)]) for w in own)
    got = lax.all_to_all(packed_cache, "ep", split_axis=0, concat_axis=0, tiled=True)

    tables = []
    for main, minor in zip(*ORDERS):
        table = [0] * CHIPS
        for number in range(CHIPS):
            digits = (number // PLANE, number // SIDE % SIDE, number % SIDE)
            place = dict(zip(main, digits[::-1]))
            index = place[minor[2]] * PLANE + place[minor[1]] * SIDE + place[minor[0]]
            table[index] = number
        tables.append(jnp.array(table, jnp.int32))
    order = jnp.where(core == 0, tables[0], tables[1])
    rows, mark = join_rows(order, arrived[0], arrived[1])
    mark = mark.reshape(CHIPS * PICKS, MARK).astype(jnp.float32)
    weight = mark[:, TOPK : 2 * TOPK] + mark[:, 2 * TOPK : 3 * TOPK] + mark[:, 3 * TOPK : 4 * TOPK]
    weight = jnp.where(mark[:, :TOPK] == me.astype(jnp.float32), weight, 0.0)
    weight = jnp.sum(weight, axis=1, keepdims=True)
    produced = expert_rows(rows.reshape(CHIPS * PICKS, D), weight, (own, other))
    outward = split_rows(order, produced.reshape(CHIPS, PICKS, D))
    outward, got = lax.optimization_barrier((outward, got))
    got_slot = got[:, HALF - 1, 0].astype(jnp.int32)
    got_len = got[:, HALF - 1, 1].astype(jnp.int32)
    land_hit = got_slot[None, :] == slot_range[:, None]
    landing = jnp.sum(jnp.where(land_hit, expert_range[None, :], 0), axis=1)
    placed_len = jnp.sum(jnp.where(land_hit, got_len[None, :], 0), axis=1)

    def contexts(earlier):
        return attend(queries, new_kv, got, landing, placed_len, earlier)

    sums, context = return_rows(outward, targets, ids, contexts)
    mixture = jnp.concatenate(sums, axis=1).reshape(STEPS, SLOTS, D)
    return context, mixture


def solution(mesh):
    return jax.shard_map(
        on_device,
        mesh=mesh,
        in_specs=(
            P(("dp", "ep"), None),
            P(("dp", "ep")),
            P(("dp", "ep"), None),
            P(None, ("dp", "ep"), None),
            P(None, ("dp", "ep"), None),
            P(None, ("dp", "ep"), None),
            P(None, ("dp", "ep"), None),
            P(None, ("dp", "ep"), None),
            P("ep", None, "dp"),
            P("ep", None, "dp"),
            P("ep", "dp", None),
        ),
        out_specs=(P(None, ("dp", "ep"), None), P(None, ("dp", "ep"), None)),
        check_vma=False,
    )
```

profile of v0, /device:TPU:10, one launch (start us, length us, event | category | flops | bytes accessed | tf_op | source)
XLA Modules:
  0.0 301.2 jit_solution(4900852026887329060)
XLA Ops:
  27.7 10.1 %collective-permute-done.9.refs_1_ = bf16[256,1280]{1,0:T(8,128)(2,1)S(1)} collective-permute-done((bf16[256,1280]{1,0:T(8,128)(2,1)S(1)}, bf16[256,1280]{1,0:T(8,128)(2,1)S(1)}, u32[]{:S(2)}, u32[]{:S(2)}) %collective-permute-start.9) | collective-permute-done | bytes 655392 | tf_op jit(solution)/shard_map/ppermute | solution.py:170
  40.0 16.1 %collective-permute-done.11.refs_3_ = bf16[256,1280]{1,0:T(8,128)(2,1)} collective-permute-done((bf16[256,1280]{1,0:T(8,128)(2,1)S(1)}, bf16[256,1280]{1,0:T(8,128)(2,1)}, u32[]{:S(2)}, u32[]{:S(2)}) %collective-permute-start.11) | collective-permute-done | bytes 655392 | tf_op jit(solution)/shard_map/ppermute | solution.py:170
  59.9 4.1 %shard_map.140 = (bf16[16,16,2560]{2,1,0:T(8,128)(2,1)S(1)}, bf16[16,16,2560]{2,1,0:T(8,128)(2,1)S(1)}, bf16[16,16,2560]{2,1,0:T(8,128)(2,1)S(1)}, bf16[16,16,2560]{2,1,0:T(8,128)(2,1)S(1)}, f32[4,8,256]{2,1,0:T(8,128)S(1)}) custom-call(s32[4]{0:T(128)S(1)} %pad_add_fusion.targets_ref, bf16[256,2560]{1,0:T(8,128)(2,1)S(1)} %constant_dynamic-update-slice_fusion.refs_0_, ...), custom_call_target="tpu_custom_call" | custom-call | flops 1342177280 | bytes 10485760 | tf_op jit(solution)/shard_map/pallas_call | solution.py:214
  69.6 5.5 %collective-permute-done.15.refs_5_ = bf16[16,16,1280]{2,1,0:T(8,128)(2,1)S(1)} collective-permute-done((bf16[16,16,1280]{2,1,0:T(8,128)(2,1)S(1)}, bf16[16,16,1280]{2,1,0:T(8,128)(2,1)S(1)}, u32[]{:S(2)}, u32[]{:S(2)}) %collective-permute-start.15) | collective-permute-done | bytes 655392 | tf_op jit(solution)/shard_map/ppermute | solution.py:170
  80.7 4.1 %collective-permute-done.16.refs_6_ = bf16[16,16,1280]{2,1,0:T(8,128)(2,1)S(1)} collective-permute-done((bf16[16,16,1280]{2,1,0:T(8,128)(2,1)S(1)}, bf16[16,16,1280]{2,1,0:T(8,128)(2,1)S(1)}, u32[]{:S(2)}, u32[]{:S(2)}) %collective-permute-start.16) | collective-permute-done | bytes 655392 | tf_op jit(solution)/shard_map/ppermute | solution.py:170
  85.7 11.8 %collective-permute-done.17.refs_7_ = bf16[16,16,1280]{2,1,0:T(8,128)(2,1)S(1)} collective-permute-done((bf16[16,16,1280]{2,1,0:T(8,128)(2,1)S(1)}, bf16[16,16,1280]{2,1,0:T(8,128)(2,1)S(1)}, u32[]{:S(2)}, u32[]{:S(2)}) %collective-permute-start.17) | collective-permute-done | bytes 655392 | tf_op jit(solution)/shard_map/ppermute | solution.py:170
  111.2 11.8 %all-to-all-start = ((bf16[64,32,1152]{2,1,0:T(8,128)(2,1)}), bf16[64,32,1152]{2,1,0:T(8,128)(2,1)}, u32[]{:S(2)}, u32[]{:S(2)}) async-start(bf16[64,32,1152]{2,1,0:T(8,128)(2,1)} %copy-done), calls=%async_computation | async-start | bytes 9437184 | tf_op jit(solution)/shard_map/all_to_all | solution.py:444
  123.7 7.6 %fusion.15 = f32[1024,512]{1,0:T(8,128)S(1)} fusion(bf16[1024,3584]{1,0:T(8,128)(2,1)} %bitcast.38, bf16[3584,512]{1,0:T(8,128)(2,1)} %bitcast.12), kind=kOutput, calls=%fused_computation.54 | convolution fusion | flops 3758096384 | bytes 13107200 | tf_op jit(solution)/shard_map/dot_general | solution.py:155
  131.3 7.3 %fusion.16 = f32[1024,512]{1,0:T(8,128)} fusion(bf16[1024,3584]{1,0:T(8,128)(2,1)S(1)} %bitcast.43, bf16[3584,512]{1,0:T(8,128)(2,1)} %collective-permute-done.18), kind=kOutput, calls=%fused_computation.55 | convolution fusion | flops 3758096384 | bytes 13107200 | tf_op jit(solution)/shard_map/dot_general | solution.py:155
  138.7 15.6 %fusion = f32[1024,3584]{1,0:T(8,128)} fusion(bf16[512,3584]{1,0:T(8,128)(2,1)} %collective-permute-done.20, f32[1024,512]{1,0:T(8,128)} %fusion.16, bf16[1024,3584]{1,0:T(8,128)(2,1)} %bitcast.39, bf16[3584,512]{1,0:T(8,128)(2,1)} %collective-permute-done.19), kind=kOutput, calls=%fused_computation.5 | convolution fusion | flops 7519338496 | bytes 31457280 | tf_op jit(solution)/shard_map/dot_general | solution.py:158
  154.3 16.4 %multiply_convert_fusion = bf16[1024,3584]{1,0:T(8,128)(2,1)} fusion(f32[1024,3584]{1,0:T(8,128)} %fusion, bf16[512,3584]{1,0:T(8,128)(2,1)} %bitcast.14, f32[1024]{0:T(1024)S(1)} %fusion.4, f32[1024,512]{1,0:T(8,128)S(1)} %fusion.15, bf16[1024,3584]{1,0:T(8,128)(2,1)} %bitcast.40, bf16[3584,512]{1,0:T(8,128)(2,1)} %bitcast.13), kind=kOutput, calls=%fused_computation | convolution fusion | flops 7530348544 | bytes 38801408 | tf_op jit(solution)/shard_map/dot_general | solution.py:158
  179.5 6.1 %all-to-all-done.got_ref.refs_1_ = bf16[64,32,1152]{2,1,0:T(8,128)(2,1)} async-done(((bf16[64,32,1152]{2,1,0:T(8,128)(2,1)}), bf16[64,32,1152]{2,1,0:T(8,128)(2,1)}, u32[]{:S(2)}, u32[]{:S(2)}) %all-to-all-start) | async-done | bytes 4718624 | tf_op jit(solution)/shard_map/all_to_all | solution.py:444
  191.5 3.4 %convert_reduce_fusion = (s32[64]{0:T(128)S(1)}, s32[64]{0:T(128)S(1)}) fusion(bf16[64,32,1152]{2,1,0:T(8,128)(2,1)} %all-to-all-done.got_ref.refs_1_), kind=kLoop, calls=%fused_computation.18 | loop fusion | flops 128 | bytes 768 | tf_op jit(solution)/shard_map/convert_element_type | solution.py:465
  195.1 4.7 %collective-permute-done.24.refs_1_ = bf16[16,16,1152]{2,1,0:T(8,128)(2,1)} collective-permute-done((bf16[16,16,1152]{2,1,0:T(8,128)(2,1)}, bf16[16,16,1152]{2,1,0:T(8,128)(2,1)}, u32[]{:S(2)}, u32[]{:S(2)}) %collective-permute-start.24) | collective-permute-done | bytes 589856 | tf_op jit(solution)/shard_map/ppermute | solution.py:170
  199.8 9.6 %collective-permute-start.26 = (bf16[16,16,1152]{2,1,0:T(8,128)(2,1)}, bf16[16,16,1152]{2,1,0:T(8,128)(2,1)S(1)}, u32[]{:S(2)}, u32[]{:S(2)}) collective-permute-start(bf16[16,16,1152]{2,1,0:T(8,128)(2,1)} %copy-done.24), channel_id=1, source_target_pairs={{0,8},{1,9},{2,10},{3,11},{4,12},{5,13},{6,14},{7,15},{8,0},{9,1},... | collective-permute-start | bytes 1769480 | tf_op jit(solution)/shard_map/ppermute | solution.py:170
  211.8 17.1 %shard_map.145.refs_5_ = bf16[2,32,32768]{2,1,0:T(8,128)(2,1)} custom-call(s32[16]{0:T(128)S(1)} %get-tuple-element.197.landing_ref, bf16[64,32,1152]{2,1,0:T(8,128)(2,1)} %all-to-all-done.got_ref.refs_1_, s32[32,1]{1,0:T(8,128)S(1)} %copy.23.len_ref.refs_2_, bf16[2,32,576]{2,1,0:T(8,128)(2,1)S(1)} %copy-done.27, bf16[2,32,36864]{2,1,0:T(8,128)(2,1)S(1)} %copy-done.19), custom_call_target="tpu_custom_call" | custom-call | flops 4982833152 | bytes 4456448 | tf_op jit(solution)/shard_map/pallas_call | solution.py:130
  229.0 4.0 %shard_map.146 = (bf16[256,2432]{1,0:T(8,128)(2,1)S(1)}, bf16[256,2432]{1,0:T(8,128)(2,1)S(1)}, bf16[256,2432]{1,0:T(8,128)(2,1)S(1)}, bf16[256,2432]{1,0:T(8,128)(2,1)S(1)}) custom-call(s32[4]{0:T(128)S(1)} %pad_add_fusion.targets_ref, f32[4,8,256]{2,1,0:T(8,128)S(1)} %get-tuple-element.101.ids_ref, bf16[16,16,2432]{2,1,0:T(8,128)(2,1)S(1)} %get-tuple-element.136.refs_0_, ...), custom_call_target="tpu_custom_call" | custom-call | flops 1275068416 | bytes 9961472 | tf_op jit(solution)/shard_map/pallas_call | solution.py:242
  235.0 4.3 %collective-permute-start.29 = (bf16[256,2432]{1,0:T(8,128)(2,1)S(1)}, bf16[256,2432]{1,0:T(8,128)(2,1)S(1)}, u32[]{:S(2)}, u32[]{:S(2)}) collective-permute-start(bf16[256,2432]{1,0:T(8,128)(2,1)S(1)} %get-tuple-element.149), channel_id=1, source_target_pairs={{0,8},{1,9},{2,10},{3,11},{4,12},{5,13},{6,14},{7,15},{8,0},{9,1},... | collective-permute-start | bytes 3735560 | tf_op jit(solution)/shard_map/ppermute | solution.py:170
  244.3 11.0 %collective-permute-done.30 = bf16[256,1152]{1,0:T(8,128)(2,1)S(1)} collective-permute-done((bf16[256,1152]{1,0:T(8,128)(2,1)S(1)}, bf16[256,1152]{1,0:T(8,128)(2,1)S(1)}, u32[]{:S(2)}, u32[]{:S(2)}) %collective-permute-start.30) | collective-permute-done | bytes 589856 | tf_op jit(solution)/shard_map/ppermute | solution.py:170
  255.3 3.4 %collective-permute-start.32 = (bf16[256,1152]{1,0:T(8,128)(2,1)S(1)}, bf16[256,1152]{1,0:T(8,128)(2,1)S(1)}, u32[]{:S(2)}, u32[]{:S(2)}) collective-permute-start(bf16[256,1152]{1,0:T(8,128)(2,1)S(1)} %get-tuple-element.157), channel_id=1, source_target_pairs={{0,32},{1,33},{2,34},{3,35},{4,36},{5,37},{6,38},{7,39},{8,40},{9,... | collective-permute-start | bytes 1769480 | tf_op jit(solution)/shard_map/ppermute | solution.py:170
  261.1 17.1 %shard_map.148 = bf16[2,32,32768]{2,1,0:T(8,128)(2,1)} custom-call(s32[16]{0:T(128)S(1)} %get-tuple-element.196.refs_0_, bf16[64,32,1152]{2,1,0:T(8,128)(2,1)} %all-to-all-done.got_ref.refs_1_, s32[32,1]{1,0:T(8,128)S(1)} %copy.23.len_ref.refs_2_, bf16[2,32,576]{2,1,0:T(8,128)(2,1)S(1)} %copy-done.27, ...), custom_call_target="tpu_custom_call", output_to_operand_aliasing={{}: (5, {})} | custom-call | flops 4982833152 | bytes 4456448 | tf_op jit(solution)/shard_map/pallas_call | solution.py:130
  282.6 6.1 %collective-permute-start.37 = (bf16[64,1152]{1,0:T(8,128)(2,1)S(1)}, bf16[64,1152]{1,0:T(8,128)(2,1)S(1)}, u32[]{:S(2)}, u32[]{:S(2)}) collective-permute-start(bf16[64,1152]{1,0:T(8,128)(2,1)S(1)} %get-tuple-element.188), channel_id=1, source_target_pairs={{0,1},{1,2},{2,3},{3,0},{4,5},{5,6},{6,7},{7,4},{8,9},{9,10},{10,1... | collective-permute-start | bytes 442376 | tf_op jit(solution)/shard_map/ppermute | solution.py:170
  288.7 4.6 %collective-permute-done.36 = bf16[64,1152]{1,0:T(8,128)(2,1)S(1)} collective-permute-done((bf16[64,1152]{1,0:T(8,128)(2,1)S(1)}, bf16[64,1152]{1,0:T(8,128)(2,1)S(1)}, u32[]{:S(2)}, u32[]{:S(2)}) %collective-permute-start.36) | collective-permute-done | bytes 147488 | tf_op jit(solution)/shard_map/ppermute | solution.py:170
  293.5 6.5 %collective-permute-done.38 = bf16[64,1152]{1,0:T(8,128)(2,1)S(1)} collective-permute-done((bf16[64,1152]{1,0:T(8,128)(2,1)S(1)}, bf16[64,1152]{1,0:T(8,128)(2,1)S(1)}, u32[]{:S(2)}, u32[]{:S(2)}) %collective-permute-start.38) | collective-permute-done | bytes 147488 | tf_op jit(solution)/shard_map/ppermute | solution.py:170
  (177 shorter events, 91.6 us)
Async XLA Ops:
  21.5 34.5 %collective-permute-start.6 = (bf16[256,2560]{1,0:T(8,128)(2,1)S(1)}, bf16[256,2560]{1,0:T(8,128)(2,1)S(1)}, u32[]{:S(2)}, u32[]{:S(2)}) collective-permute-start(bf16[256,2560]{1,0:T(8,128)(2,1)S(1)} %constant_dynamic-update-slice_fusion.refs_0_), channel_id=1, source_target_pairs={{0,4},{1,5},{2,6},{3,7},{4,8},{5,9},{6,10},{7,11},{8,12},{9,13},{1... | collective-permute-start | bytes 3932168 | tf_op jit(solution)/shard_map/ppermute | solution.py:170
  23.2 32.9 %collective-permute-start.7 = (bf16[256,2560]{1,0:T(8,128)(2,1)S(1)}, bf16[256,2560]{1,0:T(8,128)(2,1)}, u32[]{:S(2)}, u32[]{:S(2)}) collective-permute-start(bf16[256,2560]{1,0:T(8,128)(2,1)S(1)} %constant_dynamic-update-slice_fusion.refs_0_), channel_id=1, source_target_pairs={{0,12},{1,13},{2,14},{3,15},{4,0},{5,1},{6,2},{7,3},{8,4},{9,5},{1... | collective-permute-start | bytes 3932168 | tf_op jit(solution)/shard_map/ppermute | solution.py:170
  23.6 32.4 %collective-permute-start.8 = (bf16[256,2560]{1,0:T(8,128)(2,1)S(1)}, bf16[256,2560]{1,0:T(8,128)(2,1)}, u32[]{:S(2)}, u32[]{:S(2)}) collective-permute-start(bf16[256,2560]{1,0:T(8,128)(2,1)S(1)} %constant_dynamic-update-slice_fusion.refs_0_), channel_id=1, source_target_pairs={{0,8},{1,9},{2,10},{3,11},{4,12},{5,13},{6,14},{7,15},{8,0},{9,1},... | collective-permute-start | bytes 3932168 | tf_op jit(solution)/shard_map/ppermute | solution.py:170
  64.1 34.3 %collective-permute-start.12 = (bf16[16,16,2560]{2,1,0:T(8,128)(2,1)S(1)}, bf16[16,16,2560]{2,1,0:T(8,128)(2,1)S(1)}, u32[]{:S(2)}, u32[]{:S(2)}) collective-permute-start(bf16[16,16,2560]{2,1,0:T(8,128)(2,1)S(1)} %get-tuple-element.103), channel_id=1, source_target_pairs={{0,1},{1,2},{2,3},{3,0},{4,5},{5,6},{6,7},{7,4},{8,9},{9,10},{10,1... | collective-permute-start | bytes 3932168 | tf_op jit(solution)/shard_map/ppermute | solution.py:170
  64.9 33.5 %collective-permute-start.13 = (bf16[16,16,2560]{2,1,0:T(8,128)(2,1)S(1)}, bf16[16,16,2560]{2,1,0:T(8,128)(2,1)S(1)}, u32[]{:S(2)}, u32[]{:S(2)}) collective-permute-start(bf16[16,16,2560]{2,1,0:T(8,128)(2,1)S(1)} %get-tuple-element.104), channel_id=1, source_target_pairs={{0,3},{1,0},{2,1},{3,2},{4,7},{5,4},{6,5},{7,6},{8,11},{9,8},{10,9... | collective-permute-start | bytes 3932168 | tf_op jit(solution)/shard_map/ppermute | solution.py:170
  66.2 33.3 %collective-permute-start.14 = (bf16[16,16,2560]{2,1,0:T(8,128)(2,1)S(1)}, bf16[16,16,2560]{2,1,0:T(8,128)(2,1)S(1)}, u32[]{:S(2)}, u32[]{:S(2)}) collective-permute-start(bf16[16,16,2560]{2,1,0:T(8,128)(2,1)S(1)} %get-tuple-element.105), channel_id=1, source_target_pairs={{0,2},{1,3},{2,0},{3,1},{4,6},{5,7},{6,4},{7,5},{8,10},{9,11},{10,... | collective-permute-start | bytes 3932168 | tf_op jit(solution)/shard_map/ppermute | solution.py:170
  75.1 22.4 %collective-permute-start.17 = (bf16[16,16,1280]{2,1,0:T(8,128)(2,1)S(1)}, bf16[16,16,1280]{2,1,0:T(8,128)(2,1)S(1)}, u32[]{:S(2)}, u32[]{:S(2)}) collective-permute-start(bf16[16,16,1280]{2,1,0:T(8,128)(2,1)S(1)} %get-tuple-element.113), channel_id=1, source_target_pairs={{0,8},{1,9},{2,10},{3,11},{4,12},{5,13},{6,14},{7,15},{8,0},{9,1},... | collective-permute-start | bytes 1966088 | tf_op jit(solution)/shard_map/ppermute | solution.py:170
  100.6 30.7 %collective-permute-start.18 = (bf16[3584,512]{1,0:T(8,128)(2,1)}, bf16[3584,512]{1,0:T(8,128)(2,1)}, u32[]{:S(2)}, u32[]{:S(2)}) collective-permute-start(bf16[3584,512]{1,0:T(8,128)(2,1)} %bitcast.12), channel_id=1, source_target_pairs={{0,64},{64,0},{1,65},{65,1},{2,66},{66,2},{3,67},{67,3},{4,68},{68... | collective-permute-start | bytes 11010056 | tf_op jit(solution)/shard_map/ppermute | solution.py:443
  100.6 38.0 %collective-permute-start.20 = (bf16[512,3584]{1,0:T(8,128)(2,1)}, bf16[512,3584]{1,0:T(8,128)(2,1)}, u32[]{:S(2)}, u32[]{:S(2)}) collective-permute-start(bf16[512,3584]{1,0:T(8,128)(2,1)} %bitcast.14), channel_id=1, source_target_pairs={{0,64},{64,0},{1,65},{65,1},{2,66},{66,2},{3,67},{67,3},{4,68},{68... | collective-permute-start | bytes 11010056 | tf_op jit(solution)/shard_map/ppermute | solution.py:443
  101.1 37.5 %collective-permute-start.19 = (bf16[3584,512]{1,0:T(8,128)(2,1)}, bf16[3584,512]{1,0:T(8,128)(2,1)}, u32[]{:S(2)}, u32[]{:S(2)}) collective-permute-start(bf16[3584,512]{1,0:T(8,128)(2,1)} %bitcast.13), channel_id=1, source_target_pairs={{0,64},{64,0},{1,65},{65,1},{2,66},{66,2},{3,67},{67,3},{4,68},{68... | collective-permute-start | bytes 11010056 | tf_op jit(solution)/shard_map/ppermute | solution.py:443
  111.2 74.3 %all-to-all-start = ((bf16[64,32,1152]{2,1,0:T(8,128)(2,1)}), bf16[64,32,1152]{2,1,0:T(8,128)(2,1)}, u32[]{:S(2)}, u32[]{:S(2)}) async-start(bf16[64,32,1152]{2,1,0:T(8,128)(2,1)} %copy-done), calls=%async_computation | async-start | bytes 9437184 | tf_op jit(solution)/shard_map/all_to_all | solution.py:444
  185.5 43.4 %collective-permute-start.21 = (bf16[16,16,2432]{2,1,0:T(8,128)(2,1)}, bf16[16,16,2432]{2,1,0:T(8,128)(2,1)S(1)}, u32[]{:S(2)}, u32[]{:S(2)}) collective-permute-start(bf16[16,16,2432]{2,1,0:T(8,128)(2,1)} %copy-done.23), channel_id=1, source_target_pairs={{0,3},{1,0},{2,1},{3,2},{4,7},{5,4},{6,5},{7,6},{8,11},{9,8},{10,9... | collective-permute-start | bytes 3735560 | tf_op jit(solution)/shard_map/ppermute | solution.py:170
  186.0 42.9 %collective-permute-start.22 = (bf16[16,16,2432]{2,1,0:T(8,128)(2,1)}, bf16[16,16,2432]{2,1,0:T(8,128)(2,1)}, u32[]{:S(2)}, u32[]{:S(2)}) collective-permute-start(bf16[16,16,2432]{2,1,0:T(8,128)(2,1)} %copy-done.22), channel_id=1, source_target_pairs={{0,1},{1,2},{2,3},{3,0},{4,5},{5,6},{6,7},{7,4},{8,9},{9,10},{10,1... | collective-permute-start | bytes 3735560 | tf_op jit(solution)/shard_map/ppermute | solution.py:170
  187.6 41.4 %collective-permute-start.23 = (bf16[16,16,2432]{2,1,0:T(8,128)(2,1)}, bf16[16,16,2432]{2,1,0:T(8,128)(2,1)}, u32[]{:S(2)}, u32[]{:S(2)}) collective-permute-start(bf16[16,16,2432]{2,1,0:T(8,128)(2,1)} %copy-done.21), channel_id=1, source_target_pairs={{0,2},{1,3},{2,0},{3,1},{4,6},{5,7},{6,4},{7,5},{8,10},{9,11},{10,... | collective-permute-start | bytes 3735560 | tf_op jit(solution)/shard_map/ppermute | solution.py:170
  189.5 39.4 %collective-permute-start.25 = (bf16[16,16,1152]{2,1,0:T(8,128)(2,1)}, bf16[16,16,1152]{2,1,0:T(8,128)(2,1)}, u32[]{:S(2)}, u32[]{:S(2)}) collective-permute-start(bf16[16,16,1152]{2,1,0:T(8,128)(2,1)} %copy-done.25), channel_id=1, source_target_pairs={{0,4},{1,5},{2,6},{3,7},{4,8},{5,9},{6,10},{7,11},{8,12},{9,13},{1... | collective-permute-start | bytes 1769480 | tf_op jit(solution)/shard_map/ppermute | solution.py:170
  199.8 29.1 %collective-permute-start.26 = (bf16[16,16,1152]{2,1,0:T(8,128)(2,1)}, bf16[16,16,1152]{2,1,0:T(8,128)(2,1)S(1)}, u32[]{:S(2)}, u32[]{:S(2)}) collective-permute-start(bf16[16,16,1152]{2,1,0:T(8,128)(2,1)} %copy-done.24), channel_id=1, source_target_pairs={{0,8},{1,9},{2,10},{3,11},{4,12},{5,13},{6,14},{7,15},{8,0},{9,1},... | collective-permute-start | bytes 1769480 | tf_op jit(solution)/shard_map/ppermute | solution.py:170
  232.9 45.3 %collective-permute-start.27 = (bf16[256,2432]{1,0:T(8,128)(2,1)S(1)}, bf16[256,2432]{1,0:T(8,128)(2,1)S(1)}, u32[]{:S(2)}, u32[]{:S(2)}) collective-permute-start(bf16[256,2432]{1,0:T(8,128)(2,1)S(1)} %get-tuple-element.147), channel_id=1, source_target_pairs={{0,12},{1,13},{2,14},{3,15},{4,0},{5,1},{6,2},{7,3},{8,4},{9,5},{1... | collective-permute-start | bytes 3735560 | tf_op jit(solution)/shard_map/ppermute | solution.py:170
  234.1 44.1 %collective-permute-start.28 = (bf16[256,2432]{1,0:T(8,128)(2,1)S(1)}, bf16[256,2432]{1,0:T(8,128)(2,1)S(1)}, u32[]{:S(2)}, u32[]{:S(2)}) collective-permute-start(bf16[256,2432]{1,0:T(8,128)(2,1)S(1)} %get-tuple-element.148), channel_id=1, source_target_pairs={{0,4},{1,5},{2,6},{3,7},{4,8},{5,9},{6,10},{7,11},{8,12},{9,13},{1... | collective-permute-start | bytes 3735560 | tf_op jit(solution)/shard_map/ppermute | solution.py:170
  235.0 43.2 %collective-permute-start.29 = (bf16[256,2432]{1,0:T(8,128)(2,1)S(1)}, bf16[256,2432]{1,0:T(8,128)(2,1)S(1)}, u32[]{:S(2)}, u32[]{:S(2)}) collective-permute-start(bf16[256,2432]{1,0:T(8,128)(2,1)S(1)} %get-tuple-element.149), channel_id=1, source_target_pairs={{0,8},{1,9},{2,10},{3,11},{4,12},{5,13},{6,14},{7,15},{8,0},{9,1},... | collective-permute-start | bytes 3735560 | tf_op jit(solution)/shard_map/ppermute | solution.py:170
  244.3 33.9 %collective-permute-start.31 = (bf16[256,1152]{1,0:T(8,128)(2,1)S(1)}, bf16[256,1152]{1,0:T(8,128)(2,1)S(1)}, u32[]{:S(2)}, u32[]{:S(2)}) collective-permute-start(bf16[256,1152]{1,0:T(8,128)(2,1)S(1)} %get-tuple-element.156), channel_id=1, source_target_pairs={{0,16},{1,17},{2,18},{3,19},{4,20},{5,21},{6,22},{7,23},{8,24},{9,... | collective-permute-start | bytes 1769480 | tf_op jit(solution)/shard_map/ppermute | solution.py:170
  255.3 22.9 %collective-permute-start.32 = (bf16[256,1152]{1,0:T(8,128)(2,1)S(1)}, bf16[256,1152]{1,0:T(8,128)(2,1)S(1)}, u32[]{:S(2)}, u32[]{:S(2)}) collective-permute-start(bf16[256,1152]{1,0:T(8,128)(2,1)S(1)} %get-tuple-element.157), channel_id=1, source_target_pairs={{0,32},{1,33},{2,34},{3,35},{4,36},{5,37},{6,38},{7,39},{8,40},{9,... | collective-permute-start | bytes 1769480 | tf_op jit(solution)/shard_map/ppermute | solution.py:170
  278.9 21.0 %collective-permute-start.33 = (bf16[64,2432]{1,0:T(8,128)(2,1)S(1)}, bf16[64,2432]{1,0:T(8,128)(2,1)S(1)}, u32[]{:S(2)}, u32[]{:S(2)}) collective-permute-start(bf16[64,2432]{1,0:T(8,128)(2,1)S(1)} %get-tuple-element.185), channel_id=1, source_target_pairs={{0,48},{1,49},{2,50},{3,51},{4,52},{5,53},{6,54},{7,55},{8,56},{9,... | collective-permute-start | bytes 933896 | tf_op jit(solution)/shard_map/ppermute | solution.py:170
  279.9 20.1 %collective-permute-start.34 = (bf16[64,2432]{1,0:T(8,128)(2,1)S(1)}, bf16[64,2432]{1,0:T(8,128)(2,1)S(1)}, u32[]{:S(2)}, u32[]{:S(2)}) collective-permute-start(bf16[64,2432]{1,0:T(8,128)(2,1)S(1)} %get-tuple-element.184), channel_id=1, source_target_pairs={{0,16},{1,17},{2,18},{3,19},{4,20},{5,21},{6,22},{7,23},{8,24},{9,... | collective-permute-start | bytes 933896 | tf_op jit(solution)/shard_map/ppermute | solution.py:170
  281.0 18.9 %collective-permute-start.35 = (bf16[64,2432]{1,0:T(8,128)(2,1)S(1)}, bf16[64,2432]{1,0:T(8,128)(2,1)S(1)}, u32[]{:S(2)}, u32[]{:S(2)}) collective-permute-start(bf16[64,2432]{1,0:T(8,128)(2,1)S(1)} %get-tuple-element.183), channel_id=1, source_target_pairs={{0,32},{1,33},{2,34},{3,35},{4,36},{5,37},{6,38},{7,39},{8,40},{9,... | collective-permute-start | bytes 933896 | tf_op jit(solution)/shard_map/ppermute | solution.py:170
  (51 other events, 415.0 us)
where the time goes:
time: 306 us; the launch traced here: 301 us
  waiting for transfers between devices  86.5 us (28%)
  starting transfers between devices  75 us (25%)
  Pallas kernels  51.3 us (17%)
  matrix products  46.9 us (15%)
  local copies, waits for them, and re-layouts  32.3 us (11%)
  other arithmetic  7.87 us (3%)
    ppermute x36, waiting for transfers between devices, hop(): return lax.ppermute(value, ('dp', 'ep'), pairs)  80.4 us
    ppermute x36, starting transfers between devices, hop(): return lax.ppermute(value, ('dp', 'ep'), pairs)  62.7 us
    pallas_call x2, Pallas kernels, attend(): pl.pallas_call(kernel, grid=(1,), out_shape=jax.ShapeDtypeStruct((STEPS,...  34.2 us
    dot_general x2, matrix products, expert_rows(): part = jnp.dot(inner, down_mat, preferred_element_type=jnp.float32)  32 us
    unnamed x77, local copies, waits for them, and re-layouts  30 us
    dot_general x2, matrix products, expert_rows(): gate_pre = jnp.dot(token_rows, gate_mat, preferred_element_type=jnp.float32)  14.9 us
    all_to_all x1, starting transfers between devices, on_device(): lax.all_to_all(packed_cache, 'ep', split_axis=0, concat_axis=0, tiled=True)  11.8 us
    pallas_call x2, Pallas kernels, select(): pl.pallas_call(select_kernel, out_shape=[jax.ShapeDtypeStruct((PLANE, PIC...  6.81 us
  transfers between devices with their start and end apart: 40, of which 14 were waited for; matrix products, arithmetic and copies ran while one was open for 18% of the time, Pallas kernels for 15%

commit v1 on v0

--- a/solution.py
+++ b/solution.py
@@ -28,6 +28,7 @@
 LINE = SIDE * ROWS
 PLANE = SIDE * SIDE
 CHIPS = SIDE**3
+BLOCK = 32
 ORDERS = (((Z, Y, X), (Y, X, Z)), ((X, Z, Y), (X, Z, Y)))
 TARGETS = (0, 1, -1, 2)
 KEYS = GROUP * (CTX + STEPS)
@@ -37,6 +38,7 @@
 
 
 def attend_kernel(landing_ref, got_ref, len_ref, new_ref, query_ref, out_ref, even_ref, odd_ref, value_ref, bias_ref):
+    group = pl.program_id(0)
     pairs = GROUP * HALF
 
     def lanes(rows):
@@ -48,7 +50,7 @@
         value_ref[pl.ds(at, rows), :] = keys[:, :LAT].astype(jnp.bfloat16)
 
     def one(slot, carry):
-        source = landing_ref[slot]
+        source = landing_ref[group * GROUP + slot]
         block = got_ref[source]
         first = jnp.where(lanes(HALF) < KVW, block[:, :WIDE].astype(jnp.float32), 0.0)
         at = pl.multiple_of(slot * HALF, HALF)
@@ -108,56 +110,33 @@
     lax.fori_loop(0, H // (2 * TOGETHER), heads, 0)
 
 
-def attend(queries, new_kv, got, landing, placed_len, earlier):
+def attend(queries, new_kv, got, landing, placed_len):
     slots = queries.shape[1]
-    group = 0 if earlier is None else 1
-    specs = [
-        pl.BlockSpec(memory_space=pltpu.SMEM),
-        pl.BlockSpec(memory_space=pltpu.VMEM),
-        pl.BlockSpec((GROUP, 1), lambda g: (group, 0)),
-        pl.BlockSpec((STEPS, GROUP, KVW), lambda g: (0, group, 0)),
-        pl.BlockSpec((STEPS, GROUP, H * KVW), lambda g: (0, group, 0)),
-    ]
-    operands = [landing[group * GROUP :][:GROUP], got, placed_len[:, None], new_kv, queries]
-    kernel = attend_kernel
-    if earlier is not None:
-        specs.append(pl.BlockSpec(memory_space=pl.ANY))
-        operands.append(earlier)
-
-        def kernel(*refs):
-            attend_kernel(*refs[:5], *refs[6:])
-
     return pl.pallas_call(
-        kernel,
-        grid=(1,),
+        attend_kernel,
+        grid=(slots // GROUP,),
         out_shape=jax.ShapeDtypeStruct((STEPS, slots, H * LAT), jnp.bfloat16),
-        in_specs=specs,
-        out_specs=pl.BlockSpec((STEPS, GROUP, H * LAT), lambda g: (0, group, 0)),
+        in_specs=[
+            pl.BlockSpec(memory_space=pltpu.SMEM),
+            pl.BlockSpec(memory_space=pltpu.VMEM),
+            pl.BlockSpec((GROUP, 1), lambda g: (g, 0)),
+            pl.BlockSpec((STEPS, GROUP, KVW), lambda g: (0, g, 0)),
+            pl.BlockSpec((STEPS, GROUP, H * KVW), lambda g: (0, g, 0)),
+        ],
+        out_specs=pl.BlockSpec((STEPS, GROUP, H * LAT), lambda g: (0, g, 0)),
         scratch_shapes=[
             pltpu.VMEM((KEYS, WIDE), jnp.bfloat16),
             pltpu.VMEM((KEYS, WIDE), jnp.bfloat16),
             pltpu.VMEM((KEYS, LAT), jnp.bfloat16),
             pltpu.VMEM((STEPS * GROUP, KEYS), jnp.float32),
         ],
-        input_output_aliases={} if earlier is None else {5: 0},
-        compiler_params=pltpu.CompilerParams(vmem_limit_bytes=32 * 2**20),
+        compiler_params=pltpu.CompilerParams(vmem_limit_bytes=48 * 2**20),
         cost_estimate=pl.CostEstimate(
-            flops=2 * STEPS * GROUP * H * KEYS * (WIDE + LAT),
-            bytes_accessed=2 * STEPS * GROUP * H * (KVW + LAT),
-            transcendentals=STEPS * GROUP * H * KEYS,
+            flops=2 * STEPS * slots * H * KEYS * (WIDE + LAT),
+            bytes_accessed=2 * STEPS * slots * H * (KVW + LAT),
+            transcendentals=STEPS * slots * H * KEYS,
         ),
-    )(*operands)
-
-
-def expert_rows(token_rows, row_weight, halves):
-    total = None
-    for gate_mat, up_mat, down_mat in halves:
-        gate_pre = jnp.dot(token_rows, gate_mat, preferred_element_type=jnp.float32)
-        up_pre = jnp.dot(token_rows, up_mat, preferred_element_type=jnp.float32)
-        inner = (jax.nn.silu(gate_pre) * up_pre).astype(jnp.bfloat16)
-        part = jnp.dot(inner, down_mat, preferred_element_type=jnp.float32)
-        total = part if total is None else total + part
-    return (total * row_weight).astype(jnp.bfloat16)
+    )(landing, got, placed_len[:, None], new_kv, queries)
 
 
 def hop(value, strides, delta):
@@ -263,29 +242,28 @@
     return [hop(block, strides, delta) for block, delta in zip(blocks, deltas)]
 
 
-def send_rows(columns, targets):
+def send_rows(columns, targets, packed_cache):
     first, second, third = stage_axes()
     both = range(len(columns))
     rings = [exchange([columns[i]] * 3, first[i], (1, -1, 2)) for i in both]
     columns, rings = together(columns, rings)
     lines = [jnp.concatenate([columns[i]] + rings[i], axis=0) for i in both]
     rings = [exchange([lines[i]] * 3, second[i], (1, -1, 2)) for i in both]
+    packed_cache, rings[1][0] = together(packed_cache, rings[1][0])
     lines, rings = together(lines, rings)
     picked = [select(targets[i], [lines[i]] + rings[i]) for i in both]
     rings = [exchange(picked[i][1:SIDE], third[i], TARGETS[1:]) for i in both]
-    return [[picked[i][0]] + rings[i] for i in both], [p[SIDE] for p in picked]
-
-
-def return_rows(outward, targets, ids, contexts):
+    return [[picked[i][0]] + rings[i] for i in both], [p[SIDE] for p in picked], packed_cache
+
+
+def return_rows(outward, targets, ids, context):
     first, second, third = stage_axes()
     both = range(len(outward))
     rings = [exchange(outward[i][1:], third[i], (-1, 1, 2)) for i in both]
-    context = contexts(None)
     rings, context = together(rings, context)
     lines = [combine(targets[i], ids[i], [outward[i][0]] + rings[i]) for i in both]
     rings = [exchange(lines[i][1:], second[i], (-1, 1, 2)) for i in both]
-    context = contexts(context)
-    rings, context = together(rings, context)
+    lines, rings = together(lines, rings)
     sums = []
     for i in both:
         line = add(lines[i][0], *rings[i])
@@ -299,63 +277,101 @@
     return sum(t.astype(jnp.float32) for t in terms).astype(jnp.bfloat16)
 
 
-def join_kernel(order_ref, *refs):
-    main, minor, (rows_ref, mark_ref) = refs[:SIDE], refs[SIDE : 2 * SIDE], refs[2 * SIDE :]
+def half_expert(rows, gate_ref, up_ref):
+    gate_pre = jnp.dot(rows, gate_ref[...], preferred_element_type=jnp.float32)
+    up_pre = jnp.dot(rows, up_ref[...], preferred_element_type=jnp.float32)
+    return (gate_pre * (1.0 / (1.0 + jnp.exp(-gate_pre))) * up_pre).astype(jnp.bfloat16)
+
+
+def first_half_kernel(order_ref, me_ref, *refs):
+    main, minor = refs[:SIDE], refs[SIDE : 2 * SIDE]
+    gate_ref, up_ref, down_ref, rows_ref, part_ref, weight_ref = refs[2 * SIDE :]
 
     def one(group, carry):
         for j in range(SIDE):
             number = j * PLANE + group
             rows_ref[number, :, pl.ds(0, MAIN)] = main[j][group, :, pl.ds(0, MAIN)]
-            mark_ref[number] = main[j][group, :, pl.ds(MAIN, MARK)]
             rows_ref[order_ref[number], :, pl.ds(MAIN, MINOR)] = minor[j][group, :, pl.ds(0, MINOR)]
+            mark = main[j][group, :, pl.ds(MAIN, MARK)].astype(jnp.float32)
+            total = sum(pltpu.roll(mark, MARK - k * TOPK, 1) for k in range(1, 4))
+            lane = lax.broadcasted_iota(jnp.int32, mark.shape, 1)
+            mine = (lane < TOPK) & (mark == me_ref[0].astype(jnp.float32))
+            total = jnp.sum(jnp.where(mine, total, 0.0), axis=1, keepdims=True)
+            weight_ref[number] = jnp.broadcast_to(total, mark.shape)
         return carry
 
     lax.fori_loop(0, PLANE, one, 0)
 
-
-def join_rows(order, main, minor):
-    vmem = pl.BlockSpec(memory_space=pltpu.VMEM)
-    return pl.pallas_call(
-        join_kernel,
-        out_shape=[
-            jax.ShapeDtypeStruct((CHIPS, PICKS, D), jnp.bfloat16),
-            jax.ShapeDtypeStruct((CHIPS, PICKS, MARK), jnp.bfloat16),
-        ],
-        in_specs=[pl.BlockSpec(memory_space=pltpu.SMEM)] + [vmem] * (2 * SIDE),
-        out_specs=[vmem] * 2,
-        compiler_params=pltpu.CompilerParams(vmem_limit_bytes=32 * 2**20),
-        cost_estimate=pl.CostEstimate(
-            flops=0, bytes_accessed=4 * CHIPS * PICKS * D, transcendentals=0
-        ),
-    )(order, *main, *minor)
-
-
-def split_kernel(order_ref, rows_ref, *refs):
-    main, minor = refs[:SIDE], refs[SIDE:]
+    def block(index, carry):
+        at = pl.ds(index * BLOCK, BLOCK)
+        rows = rows_ref[at].reshape(BLOCK * PICKS, D)
+        inner = half_expert(rows, gate_ref, up_ref)
+        for start in range(0, D, LAT):
+            part = jnp.dot(inner, down_ref[:, start : start + LAT], preferred_element_type=jnp.float32)
+            part_ref[at, :, pl.ds(start, LAT)] = part.astype(jnp.bfloat16).reshape(BLOCK, PICKS, LAT)
+        return carry
+
+    lax.fori_loop(0, CHIPS // BLOCK, block, 0)
+
+
+def second_half_kernel(order_ref, rows_ref, part_ref, weight_ref, gate_ref, up_ref, down_ref, *refs):
+    main, minor, out_ref = refs[:SIDE], refs[SIDE : 2 * SIDE], refs[2 * SIDE]
+
+    def block(index, carry):
+        at = pl.ds(index * BLOCK, BLOCK)
+        rows = rows_ref[at].reshape(BLOCK * PICKS, D)
+        inner = half_expert(rows, gate_ref, up_ref)
+        weight = weight_ref[at].reshape(BLOCK * PICKS, MARK)
+        weight = jnp.concatenate([weight] * (LAT // MARK), axis=1)
+        for start in range(0, D, LAT):
+            part = jnp.dot(inner, down_ref[:, start : start + LAT], preferred_element_type=jnp.float32)
+            earlier = part_ref[at, :, pl.ds(start, LAT)].reshape(BLOCK * PICKS, LAT)
+            total = (earlier.astype(jnp.float32) + part) * weight
+            out_ref[at, :, pl.ds(start, LAT)] = total.astype(jnp.bfloat16).reshape(BLOCK, PICKS, LAT)
+        return carry
+
+    lax.fori_loop(0, CHIPS // BLOCK, block, 0)
 
     def one(group, carry):
         for j in range(SIDE):
             number = j * PLANE + group
-            main[j][group] = rows_ref[number, :, pl.ds(0, MAIN)]
-            minor[j][group] = rows_ref[order_ref[number], :, pl.ds(MAIN, MINOR)]
+            main[j][group] = out_ref[number, :, pl.ds(0, MAIN)]
+            minor[j][group] = out_ref[order_ref[number], :, pl.ds(MAIN, MINOR)]
         return carry
 
     lax.fori_loop(0, PLANE, one, 0)
 
 
-def split_rows(order, rows):
-    vmem = pl.BlockSpec(memory_space=pltpu.VMEM)
+HALF_COST = pl.CostEstimate(
+    flops=2 * CHIPS * PICKS * D * 512 * 3, bytes_accessed=2 * (3 * D * 512 + 3 * CHIPS * PICKS * D), transcendentals=CHIPS * PICKS * 512
+)
+
+
+def first_half(order, me, main, minor, matrices):
+    vmem, smem = pl.BlockSpec(memory_space=pltpu.VMEM), pl.BlockSpec(memory_space=pltpu.SMEM)
+    whole = jax.ShapeDtypeStruct((CHIPS, PICKS, D), jnp.bfloat16)
+    return pl.pallas_call(
+        first_half_kernel,
+        out_shape=[whole, whole, jax.ShapeDtypeStruct((CHIPS, PICKS, MARK), jnp.float32)],
+        in_specs=[smem, smem] + [vmem] * (2 * SIDE + 3),
+        out_specs=[vmem] * 3,
+        compiler_params=pltpu.CompilerParams(vmem_limit_bytes=52 * 2**20),
+        cost_estimate=HALF_COST,
+    )(order, me[None], *main, *minor, *matrices)
+
+
+def second_half(order, rows, part, weight, matrices):
+    vmem, smem = pl.BlockSpec(memory_space=pltpu.VMEM), pl.BlockSpec(memory_space=pltpu.SMEM)
     shapes = [(PLANE, PICKS, width) for width in (MAIN, MINOR) for _ in range(SIDE)]
     outs = pl.pallas_call(
-        split_kernel,
+        second_half_kernel,
         out_shape=[jax.ShapeDtypeStruct(shape, jnp.bfloat16) for shape in shapes],
-        in_specs=[pl.BlockSpec(memory_space=pltpu.SMEM), vmem],
+        in_specs=[smem] + [vmem] * 6,
         out_specs=[vmem] * (2 * SIDE),
-        compiler_params=pltpu.CompilerParams(vmem_limit_bytes=32 * 2**20),
-        cost_estimate=pl.CostEstimate(
-            flops=0, bytes_accessed=4 * CHIPS * PICKS * D, transcendentals=0
-        ),
-    )(order, rows)
+        scratch_shapes=[pltpu.VMEM((CHIPS, PICKS, D), jnp.bfloat16)],
+        compiler_params=pltpu.CompilerParams(vmem_limit_bytes=52 * 2**20),
+        cost_estimate=HALF_COST,
+    )(order, rows, part, weight, *matrices)
     return outs[:SIDE], outs[SIDE:]
 
 
@@ -429,8 +445,6 @@
         targets.append(
             jnp.stack([chip_at(stride, delta, me) for delta in TARGETS]).astype(jnp.int32)
         )
-    arrived, ids = send_rows(columns, targets)
-
     slot_range = jnp.arange(slot_count, dtype=jnp.int32)
     send_hit = expert_range[:, None] == move_list[:, 0][None, :]
     send_from = jnp.sum(jnp.where(send_hit, slot_range[None, :], 0), axis=1)
@@ -439,9 +453,10 @@
     packed_cache = pack_cache(
         send_from, sent_slot, sent_len, kv_cache.reshape(slot_count, HALF, 2 * KVW)
     )
-    packed_cache, arrived, own = together(packed_cache, arrived, own)
+    arrived, ids, packed_cache = send_rows(columns, targets, packed_cache)
+    got = lax.all_to_all(packed_cache, "ep", split_axis=0, concat_axis=0, tiled=True)
+    arrived, own = together(arrived, own)
     other = tuple(lax.ppermute(w, "dp", [(0, 1), (1, 0)]) for w in own)
-    got = lax.all_to_all(packed_cache, "ep", split_axis=0, concat_axis=0, tiled=True)
 
     tables = []
     for main, minor in zip(*ORDERS):
@@ -453,13 +468,8 @@
             table[index] = number
         tables.append(jnp.array(table, jnp.int32))
     order = jnp.where(core == 0, tables[0], tables[1])
-    rows, mark = join_rows(order, arrived[0], arrived[1])
-    mark = mark.reshape(CHIPS * PICKS, MARK).astype(jnp.float32)
-    weight = mark[:, TOPK : 2 * TOPK] + mark[:, 2 * TOPK : 3 * TOPK] + mark[:, 3 * TOPK : 4 * TOPK]
-    weight = jnp.where(mark[:, :TOPK] == me.astype(jnp.float32), weight, 0.0)
-    weight = jnp.sum(weight, axis=1, keepdims=True)
-    produced = expert_rows(rows.reshape(CHIPS * PICKS, D), weight, (own, other))
-    outward = split_rows(order, produced.reshape(CHIPS, PICKS, D))
+    rows, part, weight = first_half(order, me, arrived[0], arrived[1], own)
+    outward = second_half(order, rows, part, weight, other)
     outward, got = lax.optimization_barrier((outward, got))
     got_slot = got[:, HALF - 1, 0].astype(jnp.int32)
     got_len = got[:, HALF - 1, 1].astype(jnp.int32)
@@ -467,10 +477,8 @@
     landing = jnp.sum(jnp.where(land_hit, expert_range[None, :], 0), axis=1)
     placed_len = jnp.sum(jnp.where(land_hit, got_len[None, :], 0), axis=1)
 
-    def contexts(earlier):
-        return attend(queries, new_kv, got, landing, placed_len, earlier)
-
-    sums, context = return_rows(outward, targets, ids, contexts)
+    context = attend(queries, new_kv, got, landing, placed_len)
+    sums, context = return_rows(outward, targets, ids, context)
     mixture = jnp.concatenate(sums, axis=1).reshape(STEPS, SLOTS, D)
     return context, mixture
 

time: 306 us -> 288 us (0.941)
  matrix products: 46.9 us -> 0 us
  Pallas kernels: 51.3 us -> 93.7 us
  local copies, waits for them, and re-layouts: 32.3 us -> 12.8 us
  waiting for transfers between devices: 86.5 us -> 105 us
  starting transfers between devices: 75 us -> 62.7 us
    dot_general x4 -> x0, matrix products: 46.9 us -> none  [the longest x2 32 us: expert_rows(): part = jnp.dot(inner, down_mat, preferred_element_type=jnp.float32)]
    pallas_call x4 -> x3, Pallas kernels: 36.4 us -> 78.9 us  [the longest x1 31.4 us: attend(): pl.pallas_call(attend_kernel, grid=(slots // GROUP,), out_shape=jax.Shape...]
    unnamed x77 -> x37, local copies, waits for them, and re-layouts: 30 us -> 9.78 us
    ppermute x36, starting transfers between devices: 62.7 us -> 52.2 us  [hop(): return lax.ppermute(value, ('dp', 'ep'), pairs)]
    ppermute x36, waiting for transfers between devices: 80.4 us -> 89.8 us  [hop(): return lax.ppermute(value, ('dp', 'ep'), pairs)]
    all_to_all x1, waiting for transfers between devices: 6.09 us -> 15.1 us  [on_device(): lax.all_to_all(packed_cache, 'ep', split_axis=0, concat_axis=0, tiled=True)]
  transfers between devices with their start and end apart: 40 -> 40, of which waited for: 14 -> 15; matrix products, arithmetic and copies ran while one was open for 18% -> 4% of each run, Pallas kernels for 15% -> 31%
where the time goes in v1:
time: 288 us; the launch traced here: 282 us
  waiting for transfers between devices  105 us (36%)
  Pallas kernels  93.7 us (33%)
  starting transfers between devices  62.7 us (22%)
  local copies, waits for them, and re-layouts  12.8 us (4%)
  other arithmetic  7.21 us (3%)
    ppermute x36, waiting for transfers between devices, hop(): return lax.ppermute(value, ('dp', 'ep'), pairs)  89.8 us
    ppermute x36, starting transfers between devices, hop(): return lax.ppermute(value, ('dp', 'ep'), pairs)  52.2 us
    pallas_call x1, Pallas kernels, attend(): pl.pallas_call(attend_kernel, grid=(slots // GROUP,), out_shape=jax.Shape...  31.4 us
    pallas_call x1, Pallas kernels, first_half(): pl.pallas_call(first_half_kernel, out_shape=[whole, whole, jax.ShapeDtype...  23.9 us
    pallas_call x1, Pallas kernels, second_half(): pl.pallas_call(second_half_kernel, out_shape=[jax.ShapeDtypeStruct(shape,...  23.6 us
    all_to_all x1, waiting for transfers between devices, on_device(): lax.all_to_all(packed_cache, 'ep', split_axis=0, concat_axis=0, tiled=True)  15.1 us
    all_to_all x1, starting transfers between devices, on_device(): lax.all_to_all(packed_cache, 'ep', split_axis=0, concat_axis=0, tiled=True)  9.82 us
    unnamed x37, local copies, waits for them, and re-layouts  9.78 us
  transfers between devices with their start and end apart: 40, of which 15 were waited for; matrix products, arithmetic and copies ran while one was open for 4% of the time, Pallas kernels for 31%

profile of v1, /device:TPU:10, one launch (start us, length us, event | category | flops | bytes accessed | tf_op | source)
XLA Modules:
  0.0 282.4 jit_solution(18369842600404179094)
XLA Ops:
  14.3 3.0 %collective-permute-done.4 = bf16[64,1280]{1,0:T(8,128)(2,1)S(1)} collective-permute-done((bf16[64,1280]{1,0:T(8,128)(2,1)S(1)}, bf16[64,1280]{1,0:T(8,128)(2,1)S(1)}, u32[]{:S(2)}, u32[]{:S(2)}) %collective-permute-start.4) | collective-permute-done | bytes 163872 | tf_op jit(solution)/shard_map/ppermute | solution.py:149
  30.5 7.3 %collective-permute-done.9.refs_1_ = bf16[256,1280]{1,0:T(8,128)(2,1)S(1)} collective-permute-done((bf16[256,1280]{1,0:T(8,128)(2,1)S(1)}, bf16[256,1280]{1,0:T(8,128)(2,1)S(1)}, u32[]{:S(2)}, u32[]{:S(2)}) %collective-permute-start.9) | collective-permute-done | bytes 655392 | tf_op jit(solution)/shard_map/ppermute | solution.py:149
  45.2 11.6 %collective-permute-done.10.refs_2_ = bf16[256,1280]{1,0:T(8,128)(2,1)} collective-permute-done((bf16[256,1280]{1,0:T(8,128)(2,1)S(1)}, bf16[256,1280]{1,0:T(8,128)(2,1)}, u32[]{:S(2)}, u32[]{:S(2)}) %collective-permute-start.10) | collective-permute-done | bytes 655392 | tf_op jit(solution)/shard_map/ppermute | solution.py:149
  58.6 2.7 shard_map.142
  61.4 4.6 %shard_map.141 = (bf16[16,16,2560]{2,1,0:T(8,128)(2,1)S(1)}, bf16[16,16,2560]{2,1,0:T(8,128)(2,1)S(1)}, bf16[16,16,2560]{2,1,0:T(8,128)(2,1)S(1)}, bf16[16,16,2560]{2,1,0:T(8,128)(2,1)S(1)}, f32[4,8,256]{2,1,0:T(8,128)S(1)}) custom-call(s32[4]{0:T(128)S(1)} %pad_add_fusion.targets_ref, bf16[256,2560]{1,0:T(8,128)(2,1)} %constant_dynamic-update-slice_fusion.refs_0_, ...), custom_call_target="tpu_custom_call" | custom-call | flops 1342177280 | bytes 10485760 | tf_op jit(solution)/shard_map/pallas_call | solution.py:193
  75.6 12.2 %collective-permute-done.16.refs_6_ = bf16[16,16,1280]{2,1,0:T(8,128)(2,1)S(1)} collective-permute-done((bf16[16,16,1280]{2,1,0:T(8,128)(2,1)S(1)}, bf16[16,16,1280]{2,1,0:T(8,128)(2,1)S(1)}, u32[]{:S(2)}, u32[]{:S(2)}) %collective-permute-start.16) | collective-permute-done | bytes 655392 | tf_op jit(solution)/shard_map/ppermute | solution.py:149
  87.8 13.3 %collective-permute-done.17.refs_7_ = bf16[16,16,1280]{2,1,0:T(8,128)(2,1)S(1)} collective-permute-done((bf16[16,16,1280]{2,1,0:T(8,128)(2,1)S(1)}, bf16[16,16,1280]{2,1,0:T(8,128)(2,1)S(1)}, u32[]{:S(2)}, u32[]{:S(2)}) %collective-permute-start.17) | collective-permute-done | bytes 655392 | tf_op jit(solution)/shard_map/ppermute | solution.py:149
  103.2 9.8 %all-to-all-start = ((bf16[64,32,1152]{2,1,0:T(8,128)(2,1)}), bf16[64,32,1152]{2,1,0:T(8,128)(2,1)}, u32[]{:S(2)}, u32[]{:S(2)}) async-start(bf16[64,32,1152]{2,1,0:T(8,128)(2,1)} %copy-done), calls=%async_computation | async-start | bytes 9437184 | tf_op jit(solution)/shard_map/all_to_all | solution.py:457
  113.1 23.9 %shard_map.143 = (bf16[64,16,3584]{2,1,0:T(8,128)(2,1)}, bf16[64,16,3584]{2,1,0:T(8,128)(2,1)}, f32[64,16,128]{2,1,0:T(8,128)S(1)}) custom-call(s32[64]{0:T(128)S(1)} %broadcast_select_fusion.order_ref, s32[1]{0:T(128)} %bitcast.me_ref, bf16[16,16,2560]{2,1,0:T(8,128)(2,1)} %copy-done.4, bf16[16,16,2560]{2,1,0:T(8,128)(2,1)} %copy-done.10, ...), custom_call_target="tpu_custom_call" | custom-call | flops 11274289152 | bytes 33030144 | tf_op jit(solution)/shard_map/pallas_call | solution.py:353
  137.0 23.6 %shard_map.144 = (bf16[16,16,2432]{2,1,0:T(8,128)(2,1)}, bf16[16,16,2432]{2,1,0:T(8,128)(2,1)}, bf16[16,16,2432]{2,1,0:T(8,128)(2,1)}, bf16[16,16,2432]{2,1,0:T(...) custom-call(s32[64]{0:T(128)S(1)} %broadcast_select_fusion.order_ref, ...), custom_call_target="tpu_custom_call" | custom-call | flops 11274289152 | bytes 33030144 | tf_op jit(solution)/shard_map/pallas_call | solution.py:366
  160.6 15.1 %all-to-all-done.got_ref = bf16[64,32,1152]{2,1,0:T(8,128)(2,1)} async-done(((bf16[64,32,1152]{2,1,0:T(8,128)(2,1)}), bf16[64,32,1152]{2,1,0:T(8,128)(2,1)}, u32[]{:S(2)}, u32[]{:S(2)}) %all-to-all-start) | async-done | bytes 4718624 | tf_op jit(solution)/shard_map/all_to_all | solution.py:457
  179.7 3.4 %convert_reduce_fusion = (s32[64]{0:T(128)S(1)}, s32[64]{0:T(128)S(1)}) fusion(bf16[64,32,1152]{2,1,0:T(8,128)(2,1)} %all-to-all-done.got_ref), kind=kLoop, calls=%fused_computation.7 | loop fusion | flops 128 | bytes 768 | tf_op jit(solution)/shard_map/convert_element_type | solution.py:475
  184.7 5.1 %collective-permute-done.24.refs_1_ = bf16[16,16,1152]{2,1,0:T(8,128)(2,1)} collective-permute-done((bf16[16,16,1152]{2,1,0:T(8,128)(2,1)}, bf16[16,16,1152]{2,1,0:T(8,128)(2,1)}, u32[]{:S(2)}, u32[]{:S(2)}) %collective-permute-start.24) | collective-permute-done | bytes 589856 | tf_op jit(solution)/shard_map/ppermute | solution.py:149
  189.8 31.4 %shard_map.145 = bf16[2,32,32768]{2,1,0:T(8,128)(2,1)} custom-call(s32[32]{0:T(128)S(1)} %get-tuple-element.185.landing_ref, bf16[64,32,1152]{2,1,0:T(8,128)(2,1)} %all-to-all-done.got_ref, s32[32,1]{1,0:T(8,128)S(1)} %copy.20.len_ref, bf16[2,32,576]{2,1,0:T(8,128)(2,1)S(1)} %copy-done.5, bf16[2,32,36864]{2,1,0:T(8,128)(2,1)} %query_ref.1), custom_call_target="tpu_custom_call" | custom-call | flops 9965666304 | bytes 8912896 | tf_op jit(solution)/shard_map/pallas_call | solution.py:115
  221.3 3.6 %shard_map.146 = (bf16[256,2432]{1,0:T(8,128)(2,1)S(1)}, bf16[256,2432]{1,0:T(8,128)(2,1)S(1)}, bf16[256,2432]{1,0:T(8,128)(2,1)S(1)}, bf16[256,2432]{1,0:T(8,128)(2,1)S(1)}) custom-call(s32[4]{0:T(128)S(1)} %pad_add_fusion.targets_ref, f32[4,8,256]{2,1,0:T(8,128)S(1)} %get-tuple-element.148.ids_ref, bf16[16,16,2432]{2,1,0:T(8,128)(2,1)S(1)} %copy-done.1, ...), custom_call_target="tpu_custom_call" | custom-call | flops 1275068416 | bytes 9961472 | tf_op jit(solution)/shard_map/pallas_call | solution.py:221
  227.0 4.7 %collective-permute-start.29 = (bf16[256,2432]{1,0:T(8,128)(2,1)S(1)}, bf16[256,2432]{1,0:T(8,128)(2,1)S(1)}, u32[]{:S(2)}, u32[]{:S(2)}) collective-permute-start(bf16[256,2432]{1,0:T(8,128)(2,1)S(1)} %get-tuple-element.156), channel_id=1, source_target_pairs={{0,8},{1,9},{2,10},{3,11},{4,12},{5,13},{6,14},{7,15},{8,0},{9,1},... | collective-permute-start | bytes 3735560 | tf_op jit(solution)/shard_map/ppermute | solution.py:149
  231.7 2.6 shard_map.147
  236.4 10.2 %collective-permute-done.30 = bf16[256,1152]{1,0:T(8,128)(2,1)S(1)} collective-permute-done((bf16[256,1152]{1,0:T(8,128)(2,1)S(1)}, bf16[256,1152]{1,0:T(8,128)(2,1)S(1)}, u32[]{:S(2)}, u32[]{:S(2)}) %collective-permute-start.30) | collective-permute-done | bytes 589856 | tf_op jit(solution)/shard_map/ppermute | solution.py:149
  246.7 2.4 collective-permute-start.32
  249.1 13.6 %collective-permute-done.31 = bf16[256,1152]{1,0:T(8,128)(2,1)S(1)} collective-permute-done((bf16[256,1152]{1,0:T(8,128)(2,1)S(1)}, bf16[256,1152]{1,0:T(8,128)(2,1)S(1)}, u32[]{:S(2)}, u32[]{:S(2)}) %collective-permute-start.31) | collective-permute-done | bytes 589856 | tf_op jit(solution)/shard_map/ppermute | solution.py:149
  266.5 4.5 %collective-permute-start.36 = (bf16[64,1152]{1,0:T(8,128)(2,1)S(1)}, bf16[64,1152]{1,0:T(8,128)(2,1)S(1)}, u32[]{:S(2)}, u32[]{:S(2)}) collective-permute-start(bf16[64,1152]{1,0:T(8,128)(2,1)S(1)} %get-tuple-element.195), channel_id=1, source_target_pairs={{0,3},{1,0},{2,1},{3,2},{4,7},{5,4},{6,5},{7,6},{8,11},{9,8},{10,9... | collective-permute-start | bytes 442376 | tf_op jit(solution)/shard_map/ppermute | solution.py:149
  271.5 3.1 %collective-permute-done.36 = bf16[64,1152]{1,0:T(8,128)(2,1)S(1)} collective-permute-done((bf16[64,1152]{1,0:T(8,128)(2,1)S(1)}, bf16[64,1152]{1,0:T(8,128)(2,1)S(1)}, u32[]{:S(2)}, u32[]{:S(2)}) %collective-permute-start.36) | collective-permute-done | bytes 147488 | tf_op jit(solution)/shard_map/ppermute | solution.py:149
  274.6 2.8 collective-permute-start.38
  277.4 3.9 %collective-permute-done.38 = bf16[64,1152]{1,0:T(8,128)(2,1)S(1)} collective-permute-done((bf16[64,1152]{1,0:T(8,128)(2,1)S(1)}, bf16[64,1152]{1,0:T(8,128)(2,1)S(1)}, u32[]{:S(2)}, u32[]{:S(2)}) %collective-permute-start.38) | collective-permute-done | bytes 147488 | tf_op jit(solution)/shard_map/ppermute | solution.py:149
  (128 shorter events, 62.7 us)
Async XLA Ops:
  19.9 17.9 %collective-permute-start.9 = (bf16[256,1280]{1,0:T(8,128)(2,1)S(1)}, bf16[256,1280]{1,0:T(8,128)(2,1)S(1)}, u32[]{:S(2)}, u32[]{:S(2)}) collective-permute-start(bf16[256,1280]{1,0:T(8,128)(2,1)S(1)} %constant_dynamic-update-slice_fusion.4.refs_0_), channel_id=1, source_target_pairs={{0,16},{1,17},{2,18},{3,19},{4,20},{5,21},{6,22},{7,23},{8,24},{9,... | collective-permute-start | bytes 1966088 | tf_op jit(solution)/shard_map/ppermute | solution.py:149
  24.4 32.4 %collective-permute-start.6 = (bf16[256,2560]{1,0:T(8,128)(2,1)}, bf16[256,2560]{1,0:T(8,128)(2,1)}, u32[]{:S(2)}, u32[]{:S(2)}) collective-permute-start(bf16[256,2560]{1,0:T(8,128)(2,1)} %constant_dynamic-update-slice_fusion.refs_0_), channel_id=1, source_target_pairs={{0,4},{1,5},{2,6},{3,7},{4,8},{5,9},{6,10},{7,11},{8,12},{9,13},{1... | collective-permute-start | bytes 3932168 | tf_op jit(solution)/shard_map/ppermute | solution.py:149
  26.0 30.8 %collective-permute-start.7 = (bf16[256,2560]{1,0:T(8,128)(2,1)}, bf16[256,2560]{1,0:T(8,128)(2,1)}, u32[]{:S(2)}, u32[]{:S(2)}) collective-permute-start(bf16[256,2560]{1,0:T(8,128)(2,1)} %constant_dynamic-update-slice_fusion.refs_0_), channel_id=1, source_target_pairs={{0,12},{1,13},{2,14},{3,15},{4,0},{5,1},{6,2},{7,3},{8,4},{9,5},{1... | collective-permute-start | bytes 3932168 | tf_op jit(solution)/shard_map/ppermute | solution.py:149
  26.4 32.2 %collective-permute-start.8 = (bf16[256,2560]{1,0:T(8,128)(2,1)}, bf16[256,2560]{1,0:T(8,128)(2,1)}, u32[]{:S(2)}, u32[]{:S(2)}) collective-permute-start(bf16[256,2560]{1,0:T(8,128)(2,1)} %constant_dynamic-update-slice_fusion.refs_0_), channel_id=1, source_target_pairs={{0,8},{1,9},{2,10},{3,11},{4,12},{5,13},{6,14},{7,15},{8,0},{9,1},... | collective-permute-start | bytes 3932168 | tf_op jit(solution)/shard_map/ppermute | solution.py:149
  28.7 28.1 %collective-permute-start.10 = (bf16[256,1280]{1,0:T(8,128)(2,1)S(1)}, bf16[256,1280]{1,0:T(8,128)(2,1)}, u32[]{:S(2)}, u32[]{:S(2)}) collective-permute-start(bf16[256,1280]{1,0:T(8,128)(2,1)S(1)} %constant_dynamic-update-slice_fusion.4.refs_0_), channel_id=1, source_target_pairs={{0,48},{1,49},{2,50},{3,51},{4,52},{5,53},{6,54},{7,55},{8,56},{9,... | collective-permute-start | bytes 1966088 | tf_op jit(solution)/shard_map/ppermute | solution.py:149
  38.7 18.1 %collective-permute-start.11 = (bf16[256,1280]{1,0:T(8,128)(2,1)S(1)}, bf16[256,1280]{1,0:T(8,128)(2,1)}, u32[]{:S(2)}, u32[]{:S(2)}) collective-permute-start(bf16[256,1280]{1,0:T(8,128)(2,1)S(1)} %constant_dynamic-update-slice_fusion.4.refs_0_), channel_id=1, source_target_pairs={{0,32},{1,33},{2,34},{3,35},{4,36},{5,37},{6,38},{7,39},{8,40},{9,... | collective-permute-start | bytes 1966088 | tf_op jit(solution)/shard_map/ppermute | solution.py:149
  67.1 34.0 %collective-permute-start.12 = (bf16[16,16,2560]{2,1,0:T(8,128)(2,1)S(1)}, bf16[16,16,2560]{2,1,0:T(8,128)(2,1)S(1)}, u32[]{:S(2)}, u32[]{:S(2)}) collective-permute-start(bf16[16,16,2560]{2,1,0:T(8,128)(2,1)S(1)} %get-tuple-element.106), channel_id=1, source_target_pairs={{0,1},{1,2},{2,3},{3,0},{4,5},{5,6},{6,7},{7,4},{8,9},{9,10},{10,1... | collective-permute-start | bytes 3932168 | tf_op jit(solution)/shard_map/ppermute | solution.py:149
  68.3 32.8 %collective-permute-start.13 = (bf16[16,16,2560]{2,1,0:T(8,128)(2,1)S(1)}, bf16[16,16,2560]{2,1,0:T(8,128)(2,1)S(1)}, u32[]{:S(2)}, u32[]{:S(2)}) collective-permute-start(bf16[16,16,2560]{2,1,0:T(8,128)(2,1)S(1)} %get-tuple-element.107), channel_id=1, source_target_pairs={{0,3},{1,0},{2,1},{3,2},{4,7},{5,4},{6,5},{7,6},{8,11},{9,8},{10,9... | collective-permute-start | bytes 3932168 | tf_op jit(solution)/shard_map/ppermute | solution.py:149
  69.1 32.0 %collective-permute-start.14 = (bf16[16,16,2560]{2,1,0:T(8,128)(2,1)S(1)}, bf16[16,16,2560]{2,1,0:T(8,128)(2,1)S(1)}, u32[]{:S(2)}, u32[]{:S(2)}) collective-permute-start(bf16[16,16,2560]{2,1,0:T(8,128)(2,1)S(1)} %get-tuple-element.108), channel_id=1, source_target_pairs={{0,2},{1,3},{2,0},{3,1},{4,6},{5,7},{6,4},{7,5},{8,10},{9,11},{10,... | collective-permute-start | bytes 3932168 | tf_op jit(solution)/shard_map/ppermute | solution.py:149
  74.3 26.8 %collective-permute-start.17 = (bf16[16,16,1280]{2,1,0:T(8,128)(2,1)S(1)}, bf16[16,16,1280]{2,1,0:T(8,128)(2,1)S(1)}, u32[]{:S(2)}, u32[]{:S(2)}) collective-permute-start(bf16[16,16,1280]{2,1,0:T(8,128)(2,1)S(1)} %get-tuple-element.116), channel_id=1, source_target_pairs={{0,8},{1,9},{2,10},{3,11},{4,12},{5,13},{6,14},{7,15},{8,0},{9,1},... | collective-permute-start | bytes 1966088 | tf_op jit(solution)/shard_map/ppermute | solution.py:149
  102.6 34.4 %collective-permute-start.18 = (bf16[3584,512]{1,0:T(8,128)(2,1)}, bf16[3584,512]{1,0:T(8,128)(2,1)}, u32[]{:S(2)}, u32[]{:S(2)}) collective-permute-start(bf16[3584,512]{1,0:T(8,128)(2,1)} %bitcast.13.refs_8_), channel_id=1, source_target_pairs={{0,64},{64,0},{1,65},{65,1},{2,66},{66,2},{3,67},{67,3},{4,68},{68... | collective-permute-start | bytes 11010056 | tf_op jit(solution)/shard_map/ppermute | solution.py:459
  102.6 34.4 %collective-permute-start.19 = (bf16[3584,512]{1,0:T(8,128)(2,1)}, bf16[3584,512]{1,0:T(8,128)(2,1)}, u32[]{:S(2)}, u32[]{:S(2)}) collective-permute-start(bf16[3584,512]{1,0:T(8,128)(2,1)} %bitcast.14.refs_9_), channel_id=1, source_target_pairs={{0,64},{64,0},{1,65},{65,1},{2,66},{66,2},{3,67},{67,3},{4,68},{68... | collective-permute-start | bytes 11010056 | tf_op jit(solution)/shard_map/ppermute | solution.py:459
  103.1 33.9 %collective-permute-start.20 = (bf16[512,3584]{1,0:T(8,128)(2,1)}, bf16[512,3584]{1,0:T(8,128)(2,1)}, u32[]{:S(2)}, u32[]{:S(2)}) collective-permute-start(bf16[512,3584]{1,0:T(8,128)(2,1)} %bitcast.15.refs_10_), channel_id=1, source_target_pairs={{0,64},{64,0},{1,65},{65,1},{2,66},{66,2},{3,67},{67,3},{4,68},{68... | collective-permute-start | bytes 11010056 | tf_op jit(solution)/shard_map/ppermute | solution.py:459
  103.2 72.5 %all-to-all-start = ((bf16[64,32,1152]{2,1,0:T(8,128)(2,1)}), bf16[64,32,1152]{2,1,0:T(8,128)(2,1)}, u32[]{:S(2)}, u32[]{:S(2)}) async-start(bf16[64,32,1152]{2,1,0:T(8,128)(2,1)} %copy-done), calls=%async_computation | async-start | bytes 9437184 | tf_op jit(solution)/shard_map/all_to_all | solution.py:457
  175.7 45.5 %collective-permute-start.21 = (bf16[16,16,2432]{2,1,0:T(8,128)(2,1)}, bf16[16,16,2432]{2,1,0:T(8,128)(2,1)S(1)}, u32[]{:S(2)}, u32[]{:S(2)}) collective-permute-start(bf16[16,16,2432]{2,1,0:T(8,128)(2,1)} %get-tuple-element.140), channel_id=1, source_target_pairs={{0,3},{1,0},{2,1},{3,2},{4,7},{5,4},{6,5},{7,6},{8,11},{9,8},{10,9... | collective-permute-start | bytes 3735560 | tf_op jit(solution)/shard_map/ppermute | solution.py:149
  175.7 45.5 %collective-permute-start.22 = (bf16[16,16,2432]{2,1,0:T(8,128)(2,1)}, bf16[16,16,2432]{2,1,0:T(8,128)(2,1)S(1)}, u32[]{:S(2)}, u32[]{:S(2)}) collective-permute-start(bf16[16,16,2432]{2,1,0:T(8,128)(2,1)} %get-tuple-element.141), channel_id=1, source_target_pairs={{0,1},{1,2},{2,3},{3,0},{4,5},{5,6},{6,7},{7,4},{8,9},{9,10},{10,1... | collective-permute-start | bytes 3735560 | tf_op jit(solution)/shard_map/ppermute | solution.py:149
  177.7 43.5 %collective-permute-start.23 = (bf16[16,16,2432]{2,1,0:T(8,128)(2,1)}, bf16[16,16,2432]{2,1,0:T(8,128)(2,1)}, u32[]{:S(2)}, u32[]{:S(2)}) collective-permute-start(bf16[16,16,2432]{2,1,0:T(8,128)(2,1)} %get-tuple-element.142), channel_id=1, source_target_pairs={{0,2},{1,3},{2,0},{3,1},{4,6},{5,7},{6,4},{7,5},{8,10},{9,11},{10,... | collective-permute-start | bytes 3735560 | tf_op jit(solution)/shard_map/ppermute | solution.py:149
  183.4 37.9 %collective-permute-start.25 = (bf16[16,16,1152]{2,1,0:T(8,128)(2,1)}, bf16[16,16,1152]{2,1,0:T(8,128)(2,1)S(1)}, u32[]{:S(2)}, u32[]{:S(2)}) collective-permute-start(bf16[16,16,1152]{2,1,0:T(8,128)(2,1)} %get-tuple-element.144), channel_id=1, source_target_pairs={{0,4},{1,5},{2,6},{3,7},{4,8},{5,9},{6,10},{7,11},{8,12},{9,13},{1... | collective-permute-start | bytes 1769480 | tf_op jit(solution)/shard_map/ppermute | solution.py:149
  189.8 31.4 %collective-permute-start.26 = (bf16[16,16,1152]{2,1,0:T(8,128)(2,1)}, bf16[16,16,1152]{2,1,0:T(8,128)(2,1)S(1)}, u32[]{:S(2)}, u32[]{:S(2)}) collective-permute-start(bf16[16,16,1152]{2,1,0:T(8,128)(2,1)} %get-tuple-element.145), channel_id=1, source_target_pairs={{0,8},{1,9},{2,10},{3,11},{4,12},{5,13},{6,14},{7,15},{8,0},{9,1},... | collective-permute-start | bytes 1769480 | tf_op jit(solution)/shard_map/ppermute | solution.py:149
  224.9 37.8 %collective-permute-start.27 = (bf16[256,2432]{1,0:T(8,128)(2,1)S(1)}, bf16[256,2432]{1,0:T(8,128)(2,1)S(1)}, u32[]{:S(2)}, u32[]{:S(2)}) collective-permute-start(bf16[256,2432]{1,0:T(8,128)(2,1)S(1)} %get-tuple-element.154), channel_id=1, source_target_pairs={{0,12},{1,13},{2,14},{3,15},{4,0},{5,1},{6,2},{7,3},{8,4},{9,5},{1... | collective-permute-start | bytes 3735560 | tf_op jit(solution)/shard_map/ppermute | solution.py:149
  226.6 36.2 %collective-permute-start.28 = (bf16[256,2432]{1,0:T(8,128)(2,1)S(1)}, bf16[256,2432]{1,0:T(8,128)(2,1)S(1)}, u32[]{:S(2)}, u32[]{:S(2)}) collective-permute-start(bf16[256,2432]{1,0:T(8,128)(2,1)S(1)} %get-tuple-element.155), channel_id=1, source_target_pairs={{0,4},{1,5},{2,6},{3,7},{4,8},{5,9},{6,10},{7,11},{8,12},{9,13},{1... | collective-permute-start | bytes 3735560 | tf_op jit(solution)/shard_map/ppermute | solution.py:149
  227.0 35.7 %collective-permute-start.29 = (bf16[256,2432]{1,0:T(8,128)(2,1)S(1)}, bf16[256,2432]{1,0:T(8,128)(2,1)S(1)}, u32[]{:S(2)}, u32[]{:S(2)}) collective-permute-start(bf16[256,2432]{1,0:T(8,128)(2,1)S(1)} %get-tuple-element.156), channel_id=1, source_target_pairs={{0,8},{1,9},{2,10},{3,11},{4,12},{5,13},{6,14},{7,15},{8,0},{9,1},... | collective-permute-start | bytes 3735560 | tf_op jit(solution)/shard_map/ppermute | solution.py:149
  236.4 26.3 %collective-permute-start.31 = (bf16[256,1152]{1,0:T(8,128)(2,1)S(1)}, bf16[256,1152]{1,0:T(8,128)(2,1)S(1)}, u32[]{:S(2)}, u32[]{:S(2)}) collective-permute-start(bf16[256,1152]{1,0:T(8,128)(2,1)S(1)} %get-tuple-element.164), channel_id=1, source_target_pairs={{0,16},{1,17},{2,18},{3,19},{4,20},{5,21},{6,22},{7,23},{8,24},{9,... | collective-permute-start | bytes 1769480 | tf_op jit(solution)/shard_map/ppermute | solution.py:149
  263.5 17.9 %collective-permute-start.33 = (bf16[64,2432]{1,0:T(8,128)(2,1)S(1)}, bf16[64,2432]{1,0:T(8,128)(2,1)S(1)}, u32[]{:S(2)}, u32[]{:S(2)}) collective-permute-start(bf16[64,2432]{1,0:T(8,128)(2,1)S(1)} %get-tuple-element.191), channel_id=1, source_target_pairs={{0,48},{1,49},{2,50},{3,51},{4,52},{5,53},{6,54},{7,55},{8,56},{9,... | collective-permute-start | bytes 933896 | tf_op jit(solution)/shard_map/ppermute | solution.py:149
  (31 other events, 353.4 us)

commit v2 on v1

--- a/solution.py
+++ b/solution.py
@@ -18,7 +18,7 @@
 WIDE = 640
 SIDE = 4
 Z, Y, X = SIDE * SIDE, SIDE, 1
-MAIN = 2432
+MAIN = 2560
 MINOR = D - MAIN
 MARK = 128
 SLOTS = 32
@@ -30,7 +30,8 @@
 CHIPS = SIDE**3
 BLOCK = 32
 ORDERS = (((Z, Y, X), (Y, X, Z)), ((X, Z, Y), (X, Z, Y)))
-TARGETS = (0, 1, -1, 2)
+SOURCES = (0, -1, 2, 1)
+TARGETS = (0, 1, 2, -1)
 KEYS = GROUP * (CTX + STEPS)
 
 
@@ -38,7 +39,6 @@
 
 
 def attend_kernel(landing_ref, got_ref, len_ref, new_ref, query_ref, out_ref, even_ref, odd_ref, value_ref, bias_ref):
-    group = pl.program_id(0)
     pairs = GROUP * HALF
 
     def lanes(rows):
@@ -50,7 +50,7 @@
         value_ref[pl.ds(at, rows), :] = keys[:, :LAT].astype(jnp.bfloat16)
 
     def one(slot, carry):
-        source = landing_ref[group * GROUP + slot]
+        source = landing_ref[slot]
         block = got_ref[source]
         first = jnp.where(lanes(HALF) < KVW, block[:, :WIDE].astype(jnp.float32), 0.0)
         at = pl.multiple_of(slot * HALF, HALF)
@@ -110,33 +110,45 @@
     lax.fori_loop(0, H // (2 * TOGETHER), heads, 0)
 
 
-def attend(queries, new_kv, got, landing, placed_len):
+def attend(queries, new_kv, got, landing, placed_len, earlier):
     slots = queries.shape[1]
+    group = 0 if earlier is None else 1
+    specs = [
+        pl.BlockSpec(memory_space=pltpu.SMEM),
+        pl.BlockSpec(memory_space=pltpu.VMEM),
+        pl.BlockSpec((GROUP, 1), lambda g: (group, 0)),
+        pl.BlockSpec((STEPS, GROUP, KVW), lambda g: (0, group, 0)),
+        pl.BlockSpec((STEPS, GROUP, H * KVW), lambda g: (0, group, 0)),
+    ]
+    operands = [landing[group * GROUP :][:GROUP], got, placed_len[:, None], new_kv, queries]
+    kernel = attend_kernel
+    if earlier is not None:
+        specs.append(pl.BlockSpec(memory_space=pl.ANY))
+        operands.append(earlier)
+
+        def kernel(*refs):
+            attend_kernel(*refs[:5], *refs[6:])
+
     return pl.pallas_call(
-        attend_kernel,
-        grid=(slots // GROUP,),
+        kernel,
+        grid=(1,),
         out_shape=jax.ShapeDtypeStruct((STEPS, slots, H * LAT), jnp.bfloat16),
-        in_specs=[
-            pl.BlockSpec(memory_space=pltpu.SMEM),
-            pl.BlockSpec(memory_space=pltpu.VMEM),
-            pl.BlockSpec((GROUP, 1), lambda g: (g, 0)),
-            pl.BlockSpec((STEPS, GROUP, KVW), lambda g: (0, g, 0)),
-            pl.BlockSpec((STEPS, GROUP, H * KVW), lambda g: (0, g, 0)),
-        ],
-        out_specs=pl.BlockSpec((STEPS, GROUP, H * LAT), lambda g: (0, g, 0)),
+        in_specs=specs,
+        out_specs=pl.BlockSpec((STEPS, GROUP, H * LAT), lambda g: (0, group, 0)),
         scratch_shapes=[
             pltpu.VMEM((KEYS, WIDE), jnp.bfloat16),
             pltpu.VMEM((KEYS, WIDE), jnp.bfloat16),
             pltpu.VMEM((KEYS, LAT), jnp.bfloat16),
             pltpu.VMEM((STEPS * GROUP, KEYS), jnp.float32),
         ],
-        compiler_params=pltpu.CompilerParams(vmem_limit_bytes=48 * 2**20),
+        input_output_aliases={} if earlier is None else {5: 0},
+        compiler_params=pltpu.CompilerParams(vmem_limit_bytes=32 * 2**20),
         cost_estimate=pl.CostEstimate(
-            flops=2 * STEPS * slots * H * KEYS * (WIDE + LAT),
-            bytes_accessed=2 * STEPS * slots * H * (KVW + LAT),
-            transcendentals=STEPS * slots * H * KEYS,
+            flops=2 * STEPS * GROUP * H * KEYS * (WIDE + LAT),
+            bytes_accessed=2 * STEPS * GROUP * H * (KVW + LAT),
+            transcendentals=STEPS * GROUP * H * KEYS,
         ),
-    )(landing, got, placed_len[:, None], new_kv, queries)
+    )(*operands)
 
 
 def hop(value, strides, delta):
@@ -245,30 +257,34 @@
 def send_rows(columns, targets, packed_cache):
     first, second, third = stage_axes()
     both = range(len(columns))
-    rings = [exchange([columns[i]] * 3, first[i], (1, -1, 2)) for i in both]
+    rings = [exchange([columns[i]] * 3, first[i], TARGETS[1:]) for i in both]
     columns, rings = together(columns, rings)
     lines = [jnp.concatenate([columns[i]] + rings[i], axis=0) for i in both]
-    rings = [exchange([lines[i]] * 3, second[i], (1, -1, 2)) for i in both]
+    rings = [exchange([lines[i]] * 3, second[i], TARGETS[1:]) for i in both]
     packed_cache, rings[1][0] = together(packed_cache, rings[1][0])
     lines, rings = together(lines, rings)
-    picked = [select(targets[i], [lines[i]] + rings[i]) for i in both]
+    picked = [list(select(targets[0], [lines[0]] + rings[0]))]
+    lines[1], picked[0][SIDE] = together(lines[1], picked[0][SIDE])
+    picked.append(select(targets[1], [lines[1]] + rings[1]))
     rings = [exchange(picked[i][1:SIDE], third[i], TARGETS[1:]) for i in both]
     return [[picked[i][0]] + rings[i] for i in both], [p[SIDE] for p in picked], packed_cache
 
 
-def return_rows(outward, targets, ids, context):
+def return_rows(outward, targets, ids, contexts):
     first, second, third = stage_axes()
     both = range(len(outward))
-    rings = [exchange(outward[i][1:], third[i], (-1, 1, 2)) for i in both]
+    rings = [exchange(outward[i][1:], third[i], SOURCES[1:]) for i in both]
+    context = contexts(None)
     rings, context = together(rings, context)
     lines = [combine(targets[i], ids[i], [outward[i][0]] + rings[i]) for i in both]
-    rings = [exchange(lines[i][1:], second[i], (-1, 1, 2)) for i in both]
-    lines, rings = together(lines, rings)
+    rings = [exchange(lines[i][1:], second[i], SOURCES[1:]) for i in both]
+    context = contexts(context)
+    rings, context = together(rings, context)
     sums = []
     for i in both:
         line = add(lines[i][0], *rings[i])
         blocks = [line[k * ROWS : (k + 1) * ROWS] for k in range(SIDE)]
-        sums.append([blocks[0]] + exchange(blocks[1:], first[i], (-1, 1, 2)))
+        sums.append([blocks[0]] + exchange(blocks[1:], first[i], SOURCES[1:]))
     sums, = together(sums)
     return [add(*terms) for terms in sums], context
 
@@ -470,15 +486,16 @@
     order = jnp.where(core == 0, tables[0], tables[1])
     rows, part, weight = first_half(order, me, arrived[0], arrived[1], own)
     outward = second_half(order, rows, part, weight, other)
-    outward, got = lax.optimization_barrier((outward, got))
-    got_slot = got[:, HALF - 1, 0].astype(jnp.int32)
-    got_len = got[:, HALF - 1, 1].astype(jnp.int32)
+    got_mark = lax.optimization_barrier(got[:, HALF - 1, :128]).astype(jnp.int32)
+    got_slot, got_len = got_mark[:, 0], got_mark[:, 1]
     land_hit = got_slot[None, :] == slot_range[:, None]
     landing = jnp.sum(jnp.where(land_hit, expert_range[None, :], 0), axis=1)
     placed_len = jnp.sum(jnp.where(land_hit, got_len[None, :], 0), axis=1)
 
-    context = attend(queries, new_kv, got, landing, placed_len)
-    sums, context = return_rows(outward, targets, ids, context)
+    def contexts(earlier):
+        return attend(queries, new_kv, got, landing, placed_len, earlier)
+
+    sums, context = return_rows(outward, targets, ids, contexts)
     mixture = jnp.concatenate(sums, axis=1).reshape(STEPS, SLOTS, D)
     return context, mixture
 

time: 288 us -> 316 us (1.097)
  the two profiles are of different devices: /device:TPU:10 before, /device:TPU:24 now
where the time goes in v2:
time: 316 us
  waiting for transfers between devices  117 us (37%)
  Pallas kernels  97.9 us (31%)
  starting transfers between devices  75.6 us (24%)
  local copies, waits for them, and re-layouts  19.7 us (6%)
  other arithmetic  3.88 us (1%)
    ppermute x36, waiting for transfers between devices, hop(): return lax.ppermute(value, ('dp', 'ep'), pairs)  111 us
    ppermute x36, starting transfers between devices, hop(): return lax.ppermute(value, ('dp', 'ep'), pairs)  65.1 us
    pallas_call x2, Pallas kernels, attend(): pl.pallas_call(kernel, grid=(1,), out_shape=jax.ShapeDtypeStruct((STEPS,...  34.3 us
    pallas_call x1, Pallas kernels, first_half(): pl.pallas_call(first_half_kernel, out_shape=[whole, whole, jax.ShapeDtype...  23.9 us
    pallas_call x1, Pallas kernels, second_half(): pl.pallas_call(second_half_kernel, out_shape=[jax.ShapeDtypeStruct(shape,...  23.5 us
    unnamed x46, local copies, waits for them, and re-layouts  16.2 us
    all_to_all x1, starting transfers between devices, on_device(): lax.all_to_all(packed_cache, 'ep', split_axis=0, concat_axis=0, tiled=True)  9.98 us
    pallas_call x2, Pallas kernels, select(): pl.pallas_call(select_kernel, out_shape=[jax.ShapeDtypeStruct((PLANE, PIC...  8.42 us
  transfers between devices with their start and end apart: 40, of which 13 were waited for; matrix products, arithmetic and copies ran while one was open for 2% of the time, Pallas kernels for 28%

profile of v2, /device:TPU:24, one launch (start us, length us, event | category | flops | bytes accessed | tf_op | source)
XLA Modules:
  0.0 315.7 jit_solution(16265419134311850138)
XLA Ops:
  5.2 3.6 %collective-permute-start.1 = (bf16[64,2688]{1,0:T(8,128)(2,1)S(1)}, bf16[64,2688]{1,0:T(8,128)(2,1)S(1)}, u32[]{:S(2)}, u32[]{:S(2)}) collective-permute-start(bf16[64,2688]{1,0:T(8,128)(2,1)S(1)} %pad_maximum_fusion.1), channel_id=1, source_target_pairs={{0,32},{1,33},{2,34},{3,35},{4,36},{5,37},{6,38},{7,39},{8,40},{9,... | collective-permute-start | bytes 1032200 | tf_op jit(solution)/shard_map/ppermute | solution.py:161
  19.7 17.5 %collective-permute-done.5 = bf16[64,1152]{1,0:T(8,128)(2,1)S(1)} collective-permute-done((bf16[64,1152]{1,0:T(8,128)(2,1)S(1)}, bf16[64,1152]{1,0:T(8,128)(2,1)S(1)}, u32[]{:S(2)}, u32[]{:S(2)}) %collective-permute-start.5) | collective-permute-done | bytes 147488 | tf_op jit(solution)/shard_map/ppermute | solution.py:161
  37.4 2.8 collective-permute-start.7
  42.7 16.0 %collective-permute-done.9.refs_1_ = bf16[256,1152]{1,0:T(8,128)(2,1)} collective-permute-done((bf16[256,1152]{1,0:T(8,128)(2,1)S(1)}, bf16[256,1152]{1,0:T(8,128)(2,1)}, u32[]{:S(2)}, u32[]{:S(2)}) %collective-permute-start.9) | collective-permute-done | bytes 589856 | tf_op jit(solution)/shard_map/ppermute | solution.py:161
  63.1 8.6 %collective-permute-done.11.refs_3_ = bf16[256,1152]{1,0:T(8,128)(2,1)S(1)} collective-permute-done((bf16[256,1152]{1,0:T(8,128)(2,1)S(1)}, bf16[256,1152]{1,0:T(8,128)(2,1)S(1)}, u32[]{:S(2)}, u32[]{:S(2)}) %collective-permute-start.11) | collective-permute-done | bytes 589856 | tf_op jit(solution)/shard_map/ppermute | solution.py:161
  72.5 6.0 %shard_map.141 = (bf16[16,16,2688]{2,1,0:T(8,128)(2,1)S(1)}, bf16[16,16,2688]{2,1,0:T(8,128)(2,1)}, bf16[16,16,2688]{2,1,0:T(8,128)(2,1)}, bf16[16,16,2688]{2,1,0:T(8,128)(2,1)}, f32[4,8,256]{2,1,0:T(8,128)S(1)}) custom-call(s32[4]{0:T(128)S(1)} %pad_add_fusion.targets_ref, bf16[256,2688]{1,0:T(8,128)(2,1)S(1)} %constant_dynamic-update-slice_fusion.refs_0_, ...), custom_call_target="tpu_custom_call" | custom-call | flops 1409286144 | bytes 11010048 | tf_op jit(solution)/shard_map/pallas_call | solution.py:205
  79.5 16.8 %collective-permute-start.13 = (bf16[16,16,2688]{2,1,0:T(8,128)(2,1)}, bf16[16,16,2688]{2,1,0:T(8,128)(2,1)}, u32[]{:S(2)}, u32[]{:S(2)}) collective-permute-start(bf16[16,16,2688]{2,1,0:T(8,128)(2,1)} %get-tuple-element.102), channel_id=1, source_target_pairs={{0,2},{1,3},{2,0},{3,1},{4,6},{5,7},{6,4},{7,5},{8,10},{9,11},{10,... | collective-permute-start | bytes 4128776 | tf_op jit(solution)/shard_map/ppermute | solution.py:161
  104.0 12.8 %collective-permute-done.15.refs_5_ = bf16[16,16,1152]{2,1,0:T(8,128)(2,1)S(1)} collective-permute-done((bf16[16,16,1152]{2,1,0:T(8,128)(2,1)S(1)}, bf16[16,16,1152]{2,1,0:T(8,128)(2,1)S(1)}, u32[]{:S(2)}, u32[]{:S(2)}) %collective-permute-start.15) | collective-permute-done | bytes 589856 | tf_op jit(solution)/shard_map/ppermute | solution.py:161
  116.8 11.5 %collective-permute-done.17.refs_7_ = bf16[16,16,1152]{2,1,0:T(8,128)(2,1)S(1)} collective-permute-done((bf16[16,16,1152]{2,1,0:T(8,128)(2,1)S(1)}, bf16[16,16,1152]{2,1,0:T(8,128)(2,1)S(1)}, u32[]{:S(2)}, u32[]{:S(2)}) %collective-permute-start.17) | collective-permute-done | bytes 589856 | tf_op jit(solution)/shard_map/ppermute | solution.py:161
  129.6 10.0 %all-to-all-start = ((bf16[64,32,1152]{2,1,0:T(8,128)(2,1)}), bf16[64,32,1152]{2,1,0:T(8,128)(2,1)}, u32[]{:S(2)}, u32[]{:S(2)}) async-start(bf16[64,32,1152]{2,1,0:T(8,128)(2,1)} %copy-done), calls=%async_computation | async-start | bytes 9437184 | tf_op jit(solution)/shard_map/all_to_all | solution.py:473
  139.7 23.9 %shard_map.143 = (bf16[64,16,3584]{2,1,0:T(8,128)(2,1)}, bf16[64,16,3584]{2,1,0:T(8,128)(2,1)}, f32[64,16,128]{2,1,0:T(8,128)S(1)}) custom-call(s32[64]{0:T(128)S(1)} %broadcast_select_fusion.order_ref, s32[1]{0:T(128)} %bitcast.8.me_ref, bf16[16,16,2688]{2,1,0:T(8,128)(2,1)} %copy-done.8, bf16[16,16,2688]{2,1,0:T(8,128)(2,1)} %copy-done.16, ...), custom_call_target="tpu_custom_call" | custom-call | flops 11274289152 | bytes 33030144 | tf_op jit(solution)/shard_map/pallas_call | solution.py:369
  164.4 23.5 %shard_map.144 = (bf16[16,16,2560]{2,1,0:T(8,128)(2,1)}, bf16[16,16,2560]{2,1,0:T(8,128)(2,1)}, bf16[16,16,2560]{2,1,0:T(8,128)(2,1)}, bf16[16,16,2560]{2,1,0:T(...) custom-call(s32[64]{0:T(128)S(1)} %broadcast_select_fusion.order_ref, ...), custom_call_target="tpu_custom_call" | custom-call | flops 11274289152 | bytes 33030144 | tf_op jit(solution)/shard_map/pallas_call | solution.py:382
  194.0 6.8 %all-to-all-done.got_ref.refs_1_ = bf16[64,32,1152]{2,1,0:T(8,128)(2,1)} async-done(((bf16[64,32,1152]{2,1,0:T(8,128)(2,1)}), bf16[64,32,1152]{2,1,0:T(8,128)(2,1)}, u32[]{:S(2)}, u32[]{:S(2)}) %all-to-all-start) | async-done | bytes 4718624 | tf_op jit(solution)/shard_map/all_to_all | solution.py:473
  202.2 16.8 %collective-permute-done.24.refs_1_ = bf16[16,16,1024]{2,1,0:T(8,128)(2,1)} collective-permute-done((bf16[16,16,1024]{2,1,0:T(8,128)(2,1)}, bf16[16,16,1024]{2,1,0:T(8,128)(2,1)}, u32[]{:S(2)}, u32[]{:S(2)}) %collective-permute-start.24) | collective-permute-done | bytes 524320 | tf_op jit(solution)/shard_map/ppermute | solution.py:161
  221.5 17.2 %shard_map.145.refs_5_ = bf16[2,32,32768]{2,1,0:T(8,128)(2,1)} custom-call(s32[16]{0:T(128)S(1)} %get-tuple-element.187.landing_ref, bf16[64,32,1152]{2,1,0:T(8,128)(2,1)} %all-to-all-done.got_ref.refs_1_, s32[32,1]{1,0:T(8,128)S(1)} %copy.23.len_ref.refs_2_, bf16[2,32,576]{2,1,0:T(8,128)(2,1)S(1)} %copy-done.10, bf16[2,32,36864]{2,1,0:T(8,128)(2,1)S(1)} %copy-done.6), custom_call_target="tpu_custom_call" | custom-call | flops 4982833152 | bytes 4456448 | tf_op jit(solution)/shard_map/pallas_call | solution.py:132
  238.7 3.6 %shard_map.146 = (bf16[256,2560]{1,0:T(8,128)(2,1)S(1)}, bf16[256,2560]{1,0:T(8,128)(2,1)S(1)}, bf16[256,2560]{1,0:T(8,128)(2,1)S(1)}, bf16[256,2560]{1,0:T(8,128)(2,1)S(1)}) custom-call(s32[4]{0:T(128)S(1)} %pad_add_fusion.targets_ref, f32[4,8,256]{2,1,0:T(8,128)S(1)} %get-tuple-element.99.ids_ref, bf16[16,16,2560]{2,1,0:T(8,128)(2,1)S(1)} %copy-done.1, ...), custom_call_target="tpu_custom_call" | custom-call | flops 1342177280 | bytes 10485760 | tf_op jit(solution)/shard_map/pallas_call | solution.py:233
  244.4 2.8 collective-permute-start.29
  247.2 2.8 shard_map.147
  254.1 10.9 %collective-permute-done.30 = bf16[256,1024]{1,0:T(8,128)(2,1)S(1)} collective-permute-done((bf16[256,1024]{1,0:T(8,128)(2,1)S(1)}, bf16[256,1024]{1,0:T(8,128)(2,1)S(1)}, u32[]{:S(2)}, u32[]{:S(2)}) %collective-permute-start.30) | collective-permute-done | bytes 524320 | tf_op jit(solution)/shard_map/ppermute | solution.py:161
  265.0 10.8 %collective-permute-start.32 = (bf16[256,1024]{1,0:T(8,128)(2,1)S(1)}, bf16[256,1024]{1,0:T(8,128)(2,1)S(1)}, u32[]{:S(2)}, u32[]{:S(2)}) collective-permute-start(bf16[256,1024]{1,0:T(8,128)(2,1)S(1)} %get-tuple-element.147), channel_id=1, source_target_pairs={{0,16},{1,17},{2,18},{3,19},{4,20},{5,21},{6,22},{7,23},{8,24},{9,... | collective-permute-start | bytes 1572872 | tf_op jit(solution)/shard_map/ppermute | solution.py:161
  278.1 17.1 %shard_map.148 = bf16[2,32,32768]{2,1,0:T(8,128)(2,1)} custom-call(s32[16]{0:T(128)S(1)} %get-tuple-element.186.refs_0_, bf16[64,32,1152]{2,1,0:T(8,128)(2,1)} %all-to-all-done.got_ref.refs_1_, s32[32,1]{1,0:T(8,128)S(1)} %copy.23.len_ref.refs_2_, bf16[2,32,576]{2,1,0:T(8,128)(2,1)S(1)} %copy-done.10, ...), custom_call_target="tpu_custom_call", output_to_operand_aliasing={{}: (5, {})} | custom-call | flops 4982833152 | bytes 4456448 | tf_op jit(solution)/shard_map/pallas_call | solution.py:132
  301.0 3.7 %collective-permute-done.36 = bf16[64,1024]{1,0:T(8,128)(2,1)S(1)} collective-permute-done((bf16[64,1024]{1,0:T(8,128)(2,1)S(1)}, bf16[64,1024]{1,0:T(8,128)(2,1)S(1)}, u32[]{:S(2)}, u32[]{:S(2)}) %collective-permute-start.36) | collective-permute-done | bytes 131104 | tf_op jit(solution)/shard_map/ppermute | solution.py:161
  305.0 3.5 %collective-permute-done.37 = bf16[64,1024]{1,0:T(8,128)(2,1)S(1)} collective-permute-done((bf16[64,1024]{1,0:T(8,128)(2,1)S(1)}, bf16[64,1024]{1,0:T(8,128)(2,1)S(1)}, u32[]{:S(2)}, u32[]{:S(2)}) %collective-permute-start.37) | collective-permute-done | bytes 131104 | tf_op jit(solution)/shard_map/ppermute | solution.py:161
  308.5 6.2 %collective-permute-done.38 = bf16[64,1024]{1,0:T(8,128)(2,1)S(1)} collective-permute-done((bf16[64,1024]{1,0:T(8,128)(2,1)S(1)}, bf16[64,1024]{1,0:T(8,128)(2,1)S(1)}, u32[]{:S(2)}, u32[]{:S(2)}) %collective-permute-start.38) | collective-permute-done | bytes 131104 | tf_op jit(solution)/shard_map/ppermute | solution.py:161
  (141 shorter events, 59.4 us)
Async XLA Ops:
  3.2 34.0 %collective-permute-start = (bf16[64,2688]{1,0:T(8,128)(2,1)S(1)}, bf16[64,2688]{1,0:T(8,128)(2,1)S(1)}, u32[]{:S(2)}, u32[]{:S(2)}) collective-permute-start(bf16[64,2688]{1,0:T(8,128)(2,1)S(1)} %pad_maximum_fusion.1), channel_id=1, source_target_pairs={{0,16},{1,17},{2,18},{3,19},{4,20},{5,21},{6,22},{7,23},{8,24},{9,... | collective-permute-start | bytes 1032200 | tf_op jit(solution)/shard_map/ppermute | solution.py:161
  5.2 32.0 %collective-permute-start.1 = (bf16[64,2688]{1,0:T(8,128)(2,1)S(1)}, bf16[64,2688]{1,0:T(8,128)(2,1)S(1)}, u32[]{:S(2)}, u32[]{:S(2)}) collective-permute-start(bf16[64,2688]{1,0:T(8,128)(2,1)S(1)} %pad_maximum_fusion.1), channel_id=1, source_target_pairs={{0,32},{1,33},{2,34},{3,35},{4,36},{5,37},{6,38},{7,39},{8,40},{9,... | collective-permute-start | bytes 1032200 | tf_op jit(solution)/shard_map/ppermute | solution.py:161
  8.8 28.4 %collective-permute-start.2 = (bf16[64,2688]{1,0:T(8,128)(2,1)S(1)}, bf16[64,2688]{1,0:T(8,128)(2,1)S(1)}, u32[]{:S(2)}, u32[]{:S(2)}) collective-permute-start(bf16[64,2688]{1,0:T(8,128)(2,1)S(1)} %pad_maximum_fusion.1), channel_id=1, source_target_pairs={{0,48},{1,49},{2,50},{3,51},{4,52},{5,53},{6,54},{7,55},{8,56},{9,... | collective-permute-start | bytes 1032200 | tf_op jit(solution)/shard_map/ppermute | solution.py:161
  17.1 20.0 %collective-permute-start.5 = (bf16[64,1152]{1,0:T(8,128)(2,1)S(1)}, bf16[64,1152]{1,0:T(8,128)(2,1)S(1)}, u32[]{:S(2)}, u32[]{:S(2)}) collective-permute-start(bf16[64,1152]{1,0:T(8,128)(2,1)S(1)} %pad_maximum_fusion.2), channel_id=1, source_target_pairs={{0,3},{1,0},{2,1},{3,2},{4,7},{5,4},{6,5},{7,6},{8,11},{9,8},{10,9... | collective-permute-start | bytes 442376 | tf_op jit(solution)/shard_map/ppermute | solution.py:161
  37.3 35.1 %collective-permute-start.6 = (bf16[256,2688]{1,0:T(8,128)(2,1)S(1)}, bf16[256,2688]{1,0:T(8,128)(2,1)S(1)}, u32[]{:S(2)}, u32[]{:S(2)}) collective-permute-start(bf16[256,2688]{1,0:T(8,128)(2,1)S(1)} %constant_dynamic-update-slice_fusion.refs_0_), channel_id=1, source_target_pairs={{0,4},{1,5},{2,6},{3,7},{4,8},{5,9},{6,10},{7,11},{8,12},{9,13},{1... | collective-permute-start | bytes 4128776 | tf_op jit(solution)/shard_map/ppermute | solution.py:161
  37.4 35.1 %collective-permute-start.7 = (bf16[256,2688]{1,0:T(8,128)(2,1)S(1)}, bf16[256,2688]{1,0:T(8,128)(2,1)}, u32[]{:S(2)}, u32[]{:S(2)}) collective-permute-start(bf16[256,2688]{1,0:T(8,128)(2,1)S(1)} %constant_dynamic-update-slice_fusion.refs_0_), channel_id=1, source_target_pairs={{0,8},{1,9},{2,10},{3,11},{4,12},{5,13},{6,14},{7,15},{8,0},{9,1},... | collective-permute-start | bytes 4128776 | tf_op jit(solution)/shard_map/ppermute | solution.py:161
  40.3 32.2 %collective-permute-start.8 = (bf16[256,2688]{1,0:T(8,128)(2,1)S(1)}, bf16[256,2688]{1,0:T(8,128)(2,1)}, u32[]{:S(2)}, u32[]{:S(2)}) collective-permute-start(bf16[256,2688]{1,0:T(8,128)(2,1)S(1)} %constant_dynamic-update-slice_fusion.refs_0_), channel_id=1, source_target_pairs={{0,12},{1,13},{2,14},{3,15},{4,0},{5,1},{6,2},{7,3},{8,4},{9,5},{1... | collective-permute-start | bytes 4128776 | tf_op jit(solution)/shard_map/ppermute | solution.py:161
  79.5 48.8 %collective-permute-start.12 = (bf16[16,16,2688]{2,1,0:T(8,128)(2,1)}, bf16[16,16,2688]{2,1,0:T(8,128)(2,1)S(1)}, u32[]{:S(2)}, u32[]{:S(2)}) collective-permute-start(bf16[16,16,2688]{2,1,0:T(8,128)(2,1)} %get-tuple-element.101), channel_id=1, source_target_pairs={{0,1},{1,2},{2,3},{3,0},{4,5},{5,6},{6,7},{7,4},{8,9},{9,10},{10,1... | collective-permute-start | bytes 4128776 | tf_op jit(solution)/shard_map/ppermute | solution.py:161
  79.5 48.8 %collective-permute-start.13 = (bf16[16,16,2688]{2,1,0:T(8,128)(2,1)}, bf16[16,16,2688]{2,1,0:T(8,128)(2,1)}, u32[]{:S(2)}, u32[]{:S(2)}) collective-permute-start(bf16[16,16,2688]{2,1,0:T(8,128)(2,1)} %get-tuple-element.102), channel_id=1, source_target_pairs={{0,2},{1,3},{2,0},{3,1},{4,6},{5,7},{6,4},{7,5},{8,10},{9,11},{10,... | collective-permute-start | bytes 4128776 | tf_op jit(solution)/shard_map/ppermute | solution.py:161
  96.4 31.9 %collective-permute-start.14 = (bf16[16,16,2688]{2,1,0:T(8,128)(2,1)}, bf16[16,16,2688]{2,1,0:T(8,128)(2,1)}, u32[]{:S(2)}, u32[]{:S(2)}) collective-permute-start(bf16[16,16,2688]{2,1,0:T(8,128)(2,1)} %get-tuple-element.103), channel_id=1, source_target_pairs={{0,3},{1,0},{2,1},{3,2},{4,7},{5,4},{6,5},{7,6},{8,11},{9,8},{10,9... | collective-permute-start | bytes 4128776 | tf_op jit(solution)/shard_map/ppermute | solution.py:161
  129.1 35.2 %collective-permute-start.18 = (bf16[3584,512]{1,0:T(8,128)(2,1)}, bf16[3584,512]{1,0:T(8,128)(2,1)}, u32[]{:S(2)}, u32[]{:S(2)}) collective-permute-start(bf16[3584,512]{1,0:T(8,128)(2,1)} %bitcast.33), channel_id=1, source_target_pairs={{0,64},{64,0},{1,65},{65,1},{2,66},{66,2},{3,67},{67,3},{4,68},{68... | collective-permute-start | bytes 11010056 | tf_op jit(solution)/shard_map/ppermute | solution.py:475
  129.1 35.2 %collective-permute-start.19 = (bf16[3584,512]{1,0:T(8,128)(2,1)}, bf16[3584,512]{1,0:T(8,128)(2,1)}, u32[]{:S(2)}, u32[]{:S(2)}) collective-permute-start(bf16[3584,512]{1,0:T(8,128)(2,1)} %bitcast.35), channel_id=1, source_target_pairs={{0,64},{64,0},{1,65},{65,1},{2,66},{66,2},{3,67},{67,3},{4,68},{68... | collective-permute-start | bytes 11010056 | tf_op jit(solution)/shard_map/ppermute | solution.py:475
  129.6 34.7 %collective-permute-start.20 = (bf16[512,3584]{1,0:T(8,128)(2,1)}, bf16[512,3584]{1,0:T(8,128)(2,1)}, u32[]{:S(2)}, u32[]{:S(2)}) collective-permute-start(bf16[512,3584]{1,0:T(8,128)(2,1)} %bitcast.37), channel_id=1, source_target_pairs={{0,64},{64,0},{1,65},{65,1},{2,66},{66,2},{3,67},{67,3},{4,68},{68... | collective-permute-start | bytes 11010056 | tf_op jit(solution)/shard_map/ppermute | solution.py:475
  129.6 71.2 %all-to-all-start = ((bf16[64,32,1152]{2,1,0:T(8,128)(2,1)}), bf16[64,32,1152]{2,1,0:T(8,128)(2,1)}, u32[]{:S(2)}, u32[]{:S(2)}) async-start(bf16[64,32,1152]{2,1,0:T(8,128)(2,1)} %copy-done), calls=%async_computation | async-start | bytes 9437184 | tf_op jit(solution)/shard_map/all_to_all | solution.py:473
  188.7 50.0 %collective-permute-start.21 = (bf16[16,16,2560]{2,1,0:T(8,128)(2,1)}, bf16[16,16,2560]{2,1,0:T(8,128)(2,1)S(1)}, u32[]{:S(2)}, u32[]{:S(2)}) collective-permute-start(bf16[16,16,2560]{2,1,0:T(8,128)(2,1)} %get-tuple-element.127), channel_id=1, source_target_pairs={{0,3},{1,0},{2,1},{3,2},{4,7},{5,4},{6,5},{7,6},{8,11},{9,8},{10,9... | collective-permute-start | bytes 3932168 | tf_op jit(solution)/shard_map/ppermute | solution.py:161
  191.4 47.3 %collective-permute-start.22 = (bf16[16,16,2560]{2,1,0:T(8,128)(2,1)}, bf16[16,16,2560]{2,1,0:T(8,128)(2,1)S(1)}, u32[]{:S(2)}, u32[]{:S(2)}) collective-permute-start(bf16[16,16,2560]{2,1,0:T(8,128)(2,1)} %get-tuple-element.128), channel_id=1, source_target_pairs={{0,2},{1,3},{2,0},{3,1},{4,6},{5,7},{6,4},{7,5},{8,10},{9,11},{10,... | collective-permute-start | bytes 3932168 | tf_op jit(solution)/shard_map/ppermute | solution.py:161
  192.2 46.5 %collective-permute-start.23 = (bf16[16,16,2560]{2,1,0:T(8,128)(2,1)}, bf16[16,16,2560]{2,1,0:T(8,128)(2,1)}, u32[]{:S(2)}, u32[]{:S(2)}) collective-permute-start(bf16[16,16,2560]{2,1,0:T(8,128)(2,1)} %get-tuple-element.129), channel_id=1, source_target_pairs={{0,1},{1,2},{2,3},{3,0},{4,5},{5,6},{6,7},{7,4},{8,9},{9,10},{10,1... | collective-permute-start | bytes 3932168 | tf_op jit(solution)/shard_map/ppermute | solution.py:161
  193.1 25.9 %collective-permute-start.24 = (bf16[16,16,1024]{2,1,0:T(8,128)(2,1)}, bf16[16,16,1024]{2,1,0:T(8,128)(2,1)}, u32[]{:S(2)}, u32[]{:S(2)}) collective-permute-start(bf16[16,16,1024]{2,1,0:T(8,128)(2,1)} %get-tuple-element.130), channel_id=1, source_target_pairs={{0,12},{1,13},{2,14},{3,15},{4,0},{5,1},{6,2},{7,3},{8,4},{9,5},{1... | collective-permute-start | bytes 1572872 | tf_op jit(solution)/shard_map/ppermute | solution.py:161
  202.1 36.6 %collective-permute-start.25 = (bf16[16,16,1024]{2,1,0:T(8,128)(2,1)}, bf16[16,16,1024]{2,1,0:T(8,128)(2,1)}, u32[]{:S(2)}, u32[]{:S(2)}) collective-permute-start(bf16[16,16,1024]{2,1,0:T(8,128)(2,1)} %copy-done.9), channel_id=1, source_target_pairs={{0,8},{1,9},{2,10},{3,11},{4,12},{5,13},{6,14},{7,15},{8,0},{9,1},... | collective-permute-start | bytes 1572872 | tf_op jit(solution)/shard_map/ppermute | solution.py:161
  242.3 52.9 %collective-permute-start.27 = (bf16[256,2560]{1,0:T(8,128)(2,1)S(1)}, bf16[256,2560]{1,0:T(8,128)(2,1)S(1)}, u32[]{:S(2)}, u32[]{:S(2)}) collective-permute-start(bf16[256,2560]{1,0:T(8,128)(2,1)S(1)} %get-tuple-element.137), channel_id=1, source_target_pairs={{0,12},{1,13},{2,14},{3,15},{4,0},{5,1},{6,2},{7,3},{8,4},{9,5},{1... | collective-permute-start | bytes 3932168 | tf_op jit(solution)/shard_map/ppermute | solution.py:161
  244.4 50.8 %collective-permute-start.28 = (bf16[256,2560]{1,0:T(8,128)(2,1)S(1)}, bf16[256,2560]{1,0:T(8,128)(2,1)S(1)}, u32[]{:S(2)}, u32[]{:S(2)}) collective-permute-start(bf16[256,2560]{1,0:T(8,128)(2,1)S(1)} %get-tuple-element.138), channel_id=1, source_target_pairs={{0,8},{1,9},{2,10},{3,11},{4,12},{5,13},{6,14},{7,15},{8,0},{9,1},... | collective-permute-start | bytes 3932168 | tf_op jit(solution)/shard_map/ppermute | solution.py:161
  244.4 50.8 %collective-permute-start.29 = (bf16[256,2560]{1,0:T(8,128)(2,1)S(1)}, bf16[256,2560]{1,0:T(8,128)(2,1)S(1)}, u32[]{:S(2)}, u32[]{:S(2)}) collective-permute-start(bf16[256,2560]{1,0:T(8,128)(2,1)S(1)} %get-tuple-element.139), channel_id=1, source_target_pairs={{0,4},{1,5},{2,6},{3,7},{4,8},{5,9},{6,10},{7,11},{8,12},{9,13},{1... | collective-permute-start | bytes 3932168 | tf_op jit(solution)/shard_map/ppermute | solution.py:161
  252.4 42.8 %collective-permute-start.31 = (bf16[256,1024]{1,0:T(8,128)(2,1)S(1)}, bf16[256,1024]{1,0:T(8,128)(2,1)S(1)}, u32[]{:S(2)}, u32[]{:S(2)}) collective-permute-start(bf16[256,1024]{1,0:T(8,128)(2,1)S(1)} %get-tuple-element.146), channel_id=1, source_target_pairs={{0,32},{1,33},{2,34},{3,35},{4,36},{5,37},{6,38},{7,39},{8,40},{9,... | collective-permute-start | bytes 1572872 | tf_op jit(solution)/shard_map/ppermute | solution.py:161
  265.0 30.2 %collective-permute-start.32 = (bf16[256,1024]{1,0:T(8,128)(2,1)S(1)}, bf16[256,1024]{1,0:T(8,128)(2,1)S(1)}, u32[]{:S(2)}, u32[]{:S(2)}) collective-permute-start(bf16[256,1024]{1,0:T(8,128)(2,1)S(1)} %get-tuple-element.147), channel_id=1, source_target_pairs={{0,16},{1,17},{2,18},{3,19},{4,20},{5,21},{6,22},{7,23},{8,24},{9,... | collective-permute-start | bytes 1572872 | tf_op jit(solution)/shard_map/ppermute | solution.py:161
  (35 other events, 375.6 us)

commit v3 on v2

--- a/solution.py
+++ b/solution.py
@@ -12,13 +12,14 @@
 STEPS = 2
 CTX = 64
 KVW = 576
+LIVE = CTX - STEPS
 HALF = CTX // 2
 GROUP = 16
 TOGETHER = 8
 WIDE = 640
 SIDE = 4
 Z, Y, X = SIDE * SIDE, SIDE, 1
-MAIN = 2560
+MAIN = 2432
 MINOR = D - MAIN
 MARK = 128
 SLOTS = 32
@@ -30,53 +31,55 @@
 CHIPS = SIDE**3
 BLOCK = 32
 ORDERS = (((Z, Y, X), (Y, X, Z)), ((X, Z, Y), (X, Z, Y)))
-SOURCES = (0, -1, 2, 1)
-TARGETS = (0, 1, 2, -1)
-KEYS = GROUP * (CTX + STEPS)
+TARGETS = (0, 1, -1, 2)
+KEYS = GROUP * CTX
 
 
 score_scale = 192.0 ** (-0.5)
-
-
-def attend_kernel(landing_ref, got_ref, len_ref, new_ref, query_ref, out_ref, even_ref, odd_ref, value_ref, bias_ref):
+base_two_scale = score_scale * 1.4426950408889634
+
+
+def attend_kernel(
+    landing_ref, got_ref, len_ref, new_ref, query_ref, out_ref,
+    even_ref, odd_ref, value_ref, bias_ref, recent_ref,
+):
     pairs = GROUP * HALF
-
-    def lanes(rows):
-        return lax.broadcasted_iota(jnp.int32, (rows, WIDE), 1)
-
-    def place(keys, rows, at):
-        even_ref[pl.ds(at, rows), :] = keys.astype(jnp.bfloat16)
-        odd_ref[pl.ds(at, rows), :] = pltpu.roll(keys, WIDE - KVW, 1).astype(jnp.bfloat16)
-        value_ref[pl.ds(at, rows), :] = keys[:, :LAT].astype(jnp.bfloat16)
-
-    def one(slot, carry):
-        source = landing_ref[slot]
-        block = got_ref[source]
-        first = jnp.where(lanes(HALF) < KVW, block[:, :WIDE].astype(jnp.float32), 0.0)
-        at = pl.multiple_of(slot * HALF, HALF)
-        place(first, HALF, at)
-        second = block[:, LAT:].astype(jnp.float32)
-        second = jnp.where(lanes(HALF) < WIDE - KVW, 0.0, second)
-        place(pltpu.roll(second, KVW, 1), HALF, pl.multiple_of(pairs + at, HALF))
-        return carry
-
-    lax.fori_loop(0, GROUP, one, 0)
+    lane = lax.broadcasted_iota(jnp.int32, (HALF, WIDE), 1)
+    last = lax.broadcasted_iota(jnp.int32, (HALF, WIDE), 0) == HALF - 1
     for step in range(STEPS):
         rows = new_ref[step].astype(jnp.float32)
-        rows = jnp.concatenate([rows, jnp.zeros((GROUP, WIDE - KVW), jnp.float32)], axis=1)
-        place(rows, GROUP, 2 * pairs + step * GROUP)
+        recent_ref[step] = jnp.concatenate(
+            [rows, jnp.zeros((GROUP, WIDE - KVW), jnp.float32)], axis=1
+        )
+
+    def place(keys, at):
+        even_ref[pl.ds(at, HALF), :] = keys.astype(jnp.bfloat16)
+        odd_ref[pl.ds(at, HALF), :] = pltpu.roll(keys, WIDE - KVW, 1).astype(jnp.bfloat16)
+        value_ref[pl.ds(at, HALF), :] = keys[:, :LAT].astype(jnp.bfloat16)
+
+    def one(slot, carry):
+        block = got_ref[landing_ref[slot]]
+        first = jnp.where(lane < KVW, block[:, :WIDE].astype(jnp.float32), 0.0)
+        first = jnp.where(last, recent_ref[0, pl.ds(slot, 1), :], first)
+        at = pl.multiple_of(slot * HALF, HALF)
+        place(first, at)
+        second = block[:, LAT:].astype(jnp.float32)
+        second = pltpu.roll(jnp.where(lane < WIDE - KVW, 0.0, second), KVW, 1)
+        second = jnp.where(last, recent_ref[1, pl.ds(slot, 1), :], second)
+        place(second, pl.multiple_of(pairs + at, HALF))
+        return carry
+
+    lax.fori_loop(0, GROUP, one, 0)
 
     column = lax.broadcasted_iota(jnp.int32, (GROUP, KEYS), 1)
     row = lax.broadcasted_iota(jnp.int32, (GROUP, KEYS), 0)
-    cached = column < 2 * pairs
     half = (column >= pairs).astype(jnp.int32)
     within = column - half * pairs
     position = 2 * (within % HALF) + half
-    recent = column - 2 * pairs
-    owner = jnp.where(cached, within // HALF, recent % GROUP)
-    live = cached & (position < len_ref[...])
+    cached = position < len_ref[...]
     for step in range(STEPS):
-        allowed = (live | (~cached & (recent < (step + 1) * GROUP))) & (owner == row)
+        recent = (position >= LIVE) & (position <= LIVE + step)
+        allowed = (cached | recent) & (within // HALF == row)
         bias_ref[pl.ds(step * GROUP, GROUP), :] = jnp.where(allowed, 0.0, -jnp.inf)
 
     def heads(index, carry):
@@ -94,12 +97,13 @@
                 (((1,), (1,)), ((), ())),
                 preferred_element_type=jnp.float32,
             )
-            score = score * score_scale + bias
-            weight = jnp.exp(score - jnp.max(score, axis=1, keepdims=True))
-            prob = weight * (1.0 / jnp.sum(weight, axis=1, keepdims=True))
+            score = score + bias
+            weight = jnp.exp2((score - jnp.max(score, axis=1, keepdims=True)) * base_two_scale)
+            total = jnp.sum(weight, axis=1, keepdims=True)
             mixed = jnp.dot(
-                prob.astype(jnp.bfloat16), value_ref[...], preferred_element_type=jnp.float32
-            ).astype(jnp.bfloat16)
+                weight.astype(jnp.bfloat16), value_ref[...], preferred_element_type=jnp.float32
+            )
+            mixed = (mixed * (1.0 / total)).astype(jnp.bfloat16)
             for k in range(TOGETHER):
                 start = pl.multiple_of(((index * TOGETHER + k) * 2 + odd) * LAT, LAT)
                 for step in range(STEPS):
@@ -140,6 +144,7 @@
             pltpu.VMEM((KEYS, WIDE), jnp.bfloat16),
             pltpu.VMEM((KEYS, LAT), jnp.bfloat16),
             pltpu.VMEM((STEPS * GROUP, KEYS), jnp.float32),
+            pltpu.VMEM((STEPS, GROUP, WIDE), jnp.float32),
         ],
         input_output_aliases={} if earlier is None else {5: 0},
         compiler_params=pltpu.CompilerParams(vmem_limit_bytes=32 * 2**20),
@@ -257,15 +262,13 @@
 def send_rows(columns, targets, packed_cache):
     first, second, third = stage_axes()
     both = range(len(columns))
-    rings = [exchange([columns[i]] * 3, first[i], TARGETS[1:]) for i in both]
+    rings = [exchange([columns[i]] * 3, first[i], (1, -1, 2)) for i in both]
     columns, rings = together(columns, rings)
     lines = [jnp.concatenate([columns[i]] + rings[i], axis=0) for i in both]
-    rings = [exchange([lines[i]] * 3, second[i], TARGETS[1:]) for i in both]
+    rings = [exchange([lines[i]] * 3, second[i], (1, -1, 2)) for i in both]
     packed_cache, rings[1][0] = together(packed_cache, rings[1][0])
     lines, rings = together(lines, rings)
-    picked = [list(select(targets[0], [lines[0]] + rings[0]))]
-    lines[1], picked[0][SIDE] = together(lines[1], picked[0][SIDE])
-    picked.append(select(targets[1], [lines[1]] + rings[1]))
+    picked = [select(targets[i], [lines[i]] + rings[i]) for i in both]
     rings = [exchange(picked[i][1:SIDE], third[i], TARGETS[1:]) for i in both]
     return [[picked[i][0]] + rings[i] for i in both], [p[SIDE] for p in picked], packed_cache
 
@@ -273,18 +276,18 @@
 def return_rows(outward, targets, ids, contexts):
     first, second, third = stage_axes()
     both = range(len(outward))
-    rings = [exchange(outward[i][1:], third[i], SOURCES[1:]) for i in both]
+    rings = [exchange(outward[i][1:], third[i], (-1, 1, 2)) for i in both]
     context = contexts(None)
     rings, context = together(rings, context)
     lines = [combine(targets[i], ids[i], [outward[i][0]] + rings[i]) for i in both]
-    rings = [exchange(lines[i][1:], second[i], SOURCES[1:]) for i in both]
+    rings = [exchange(lines[i][1:], second[i], (-1, 1, 2)) for i in both]
     context = contexts(context)
     rings, context = together(rings, context)
     sums = []
     for i in both:
         line = add(lines[i][0], *rings[i])
         blocks = [line[k * ROWS : (k + 1) * ROWS] for k in range(SIDE)]
-        sums.append([blocks[0]] + exchange(blocks[1:], first[i], SOURCES[1:]))
+        sums.append([blocks[0]] + exchange(blocks[1:], first[i], (-1, 1, 2)))
     sums, = together(sums)
     return [add(*terms) for terms in sums], context
 
@@ -486,6 +489,7 @@
     order = jnp.where(core == 0, tables[0], tables[1])
     rows, part, weight = first_half(order, me, arrived[0], arrived[1], own)
     outward = second_half(order, rows, part, weight, other)
+    outward, got = lax.optimization_barrier((outward, got))
     got_mark = lax.optimization_barrier(got[:, HALF - 1, :128]).astype(jnp.int32)
     got_slot, got_len = got_mark[:, 0], got_mark[:, 1]
     land_hit = got_slot[None, :] == slot_range[:, None]

time: 316 us -> 276 us (0.87)
  the two profiles are of different devices: /device:TPU:24 before, /device:TPU:10 now
where the time goes in v3:
time: 276 us; the launch traced here: 273 us
  waiting for transfers between devices  92.9 us (34%)
  Pallas kernels  91.4 us (33%)
  starting transfers between devices  65.3 us (24%)
  local copies, waits for them, and re-layouts  19 us (7%)
  other arithmetic  3.84 us (1%)
    ppermute x36, waiting for transfers between devices, hop(): return lax.ppermute(value, ('dp', 'ep'), pairs)  79.3 us
    ppermute x36, starting transfers between devices, hop(): return lax.ppermute(value, ('dp', 'ep'), pairs)  55.4 us
    pallas_call x2, Pallas kernels, attend(): pl.pallas_call(kernel, grid=(1,), out_shape=jax.ShapeDtypeStruct((STEPS,...  28.9 us
    pallas_call x1, Pallas kernels, first_half(): pl.pallas_call(first_half_kernel, out_shape=[whole, whole, jax.ShapeDtype...  23.9 us
    pallas_call x1, Pallas kernels, second_half(): pl.pallas_call(second_half_kernel, out_shape=[jax.ShapeDtypeStruct(shape,...  23.6 us
    unnamed x42, local copies, waits for them, and re-layouts  14.8 us
    all_to_all x1, waiting for transfers between devices, on_device(): lax.all_to_all(packed_cache, 'ep', split_axis=0, concat_axis=0, tiled=True)  13.6 us
    all_to_all x1, starting transfers between devices, on_device(): lax.all_to_all(packed_cache, 'ep', split_axis=0, concat_axis=0, tiled=True)  9.4 us
  transfers between devices with their start and end apart: 40, of which 15 were waited for; matrix products, arithmetic and copies ran while one was open for 3% of the time, Pallas kernels for 31%

profile of v3, /device:TPU:10, one launch (start us, length us, event | category | flops | bytes accessed | tf_op | source)
XLA Modules:
  0.0 273.4 jit_solution(5100885164065500413)
XLA Ops:
  14.3 3.0 %collective-permute-done.4 = bf16[64,1280]{1,0:T(8,128)(2,1)S(1)} collective-permute-done((bf16[64,1280]{1,0:T(8,128)(2,1)S(1)}, bf16[64,1280]{1,0:T(8,128)(2,1)S(1)}, u32[]{:S(2)}, u32[]{:S(2)}) %collective-permute-start.4) | collective-permute-done | bytes 163872 | tf_op jit(solution)/shard_map/ppermute | solution.py:166
  30.5 8.0 %collective-permute-done.9.refs_1_ = bf16[256,1280]{1,0:T(8,128)(2,1)S(1)} collective-permute-done((bf16[256,1280]{1,0:T(8,128)(2,1)S(1)}, bf16[256,1280]{1,0:T(8,128)(2,1)S(1)}, u32[]{:S(2)}, u32[]{:S(2)}) %collective-permute-start.9) | collective-permute-done | bytes 655392 | tf_op jit(solution)/shard_map/ppermute | solution.py:166
  45.9 10.9 %collective-permute-done.10.refs_2_ = bf16[256,1280]{1,0:T(8,128)(2,1)} collective-permute-done((bf16[256,1280]{1,0:T(8,128)(2,1)S(1)}, bf16[256,1280]{1,0:T(8,128)(2,1)}, u32[]{:S(2)}, u32[]{:S(2)}) %collective-permute-start.10) | collective-permute-done | bytes 655392 | tf_op jit(solution)/shard_map/ppermute | solution.py:166
  61.4 4.6 %shard_map.141 = (bf16[16,16,2560]{2,1,0:T(8,128)(2,1)S(1)}, bf16[16,16,2560]{2,1,0:T(8,128)(2,1)S(1)}, bf16[16,16,2560]{2,1,0:T(8,128)(2,1)S(1)}, bf16[16,16,2560]{2,1,0:T(8,128)(2,1)S(1)}, f32[4,8,256]{2,1,0:T(8,128)S(1)}) custom-call(s32[4]{0:T(128)S(1)} %pad_add_fusion.targets_ref, bf16[256,2560]{1,0:T(8,128)(2,1)} %constant_dynamic-update-slice_fusion.refs_0_, ...), custom_call_target="tpu_custom_call" | custom-call | flops 1342177280 | bytes 10485760 | tf_op jit(solution)/shard_map/pallas_call | solution.py:210
  76.3 11.5 %collective-permute-done.16.refs_6_ = bf16[16,16,1280]{2,1,0:T(8,128)(2,1)S(1)} collective-permute-done((bf16[16,16,1280]{2,1,0:T(8,128)(2,1)S(1)}, bf16[16,16,1280]{2,1,0:T(8,128)(2,1)S(1)}, u32[]{:S(2)}, u32[]{:S(2)}) %collective-permute-start.16) | collective-permute-done | bytes 655392 | tf_op jit(solution)/shard_map/ppermute | solution.py:166
  87.8 13.3 %collective-permute-done.17.refs_7_ = bf16[16,16,1280]{2,1,0:T(8,128)(2,1)S(1)} collective-permute-done((bf16[16,16,1280]{2,1,0:T(8,128)(2,1)S(1)}, bf16[16,16,1280]{2,1,0:T(8,128)(2,1)S(1)}, u32[]{:S(2)}, u32[]{:S(2)}) %collective-permute-start.17) | collective-permute-done | bytes 655392 | tf_op jit(solution)/shard_map/ppermute | solution.py:166
  103.5 9.4 %all-to-all-start = ((bf16[64,32,1152]{2,1,0:T(8,128)(2,1)}), bf16[64,32,1152]{2,1,0:T(8,128)(2,1)}, u32[]{:S(2)}, u32[]{:S(2)}) async-start(bf16[64,32,1152]{2,1,0:T(8,128)(2,1)} %copy-done), calls=%async_computation | async-start | bytes 9437184 | tf_op jit(solution)/shard_map/all_to_all | solution.py:476
  113.0 23.9 %shard_map.143 = (bf16[64,16,3584]{2,1,0:T(8,128)(2,1)}, bf16[64,16,3584]{2,1,0:T(8,128)(2,1)}, f32[64,16,128]{2,1,0:T(8,128)S(1)}) custom-call(s32[64]{0:T(128)S(1)} %broadcast_select_fusion.order_ref, s32[1]{0:T(128)} %bitcast.8.me_ref, bf16[16,16,2560]{2,1,0:T(8,128)(2,1)} %copy-done.7, bf16[16,16,2560]{2,1,0:T(8,128)(2,1)} %copy-done.12, ...), custom_call_target="tpu_custom_call" | custom-call | flops 11274289152 | bytes 33030144 | tf_op jit(solution)/shard_map/pallas_call | solution.py:372
  136.9 23.6 %shard_map.144 = (bf16[16,16,2432]{2,1,0:T(8,128)(2,1)}, bf16[16,16,2432]{2,1,0:T(8,128)(2,1)}, bf16[16,16,2432]{2,1,0:T(8,128)(2,1)}, bf16[16,16,2432]{2,1,0:T(...) custom-call(s32[64]{0:T(128)S(1)} %broadcast_select_fusion.order_ref, ...), custom_call_target="tpu_custom_call" | custom-call | flops 11274289152 | bytes 33030144 | tf_op jit(solution)/shard_map/pallas_call | solution.py:385
  160.5 13.6 %all-to-all-done.got_ref.refs_1_ = bf16[64,32,1152]{2,1,0:T(8,128)(2,1)} async-done(((bf16[64,32,1152]{2,1,0:T(8,128)(2,1)}), bf16[64,32,1152]{2,1,0:T(8,128)(2,1)}, u32[]{:S(2)}, u32[]{:S(2)}) %all-to-all-start) | async-done | bytes 4718624 | tf_op jit(solution)/shard_map/all_to_all | solution.py:476
  174.4 3.5 %collective-permute-start.22 = (bf16[16,16,2432]{2,1,0:T(8,128)(2,1)}, bf16[16,16,2432]{2,1,0:T(8,128)(2,1)S(1)}, u32[]{:S(2)}, u32[]{:S(2)}) collective-permute-start(bf16[16,16,2432]{2,1,0:T(8,128)(2,1)} %get-tuple-element.142), channel_id=1, source_target_pairs={{0,1},{1,2},{2,3},{3,0},{4,5},{5,6},{6,7},{7,4},{8,9},{9,10},{10,1... | collective-permute-start | bytes 3735560 | tf_op jit(solution)/shard_map/ppermute | solution.py:166
  182.3 5.2 %collective-permute-done.24.refs_1_ = bf16[16,16,1152]{2,1,0:T(8,128)(2,1)} collective-permute-done((bf16[16,16,1152]{2,1,0:T(8,128)(2,1)}, bf16[16,16,1152]{2,1,0:T(8,128)(2,1)}, u32[]{:S(2)}, u32[]{:S(2)}) %collective-permute-start.24) | collective-permute-done | bytes 589856 | tf_op jit(solution)/shard_map/ppermute | solution.py:166
  191.4 14.5 %shard_map.145.refs_5_ = bf16[2,32,32768]{2,1,0:T(8,128)(2,1)} custom-call(s32[16]{0:T(128)S(1)} %get-tuple-element.201.landing_ref, bf16[64,32,1152]{2,1,0:T(8,128)(2,1)} %all-to-all-done.got_ref.refs_1_, s32[32,1]{1,0:T(8,128)S(1)} %copy.23.len_ref.refs_2_, bf16[2,32,576]{2,1,0:T(8,128)(2,1)S(1)} %copy-done.6, bf16[2,32,36864]{2,1,0:T(8,128)(2,1)S(1)} %copy-done.1), custom_call_target="tpu_custom_call" | custom-call | flops 4831838208 | bytes 4456448 | tf_op jit(solution)/shard_map/pallas_call | solution.py:136
  207.8 3.6 %shard_map.146 = (bf16[256,2432]{1,0:T(8,128)(2,1)S(1)}, bf16[256,2432]{1,0:T(8,128)(2,1)S(1)}, bf16[256,2432]{1,0:T(8,128)(2,1)S(1)}, bf16[256,2432]{1,0:T(8,128)(2,1)S(1)}) custom-call(s32[4]{0:T(128)S(1)} %pad_add_fusion.targets_ref, f32[4,8,256]{2,1,0:T(8,128)S(1)} %get-tuple-element.104.ids_ref, bf16[16,16,2432]{2,1,0:T(8,128)(2,1)S(1)} %copy-done.3, ...), custom_call_target="tpu_custom_call" | custom-call | flops 1275068416 | bytes 9961472 | tf_op jit(solution)/shard_map/pallas_call | solution.py:238
  214.9 2.8 %shard_map.147 = (bf16[256,1152]{1,0:T(8,128)(2,1)S(1)}, bf16[256,1152]{1,0:T(8,128)(2,1)S(1)}, bf16[256,1152]{1,0:T(8,128)(2,1)S(1)}, bf16[256,1152]{1,0:T(8,128)(2,1)S(1)}) custom-call(s32[4]{0:T(128)S(1)} %pad_add_fusion.1.targets_ref, f32[4,8,256]{2,1,0:T(8,128)S(1)} %get-tuple-element.154.ids_ref, bf16[16,16,1152]{2,1,0:T(8,128)(2,1)S(1)} %get-tuple-element.155.refs_0_, ...), custom_call_target="tpu_custom_call" | custom-call | flops 603979776 | bytes 4718592 | tf_op jit(solution)/shard_map/pallas_call | solution.py:238
  217.7 3.0 %collective-permute-start.30 = (bf16[256,1152]{1,0:T(8,128)(2,1)S(1)}, bf16[256,1152]{1,0:T(8,128)(2,1)S(1)}, u32[]{:S(2)}, u32[]{:S(2)}) collective-permute-start(bf16[256,1152]{1,0:T(8,128)(2,1)S(1)} %get-tuple-element.159), channel_id=1, source_target_pairs={{0,48},{1,49},{2,50},{3,51},{4,52},{5,53},{6,54},{7,55},{8,56},{9,... | collective-permute-start | bytes 1769480 | tf_op jit(solution)/shard_map/ppermute | solution.py:166
  220.7 11.8 %collective-permute-done.30 = bf16[256,1152]{1,0:T(8,128)(2,1)S(1)} collective-permute-done((bf16[256,1152]{1,0:T(8,128)(2,1)S(1)}, bf16[256,1152]{1,0:T(8,128)(2,1)S(1)}, u32[]{:S(2)}, u32[]{:S(2)}) %collective-permute-start.30) | collective-permute-done | bytes 589856 | tf_op jit(solution)/shard_map/ppermute | solution.py:166
  232.5 3.0 %collective-permute-start.32 = (bf16[256,1152]{1,0:T(8,128)(2,1)S(1)}, bf16[256,1152]{1,0:T(8,128)(2,1)S(1)}, u32[]{:S(2)}, u32[]{:S(2)}) collective-permute-start(bf16[256,1152]{1,0:T(8,128)(2,1)S(1)} %get-tuple-element.161), channel_id=1, source_target_pairs={{0,32},{1,33},{2,34},{3,35},{4,36},{5,37},{6,38},{7,39},{8,40},{9,... | collective-permute-start | bytes 1769480 | tf_op jit(solution)/shard_map/ppermute | solution.py:166
  237.8 14.4 %shard_map.148 = bf16[2,32,32768]{2,1,0:T(8,128)(2,1)} custom-call(s32[16]{0:T(128)S(1)} %get-tuple-element.200.refs_0_, bf16[64,32,1152]{2,1,0:T(8,128)(2,1)} %all-to-all-done.got_ref.refs_1_, s32[32,1]{1,0:T(8,128)S(1)} %copy.23.len_ref.refs_2_, bf16[2,32,576]{2,1,0:T(8,128)(2,1)S(1)} %copy-done.6, ...), custom_call_target="tpu_custom_call", output_to_operand_aliasing={{}: (5, {})} | custom-call | flops 4831838208 | bytes 4456448 | tf_op jit(solution)/shard_map/pallas_call | solution.py:136
  256.2 3.0 %collective-permute-start.36 = (bf16[64,1152]{1,0:T(8,128)(2,1)S(1)}, bf16[64,1152]{1,0:T(8,128)(2,1)S(1)}, u32[]{:S(2)}, u32[]{:S(2)}) collective-permute-start(bf16[64,1152]{1,0:T(8,128)(2,1)S(1)} %get-tuple-element.193), channel_id=1, source_target_pairs={{0,3},{1,0},{2,1},{3,2},{4,7},{5,4},{6,5},{7,6},{8,11},{9,8},{10,9... | collective-permute-start | bytes 442376 | tf_op jit(solution)/shard_map/ppermute | solution.py:166
  259.3 3.1 %collective-permute-start.37 = (bf16[64,1152]{1,0:T(8,128)(2,1)S(1)}, bf16[64,1152]{1,0:T(8,128)(2,1)S(1)}, u32[]{:S(2)}, u32[]{:S(2)}) collective-permute-start(bf16[64,1152]{1,0:T(8,128)(2,1)S(1)} %get-tuple-element.192), channel_id=1, source_target_pairs={{0,1},{1,2},{2,3},{3,0},{4,5},{5,6},{6,7},{7,4},{8,9},{9,10},{10,1... | collective-permute-start | bytes 442376 | tf_op jit(solution)/shard_map/ppermute | solution.py:166
  262.4 3.4 %collective-permute-done.36 = bf16[64,1152]{1,0:T(8,128)(2,1)S(1)} collective-permute-done((bf16[64,1152]{1,0:T(8,128)(2,1)S(1)}, bf16[64,1152]{1,0:T(8,128)(2,1)S(1)}, u32[]{:S(2)}, u32[]{:S(2)}) %collective-permute-start.36) | collective-permute-done | bytes 147488 | tf_op jit(solution)/shard_map/ppermute | solution.py:166
  265.7 3.5 %collective-permute-start.38 = (bf16[64,1152]{1,0:T(8,128)(2,1)S(1)}, bf16[64,1152]{1,0:T(8,128)(2,1)S(1)}, u32[]{:S(2)}, u32[]{:S(2)}) collective-permute-start(bf16[64,1152]{1,0:T(8,128)(2,1)S(1)} %get-tuple-element.191), channel_id=1, source_target_pairs={{0,2},{1,3},{2,0},{3,1},{4,6},{5,7},{6,4},{7,5},{8,10},{9,11},{10,... | collective-permute-start | bytes 442376 | tf_op jit(solution)/shard_map/ppermute | solution.py:166
  269.2 3.1 %collective-permute-done.38 = bf16[64,1152]{1,0:T(8,128)(2,1)S(1)} collective-permute-done((bf16[64,1152]{1,0:T(8,128)(2,1)S(1)}, bf16[64,1152]{1,0:T(8,128)(2,1)S(1)}, u32[]{:S(2)}, u32[]{:S(2)}) %collective-permute-start.38) | collective-permute-done | bytes 147488 | tf_op jit(solution)/shard_map/ppermute | solution.py:166
  (137 shorter events, 72.7 us)
Async XLA Ops:
  24.4 32.4 %collective-permute-start.6 = (bf16[256,2560]{1,0:T(8,128)(2,1)}, bf16[256,2560]{1,0:T(8,128)(2,1)}, u32[]{:S(2)}, u32[]{:S(2)}) collective-permute-start(bf16[256,2560]{1,0:T(8,128)(2,1)} %constant_dynamic-update-slice_fusion.refs_0_), channel_id=1, source_target_pairs={{0,4},{1,5},{2,6},{3,7},{4,8},{5,9},{6,10},{7,11},{8,12},{9,13},{1... | collective-permute-start | bytes 3932168 | tf_op jit(solution)/shard_map/ppermute | solution.py:166
  26.0 30.8 %collective-permute-start.7 = (bf16[256,2560]{1,0:T(8,128)(2,1)}, bf16[256,2560]{1,0:T(8,128)(2,1)}, u32[]{:S(2)}, u32[]{:S(2)}) collective-permute-start(bf16[256,2560]{1,0:T(8,128)(2,1)} %constant_dynamic-update-slice_fusion.refs_0_), channel_id=1, source_target_pairs={{0,12},{1,13},{2,14},{3,15},{4,0},{5,1},{6,2},{7,3},{8,4},{9,5},{1... | collective-permute-start | bytes 3932168 | tf_op jit(solution)/shard_map/ppermute | solution.py:166
  26.4 32.2 %collective-permute-start.8 = (bf16[256,2560]{1,0:T(8,128)(2,1)}, bf16[256,2560]{1,0:T(8,128)(2,1)}, u32[]{:S(2)}, u32[]{:S(2)}) collective-permute-start(bf16[256,2560]{1,0:T(8,128)(2,1)} %constant_dynamic-update-slice_fusion.refs_0_), channel_id=1, source_target_pairs={{0,8},{1,9},{2,10},{3,11},{4,12},{5,13},{6,14},{7,15},{8,0},{9,1},... | collective-permute-start | bytes 3932168 | tf_op jit(solution)/shard_map/ppermute | solution.py:166
  28.7 28.1 %collective-permute-start.10 = (bf16[256,1280]{1,0:T(8,128)(2,1)S(1)}, bf16[256,1280]{1,0:T(8,128)(2,1)}, u32[]{:S(2)}, u32[]{:S(2)}) collective-permute-start(bf16[256,1280]{1,0:T(8,128)(2,1)S(1)} %constant_dynamic-update-slice_fusion.4.refs_0_), channel_id=1, source_target_pairs={{0,48},{1,49},{2,50},{3,51},{4,52},{5,53},{6,54},{7,55},{8,56},{9,... | collective-permute-start | bytes 1966088 | tf_op jit(solution)/shard_map/ppermute | solution.py:166
  67.1 34.0 %collective-permute-start.12 = (bf16[16,16,2560]{2,1,0:T(8,128)(2,1)S(1)}, bf16[16,16,2560]{2,1,0:T(8,128)(2,1)S(1)}, u32[]{:S(2)}, u32[]{:S(2)}) collective-permute-start(bf16[16,16,2560]{2,1,0:T(8,128)(2,1)S(1)} %get-tuple-element.106), channel_id=1, source_target_pairs={{0,1},{1,2},{2,3},{3,0},{4,5},{5,6},{6,7},{7,4},{8,9},{9,10},{10,1... | collective-permute-start | bytes 3932168 | tf_op jit(solution)/shard_map/ppermute | solution.py:166
  68.3 32.8 %collective-permute-start.13 = (bf16[16,16,2560]{2,1,0:T(8,128)(2,1)S(1)}, bf16[16,16,2560]{2,1,0:T(8,128)(2,1)S(1)}, u32[]{:S(2)}, u32[]{:S(2)}) collective-permute-start(bf16[16,16,2560]{2,1,0:T(8,128)(2,1)S(1)} %get-tuple-element.107), channel_id=1, source_target_pairs={{0,3},{1,0},{2,1},{3,2},{4,7},{5,4},{6,5},{7,6},{8,11},{9,8},{10,9... | collective-permute-start | bytes 3932168 | tf_op jit(solution)/shard_map/ppermute | solution.py:166
  69.1 32.0 %collective-permute-start.14 = (bf16[16,16,2560]{2,1,0:T(8,128)(2,1)S(1)}, bf16[16,16,2560]{2,1,0:T(8,128)(2,1)S(1)}, u32[]{:S(2)}, u32[]{:S(2)}) collective-permute-start(bf16[16,16,2560]{2,1,0:T(8,128)(2,1)S(1)} %get-tuple-element.108), channel_id=1, source_target_pairs={{0,2},{1,3},{2,0},{3,1},{4,6},{5,7},{6,4},{7,5},{8,10},{9,11},{10,... | collective-permute-start | bytes 3932168 | tf_op jit(solution)/shard_map/ppermute | solution.py:166
  75.0 26.1 %collective-permute-start.17 = (bf16[16,16,1280]{2,1,0:T(8,128)(2,1)S(1)}, bf16[16,16,1280]{2,1,0:T(8,128)(2,1)S(1)}, u32[]{:S(2)}, u32[]{:S(2)}) collective-permute-start(bf16[16,16,1280]{2,1,0:T(8,128)(2,1)S(1)} %get-tuple-element.116), channel_id=1, source_target_pairs={{0,8},{1,9},{2,10},{3,11},{4,12},{5,13},{6,14},{7,15},{8,0},{9,1},... | collective-permute-start | bytes 1966088 | tf_op jit(solution)/shard_map/ppermute | solution.py:166
  102.7 34.2 %collective-permute-start.18 = (bf16[3584,512]{1,0:T(8,128)(2,1)}, bf16[3584,512]{1,0:T(8,128)(2,1)}, u32[]{:S(2)}, u32[]{:S(2)}) collective-permute-start(bf16[3584,512]{1,0:T(8,128)(2,1)} %bitcast.13.refs_8_), channel_id=1, source_target_pairs={{0,64},{64,0},{1,65},{65,1},{2,66},{66,2},{3,67},{67,3},{4,68},{68... | collective-permute-start | bytes 11010056 | tf_op jit(solution)/shard_map/ppermute | solution.py:478
  103.0 33.9 %collective-permute-start.19 = (bf16[3584,512]{1,0:T(8,128)(2,1)}, bf16[3584,512]{1,0:T(8,128)(2,1)}, u32[]{:S(2)}, u32[]{:S(2)}) collective-permute-start(bf16[3584,512]{1,0:T(8,128)(2,1)} %bitcast.14.refs_9_), channel_id=1, source_target_pairs={{0,64},{64,0},{1,65},{65,1},{2,66},{66,2},{3,67},{67,3},{4,68},{68... | collective-permute-start | bytes 11010056 | tf_op jit(solution)/shard_map/ppermute | solution.py:478
  103.2 33.7 %collective-permute-start.20 = (bf16[512,3584]{1,0:T(8,128)(2,1)}, bf16[512,3584]{1,0:T(8,128)(2,1)}, u32[]{:S(2)}, u32[]{:S(2)}) collective-permute-start(bf16[512,3584]{1,0:T(8,128)(2,1)} %bitcast.15.refs_10_), channel_id=1, source_target_pairs={{0,64},{64,0},{1,65},{65,1},{2,66},{66,2},{3,67},{67,3},{4,68},{68... | collective-permute-start | bytes 11010056 | tf_op jit(solution)/shard_map/ppermute | solution.py:478
  103.5 70.6 %all-to-all-start = ((bf16[64,32,1152]{2,1,0:T(8,128)(2,1)}), bf16[64,32,1152]{2,1,0:T(8,128)(2,1)}, u32[]{:S(2)}, u32[]{:S(2)}) async-start(bf16[64,32,1152]{2,1,0:T(8,128)(2,1)} %copy-done), calls=%async_computation | async-start | bytes 9437184 | tf_op jit(solution)/shard_map/all_to_all | solution.py:476
  174.1 31.8 %collective-permute-start.21 = (bf16[16,16,2432]{2,1,0:T(8,128)(2,1)}, bf16[16,16,2432]{2,1,0:T(8,128)(2,1)S(1)}, u32[]{:S(2)}, u32[]{:S(2)}) collective-permute-start(bf16[16,16,2432]{2,1,0:T(8,128)(2,1)} %get-tuple-element.141), channel_id=1, source_target_pairs={{0,3},{1,0},{2,1},{3,2},{4,7},{5,4},{6,5},{7,6},{8,11},{9,8},{10,9... | collective-permute-start | bytes 3735560 | tf_op jit(solution)/shard_map/ppermute | solution.py:166
  174.4 31.6 %collective-permute-start.22 = (bf16[16,16,2432]{2,1,0:T(8,128)(2,1)}, bf16[16,16,2432]{2,1,0:T(8,128)(2,1)S(1)}, u32[]{:S(2)}, u32[]{:S(2)}) collective-permute-start(bf16[16,16,2432]{2,1,0:T(8,128)(2,1)} %get-tuple-element.142), channel_id=1, source_target_pairs={{0,1},{1,2},{2,3},{3,0},{4,5},{5,6},{6,7},{7,4},{8,9},{9,10},{10,1... | collective-permute-start | bytes 3735560 | tf_op jit(solution)/shard_map/ppermute | solution.py:166
  177.8 30.0 %collective-permute-start.23 = (bf16[16,16,2432]{2,1,0:T(8,128)(2,1)}, bf16[16,16,2432]{2,1,0:T(8,128)(2,1)}, u32[]{:S(2)}, u32[]{:S(2)}) collective-permute-start(bf16[16,16,2432]{2,1,0:T(8,128)(2,1)} %get-tuple-element.143), channel_id=1, source_target_pairs={{0,2},{1,3},{2,0},{3,1},{4,6},{5,7},{6,4},{7,5},{8,10},{9,11},{10,... | collective-permute-start | bytes 3735560 | tf_op jit(solution)/shard_map/ppermute | solution.py:166
  179.3 26.6 %collective-permute-start.25 = (bf16[16,16,1152]{2,1,0:T(8,128)(2,1)}, bf16[16,16,1152]{2,1,0:T(8,128)(2,1)}, u32[]{:S(2)}, u32[]{:S(2)}) collective-permute-start(bf16[16,16,1152]{2,1,0:T(8,128)(2,1)} %get-tuple-element.145), channel_id=1, source_target_pairs={{0,4},{1,5},{2,6},{3,7},{4,8},{5,9},{6,10},{7,11},{8,12},{9,13},{1... | collective-permute-start | bytes 1769480 | tf_op jit(solution)/shard_map/ppermute | solution.py:166
  187.5 18.4 %collective-permute-start.26 = (bf16[16,16,1152]{2,1,0:T(8,128)(2,1)}, bf16[16,16,1152]{2,1,0:T(8,128)(2,1)S(1)}, u32[]{:S(2)}, u32[]{:S(2)}) collective-permute-start(bf16[16,16,1152]{2,1,0:T(8,128)(2,1)} %get-tuple-element.146), channel_id=1, source_target_pairs={{0,8},{1,9},{2,10},{3,11},{4,12},{5,13},{6,14},{7,15},{8,0},{9,1},... | collective-permute-start | bytes 1769480 | tf_op jit(solution)/shard_map/ppermute | solution.py:166
  211.4 40.8 %collective-permute-start.27 = (bf16[256,2432]{1,0:T(8,128)(2,1)S(1)}, bf16[256,2432]{1,0:T(8,128)(2,1)S(1)}, u32[]{:S(2)}, u32[]{:S(2)}) collective-permute-start(bf16[256,2432]{1,0:T(8,128)(2,1)S(1)} %get-tuple-element.151), channel_id=1, source_target_pairs={{0,12},{1,13},{2,14},{3,15},{4,0},{5,1},{6,2},{7,3},{8,4},{9,5},{1... | collective-permute-start | bytes 3735560 | tf_op jit(solution)/shard_map/ppermute | solution.py:166
  211.5 40.7 %collective-permute-start.28 = (bf16[256,2432]{1,0:T(8,128)(2,1)S(1)}, bf16[256,2432]{1,0:T(8,128)(2,1)S(1)}, u32[]{:S(2)}, u32[]{:S(2)}) collective-permute-start(bf16[256,2432]{1,0:T(8,128)(2,1)S(1)} %get-tuple-element.152), channel_id=1, source_target_pairs={{0,4},{1,5},{2,6},{3,7},{4,8},{5,9},{6,10},{7,11},{8,12},{9,13},{1... | collective-permute-start | bytes 3735560 | tf_op jit(solution)/shard_map/ppermute | solution.py:166
  213.5 38.7 %collective-permute-start.29 = (bf16[256,2432]{1,0:T(8,128)(2,1)S(1)}, bf16[256,2432]{1,0:T(8,128)(2,1)S(1)}, u32[]{:S(2)}, u32[]{:S(2)}) collective-permute-start(bf16[256,2432]{1,0:T(8,128)(2,1)S(1)} %get-tuple-element.153), channel_id=1, source_target_pairs={{0,8},{1,9},{2,10},{3,11},{4,12},{5,13},{6,14},{7,15},{8,0},{9,1},... | collective-permute-start | bytes 3735560 | tf_op jit(solution)/shard_map/ppermute | solution.py:166
  220.7 31.5 %collective-permute-start.31 = (bf16[256,1152]{1,0:T(8,128)(2,1)S(1)}, bf16[256,1152]{1,0:T(8,128)(2,1)S(1)}, u32[]{:S(2)}, u32[]{:S(2)}) collective-permute-start(bf16[256,1152]{1,0:T(8,128)(2,1)S(1)} %get-tuple-element.160), channel_id=1, source_target_pairs={{0,16},{1,17},{2,18},{3,19},{4,20},{5,21},{6,22},{7,23},{8,24},{9,... | collective-permute-start | bytes 1769480 | tf_op jit(solution)/shard_map/ppermute | solution.py:166
  232.5 19.7 %collective-permute-start.32 = (bf16[256,1152]{1,0:T(8,128)(2,1)S(1)}, bf16[256,1152]{1,0:T(8,128)(2,1)S(1)}, u32[]{:S(2)}, u32[]{:S(2)}) collective-permute-start(bf16[256,1152]{1,0:T(8,128)(2,1)S(1)} %get-tuple-element.161), channel_id=1, source_target_pairs={{0,32},{1,33},{2,34},{3,35},{4,36},{5,37},{6,38},{7,39},{8,40},{9,... | collective-permute-start | bytes 1769480 | tf_op jit(solution)/shard_map/ppermute | solution.py:166
  253.0 19.4 %collective-permute-start.33 = (bf16[64,2432]{1,0:T(8,128)(2,1)S(1)}, bf16[64,2432]{1,0:T(8,128)(2,1)S(1)}, u32[]{:S(2)}, u32[]{:S(2)}) collective-permute-start(bf16[64,2432]{1,0:T(8,128)(2,1)S(1)} %get-tuple-element.189), channel_id=1, source_target_pairs={{0,48},{1,49},{2,50},{3,51},{4,52},{5,53},{6,54},{7,55},{8,56},{9,... | collective-permute-start | bytes 933896 | tf_op jit(solution)/shard_map/ppermute | solution.py:166
  253.9 18.4 %collective-permute-start.34 = (bf16[64,2432]{1,0:T(8,128)(2,1)S(1)}, bf16[64,2432]{1,0:T(8,128)(2,1)S(1)}, u32[]{:S(2)}, u32[]{:S(2)}) collective-permute-start(bf16[64,2432]{1,0:T(8,128)(2,1)S(1)} %get-tuple-element.188), channel_id=1, source_target_pairs={{0,16},{1,17},{2,18},{3,19},{4,20},{5,21},{6,22},{7,23},{8,24},{9,... | collective-permute-start | bytes 933896 | tf_op jit(solution)/shard_map/ppermute | solution.py:166
  (33 other events, 353.4 us)

commit v4 on v3

--- a/solution.py
+++ b/solution.py
@@ -266,10 +266,10 @@
     columns, rings = together(columns, rings)
     lines = [jnp.concatenate([columns[i]] + rings[i], axis=0) for i in both]
     rings = [exchange([lines[i]] * 3, second[i], (1, -1, 2)) for i in both]
-    packed_cache, rings[1][0] = together(packed_cache, rings[1][0])
     lines, rings = together(lines, rings)
     picked = [select(targets[i], [lines[i]] + rings[i]) for i in both]
     rings = [exchange(picked[i][1:SIDE], third[i], TARGETS[1:]) for i in both]
+    packed_cache, rings[1][0] = together(packed_cache, rings[1][0])
     return [[picked[i][0]] + rings[i] for i in both], [p[SIDE] for p in picked], packed_cache
 
 

time: 276 us -> 275 us (level)
  waiting for transfers between devices: 92.9 us -> 98.8 us
  local copies, waits for them, and re-layouts: 19 us -> 15.3 us
    ppermute x36, waiting for transfers between devices: 79.3 us -> 83.7 us  [hop(): return lax.ppermute(value, ('dp', 'ep'), pairs)]
    unnamed x42 -> x52, local copies, waits for them, and re-layouts: 14.8 us -> 11.8 us
  transfers between devices with their start and end apart: 40 -> 40, of which waited for: 15 -> 14; matrix products, arithmetic and copies ran while one was open for 3% -> 1% of each run, Pallas kernels for 31% -> 31%
where the time goes in v4:
time: 275 us
  waiting for transfers between devices  98.8 us (36%)
  Pallas kernels  90.7 us (33%)
  starting transfers between devices  65.1 us (24%)
  local copies, waits for them, and re-layouts  15.3 us (6%)
  other arithmetic  3.79 us (1%)
    ppermute x36, waiting for transfers between devices, hop(): return lax.ppermute(value, ('dp', 'ep'), pairs)  83.7 us
    ppermute x36, starting transfers between devices, hop(): return lax.ppermute(value, ('dp', 'ep'), pairs)  53.5 us
    pallas_call x2, Pallas kernels, attend(): pl.pallas_call(kernel, grid=(1,), out_shape=jax.ShapeDtypeStruct((STEPS,...  28.9 us
    pallas_call x1, Pallas kernels, first_half(): pl.pallas_call(first_half_kernel, out_shape=[whole, whole, jax.ShapeDtype...  23.9 us
    pallas_call x1, Pallas kernels, second_half(): pl.pallas_call(second_half_kernel, out_shape=[jax.ShapeDtypeStruct(shape,...  23.6 us
    all_to_all x1, waiting for transfers between devices, on_device(): lax.all_to_all(packed_cache, 'ep', split_axis=0, concat_axis=0, tiled=True)  15.1 us
    unnamed x52, local copies, waits for them, and re-layouts  11.8 us
    all_to_all x1, starting transfers between devices, on_device(): lax.all_to_all(packed_cache, 'ep', split_axis=0, concat_axis=0, tiled=True)  10.9 us
  transfers between devices with their start and end apart: 40, of which 14 were waited for; matrix products, arithmetic and copies ran while one was open for 1% of the time, Pallas kernels for 31%

profile of v4, /device:TPU:10, one launch (start us, length us, event | category | flops | bytes accessed | tf_op | source)
XLA Modules:
  0.0 274.8 jit_solution(4074005309198988983)
XLA Ops:
  14.3 3.0 %collective-permute-done.4 = bf16[64,1280]{1,0:T(8,128)(2,1)S(1)} collective-permute-done((bf16[64,1280]{1,0:T(8,128)(2,1)S(1)}, bf16[64,1280]{1,0:T(8,128)(2,1)S(1)}, u32[]{:S(2)}, u32[]{:S(2)}) %collective-permute-start.4) | collective-permute-done | bytes 163872 | tf_op jit(solution)/shard_map/ppermute | solution.py:166
  27.7 10.1 %collective-permute-done.9.refs_1_ = bf16[256,1280]{1,0:T(8,128)(2,1)S(1)} collective-permute-done((bf16[256,1280]{1,0:T(8,128)(2,1)S(1)}, bf16[256,1280]{1,0:T(8,128)(2,1)S(1)}, u32[]{:S(2)}, u32[]{:S(2)}) %collective-permute-start.9) | collective-permute-done | bytes 655392 | tf_op jit(solution)/shard_map/ppermute | solution.py:166
  40.0 16.1 %collective-permute-done.11.refs_3_ = bf16[256,1280]{1,0:T(8,128)(2,1)} collective-permute-done((bf16[256,1280]{1,0:T(8,128)(2,1)S(1)}, bf16[256,1280]{1,0:T(8,128)(2,1)}, u32[]{:S(2)}, u32[]{:S(2)}) %collective-permute-start.11) | collective-permute-done | bytes 655392 | tf_op jit(solution)/shard_map/ppermute | solution.py:166
  57.1 2.7 shard_map.141
  60.7 4.0 %shard_map.140 = (bf16[16,16,2560]{2,1,0:T(8,128)(2,1)S(1)}, bf16[16,16,2560]{2,1,0:T(8,128)(2,1)S(1)}, bf16[16,16,2560]{2,1,0:T(8,128)(2,1)S(1)}, bf16[16,16,2560]{2,1,0:T(8,128)(2,1)S(1)}, f32[4,8,256]{2,1,0:T(8,128)S(1)}) custom-call(s32[4]{0:T(128)S(1)} %pad_add_fusion.targets_ref, bf16[256,2560]{1,0:T(8,128)(2,1)S(1)} %constant_dynamic-update-slice_fusion.refs_0_, ...), custom_call_target="tpu_custom_call" | custom-call | flops 1342177280 | bytes 10485760 | tf_op jit(solution)/shard_map/pallas_call | solution.py:210
  70.2 5.7 %collective-permute-done.15.refs_5_ = bf16[16,16,1280]{2,1,0:T(8,128)(2,1)S(1)} collective-permute-done((bf16[16,16,1280]{2,1,0:T(8,128)(2,1)S(1)}, bf16[16,16,1280]{2,1,0:T(8,128)(2,1)S(1)}, u32[]{:S(2)}, u32[]{:S(2)}) %collective-permute-start.15) | collective-permute-done | bytes 655392 | tf_op jit(solution)/shard_map/ppermute | solution.py:166
  81.4 4.0 %collective-permute-done.16.refs_6_ = bf16[16,16,1280]{2,1,0:T(8,128)(2,1)S(1)} collective-permute-done((bf16[16,16,1280]{2,1,0:T(8,128)(2,1)S(1)}, bf16[16,16,1280]{2,1,0:T(8,128)(2,1)S(1)}, u32[]{:S(2)}, u32[]{:S(2)}) %collective-permute-start.16) | collective-permute-done | bytes 655392 | tf_op jit(solution)/shard_map/ppermute | solution.py:166
  85.4 13.1 %collective-permute-done.17.refs_7_ = bf16[16,16,1280]{2,1,0:T(8,128)(2,1)S(1)} collective-permute-done((bf16[16,16,1280]{2,1,0:T(8,128)(2,1)S(1)}, bf16[16,16,1280]{2,1,0:T(8,128)(2,1)S(1)}, u32[]{:S(2)}, u32[]{:S(2)}) %collective-permute-start.17) | collective-permute-done | bytes 655392 | tf_op jit(solution)/shard_map/ppermute | solution.py:166
  100.7 10.9 %all-to-all-start = ((bf16[64,32,1152]{2,1,0:T(8,128)(2,1)}), bf16[64,32,1152]{2,1,0:T(8,128)(2,1)}, u32[]{:S(2)}, u32[]{:S(2)}) async-start(bf16[64,32,1152]{2,1,0:T(8,128)(2,1)} %copy-done), calls=%async_computation | async-start | bytes 9437184 | tf_op jit(solution)/shard_map/all_to_all | solution.py:476
  111.6 23.9 %shard_map.143 = (bf16[64,16,3584]{2,1,0:T(8,128)(2,1)}, bf16[64,16,3584]{2,1,0:T(8,128)(2,1)}, f32[64,16,128]{2,1,0:T(8,128)S(1)}) custom-call(s32[64]{0:T(128)S(1)} %broadcast_select_fusion.order_ref, s32[1]{0:T(128)} %bitcast.6.me_ref, bf16[16,16,2560]{2,1,0:T(8,128)(2,1)} %copy-done.7, bf16[16,16,2560]{2,1,0:T(8,128)(2,1)} %copy-done.17, ...), custom_call_target="tpu_custom_call" | custom-call | flops 11274289152 | bytes 33030144 | tf_op jit(solution)/shard_map/pallas_call | solution.py:372
  135.6 23.6 %shard_map.144 = (bf16[16,16,2432]{2,1,0:T(8,128)(2,1)}, bf16[16,16,2432]{2,1,0:T(8,128)(2,1)}, bf16[16,16,2432]{2,1,0:T(8,128)(2,1)}, bf16[16,16,2432]{2,1,0:T(...) custom-call(s32[64]{0:T(128)S(1)} %broadcast_select_fusion.order_ref, ...), custom_call_target="tpu_custom_call" | custom-call | flops 11274289152 | bytes 33030144 | tf_op jit(solution)/shard_map/pallas_call | solution.py:385
  159.2 15.1 %all-to-all-done.got_ref.refs_1_ = bf16[64,32,1152]{2,1,0:T(8,128)(2,1)} async-done(((bf16[64,32,1152]{2,1,0:T(8,128)(2,1)}), bf16[64,32,1152]{2,1,0:T(8,128)(2,1)}, u32[]{:S(2)}, u32[]{:S(2)}) %all-to-all-start) | async-done | bytes 4718624 | tf_op jit(solution)/shard_map/all_to_all | solution.py:476
  181.1 6.9 %collective-permute-done.24.refs_1_ = bf16[16,16,1152]{2,1,0:T(8,128)(2,1)} collective-permute-done((bf16[16,16,1152]{2,1,0:T(8,128)(2,1)}, bf16[16,16,1152]{2,1,0:T(8,128)(2,1)}, u32[]{:S(2)}, u32[]{:S(2)}) %collective-permute-start.24) | collective-permute-done | bytes 589856 | tf_op jit(solution)/shard_map/ppermute | solution.py:166
  188.1 2.3 copy-done.1
  190.5 14.5 %shard_map.145.refs_5_ = bf16[2,32,32768]{2,1,0:T(8,128)(2,1)} custom-call(s32[16]{0:T(128)S(1)} %get-tuple-element.201.landing_ref, bf16[64,32,1152]{2,1,0:T(8,128)(2,1)} %all-to-all-done.got_ref.refs_1_, s32[32,1]{1,0:T(8,128)S(1)} %copy.23.len_ref.refs_2_, bf16[2,32,576]{2,1,0:T(8,128)(2,1)S(1)} %copy-done.6, bf16[2,32,36864]{2,1,0:T(8,128)(2,1)S(1)} %copy-done.1), custom_call_target="tpu_custom_call" | custom-call | flops 4831838208 | bytes 4456448 | tf_op jit(solution)/shard_map/pallas_call | solution.py:136
  205.0 3.6 %shard_map.146 = (bf16[256,2432]{1,0:T(8,128)(2,1)S(1)}, bf16[256,2432]{1,0:T(8,128)(2,1)S(1)}, bf16[256,2432]{1,0:T(8,128)(2,1)S(1)}, bf16[256,2432]{1,0:T(8,128)(2,1)S(1)}) custom-call(s32[4]{0:T(128)S(1)} %pad_add_fusion.targets_ref, f32[4,8,256]{2,1,0:T(8,128)S(1)} %get-tuple-element.103.ids_ref, bf16[16,16,2432]{2,1,0:T(8,128)(2,1)S(1)} %copy-done.3, ...), custom_call_target="tpu_custom_call" | custom-call | flops 1275068416 | bytes 9961472 | tf_op jit(solution)/shard_map/pallas_call | solution.py:238
  210.9 4.6 %collective-permute-start.29 = (bf16[256,2432]{1,0:T(8,128)(2,1)S(1)}, bf16[256,2432]{1,0:T(8,128)(2,1)S(1)}, u32[]{:S(2)}, u32[]{:S(2)}) collective-permute-start(bf16[256,2432]{1,0:T(8,128)(2,1)S(1)} %get-tuple-element.153), channel_id=1, source_target_pairs={{0,8},{1,9},{2,10},{3,11},{4,12},{5,13},{6,14},{7,15},{8,0},{9,1},... | collective-permute-start | bytes 3735560 | tf_op jit(solution)/shard_map/ppermute | solution.py:166
  215.5 2.8 %shard_map.147 = (bf16[256,1152]{1,0:T(8,128)(2,1)S(1)}, bf16[256,1152]{1,0:T(8,128)(2,1)S(1)}, bf16[256,1152]{1,0:T(8,128)(2,1)S(1)}, bf16[256,1152]{1,0:T(8,128)(2,1)S(1)}) custom-call(s32[4]{0:T(128)S(1)} %pad_add_fusion.1.targets_ref, f32[4,8,256]{2,1,0:T(8,128)S(1)} %get-tuple-element.154.ids_ref, bf16[16,16,1152]{2,1,0:T(8,128)(2,1)S(1)} %get-tuple-element.155.refs_0_, ...), custom_call_target="tpu_custom_call" | custom-call | flops 603979776 | bytes 4718592 | tf_op jit(solution)/shard_map/pallas_call | solution.py:238
  220.4 10.7 %collective-permute-done.30 = bf16[256,1152]{1,0:T(8,128)(2,1)S(1)} collective-permute-done((bf16[256,1152]{1,0:T(8,128)(2,1)S(1)}, bf16[256,1152]{1,0:T(8,128)(2,1)S(1)}, u32[]{:S(2)}, u32[]{:S(2)}) %collective-permute-start.30) | collective-permute-done | bytes 589856 | tf_op jit(solution)/shard_map/ppermute | solution.py:166
  235.6 14.4 %shard_map.148 = bf16[2,32,32768]{2,1,0:T(8,128)(2,1)} custom-call(s32[16]{0:T(128)S(1)} %get-tuple-element.200.refs_0_, bf16[64,32,1152]{2,1,0:T(8,128)(2,1)} %all-to-all-done.got_ref.refs_1_, s32[32,1]{1,0:T(8,128)S(1)} %copy.23.len_ref.refs_2_, bf16[2,32,576]{2,1,0:T(8,128)(2,1)S(1)} %copy-done.6, ...), custom_call_target="tpu_custom_call", output_to_operand_aliasing={{}: (5, {})} | custom-call | flops 4831838208 | bytes 4456448 | tf_op jit(solution)/shard_map/pallas_call | solution.py:136
  255.4 2.4 collective-permute-start.36
  257.8 4.6 %collective-permute-start.37 = (bf16[64,1152]{1,0:T(8,128)(2,1)S(1)}, bf16[64,1152]{1,0:T(8,128)(2,1)S(1)}, u32[]{:S(2)}, u32[]{:S(2)}) collective-permute-start(bf16[64,1152]{1,0:T(8,128)(2,1)S(1)} %get-tuple-element.192), channel_id=1, source_target_pairs={{0,1},{1,2},{2,3},{3,0},{4,5},{5,6},{6,7},{7,4},{8,9},{9,10},{10,1... | collective-permute-start | bytes 442376 | tf_op jit(solution)/shard_map/ppermute | solution.py:166
  262.4 4.6 %collective-permute-done.36 = bf16[64,1152]{1,0:T(8,128)(2,1)S(1)} collective-permute-done((bf16[64,1152]{1,0:T(8,128)(2,1)S(1)}, bf16[64,1152]{1,0:T(8,128)(2,1)S(1)}, u32[]{:S(2)}, u32[]{:S(2)}) %collective-permute-start.36) | collective-permute-done | bytes 147488 | tf_op jit(solution)/shard_map/ppermute | solution.py:166
  267.1 6.6 %collective-permute-done.38 = bf16[64,1152]{1,0:T(8,128)(2,1)S(1)} collective-permute-done((bf16[64,1152]{1,0:T(8,128)(2,1)S(1)}, bf16[64,1152]{1,0:T(8,128)(2,1)S(1)}, u32[]{:S(2)}, u32[]{:S(2)}) %collective-permute-start.38) | collective-permute-done | bytes 147488 | tf_op jit(solution)/shard_map/ppermute | solution.py:166
  (147 shorter events, 63.5 us)
Async XLA Ops:
  19.9 17.9 %collective-permute-start.9 = (bf16[256,1280]{1,0:T(8,128)(2,1)S(1)}, bf16[256,1280]{1,0:T(8,128)(2,1)S(1)}, u32[]{:S(2)}, u32[]{:S(2)}) collective-permute-start(bf16[256,1280]{1,0:T(8,128)(2,1)S(1)} %constant_dynamic-update-slice_fusion.4.refs_0_), channel_id=1, source_target_pairs={{0,16},{1,17},{2,18},{3,19},{4,20},{5,21},{6,22},{7,23},{8,24},{9,... | collective-permute-start | bytes 1966088 | tf_op jit(solution)/shard_map/ppermute | solution.py:166
  21.5 34.5 %collective-permute-start.6 = (bf16[256,2560]{1,0:T(8,128)(2,1)S(1)}, bf16[256,2560]{1,0:T(8,128)(2,1)S(1)}, u32[]{:S(2)}, u32[]{:S(2)}) collective-permute-start(bf16[256,2560]{1,0:T(8,128)(2,1)S(1)} %constant_dynamic-update-slice_fusion.refs_0_), channel_id=1, source_target_pairs={{0,4},{1,5},{2,6},{3,7},{4,8},{5,9},{6,10},{7,11},{8,12},{9,13},{1... | collective-permute-start | bytes 3932168 | tf_op jit(solution)/shard_map/ppermute | solution.py:166
  23.2 32.9 %collective-permute-start.7 = (bf16[256,2560]{1,0:T(8,128)(2,1)S(1)}, bf16[256,2560]{1,0:T(8,128)(2,1)}, u32[]{:S(2)}, u32[]{:S(2)}) collective-permute-start(bf16[256,2560]{1,0:T(8,128)(2,1)S(1)} %constant_dynamic-update-slice_fusion.refs_0_), channel_id=1, source_target_pairs={{0,12},{1,13},{2,14},{3,15},{4,0},{5,1},{6,2},{7,3},{8,4},{9,5},{1... | collective-permute-start | bytes 3932168 | tf_op jit(solution)/shard_map/ppermute | solution.py:166
  23.6 32.4 %collective-permute-start.8 = (bf16[256,2560]{1,0:T(8,128)(2,1)S(1)}, bf16[256,2560]{1,0:T(8,128)(2,1)}, u32[]{:S(2)}, u32[]{:S(2)}) collective-permute-start(bf16[256,2560]{1,0:T(8,128)(2,1)S(1)} %constant_dynamic-update-slice_fusion.refs_0_), channel_id=1, source_target_pairs={{0,8},{1,9},{2,10},{3,11},{4,12},{5,13},{6,14},{7,15},{8,0},{9,1},... | collective-permute-start | bytes 3932168 | tf_op jit(solution)/shard_map/ppermute | solution.py:166
  64.7 33.8 %collective-permute-start.12 = (bf16[16,16,2560]{2,1,0:T(8,128)(2,1)S(1)}, bf16[16,16,2560]{2,1,0:T(8,128)(2,1)S(1)}, u32[]{:S(2)}, u32[]{:S(2)}) collective-permute-start(bf16[16,16,2560]{2,1,0:T(8,128)(2,1)S(1)} %get-tuple-element.105), channel_id=1, source_target_pairs={{0,1},{1,2},{2,3},{3,0},{4,5},{5,6},{6,7},{7,4},{8,9},{9,10},{10,1... | collective-permute-start | bytes 3932168 | tf_op jit(solution)/shard_map/ppermute | solution.py:166
  65.5 32.9 %collective-permute-start.13 = (bf16[16,16,2560]{2,1,0:T(8,128)(2,1)S(1)}, bf16[16,16,2560]{2,1,0:T(8,128)(2,1)S(1)}, u32[]{:S(2)}, u32[]{:S(2)}) collective-permute-start(bf16[16,16,2560]{2,1,0:T(8,128)(2,1)S(1)} %get-tuple-element.106), channel_id=1, source_target_pairs={{0,3},{1,0},{2,1},{3,2},{4,7},{5,4},{6,5},{7,6},{8,11},{9,8},{10,9... | collective-permute-start | bytes 3932168 | tf_op jit(solution)/shard_map/ppermute | solution.py:166
  66.8 31.7 %collective-permute-start.14 = (bf16[16,16,2560]{2,1,0:T(8,128)(2,1)S(1)}, bf16[16,16,2560]{2,1,0:T(8,128)(2,1)S(1)}, u32[]{:S(2)}, u32[]{:S(2)}) collective-permute-start(bf16[16,16,2560]{2,1,0:T(8,128)(2,1)S(1)} %get-tuple-element.107), channel_id=1, source_target_pairs={{0,2},{1,3},{2,0},{3,1},{4,6},{5,7},{6,4},{7,5},{8,10},{9,11},{10,... | collective-permute-start | bytes 3932168 | tf_op jit(solution)/shard_map/ppermute | solution.py:166
  75.9 22.6 %collective-permute-start.17 = (bf16[16,16,1280]{2,1,0:T(8,128)(2,1)S(1)}, bf16[16,16,1280]{2,1,0:T(8,128)(2,1)S(1)}, u32[]{:S(2)}, u32[]{:S(2)}) collective-permute-start(bf16[16,16,1280]{2,1,0:T(8,128)(2,1)S(1)} %get-tuple-element.116), channel_id=1, source_target_pairs={{0,8},{1,9},{2,10},{3,11},{4,12},{5,13},{6,14},{7,15},{8,0},{9,1},... | collective-permute-start | bytes 1966088 | tf_op jit(solution)/shard_map/ppermute | solution.py:166
  100.0 35.6 %collective-permute-start.18 = (bf16[3584,512]{1,0:T(8,128)(2,1)}, bf16[3584,512]{1,0:T(8,128)(2,1)}, u32[]{:S(2)}, u32[]{:S(2)}) collective-permute-start(bf16[3584,512]{1,0:T(8,128)(2,1)} %bitcast.13.refs_8_), channel_id=1, source_target_pairs={{0,64},{64,0},{1,65},{65,1},{2,66},{66,2},{3,67},{67,3},{4,68},{68... | collective-permute-start | bytes 11010056 | tf_op jit(solution)/shard_map/ppermute | solution.py:478
  100.1 35.5 %collective-permute-start.19 = (bf16[3584,512]{1,0:T(8,128)(2,1)}, bf16[3584,512]{1,0:T(8,128)(2,1)}, u32[]{:S(2)}, u32[]{:S(2)}) collective-permute-start(bf16[3584,512]{1,0:T(8,128)(2,1)} %bitcast.14.refs_9_), channel_id=1, source_target_pairs={{0,64},{64,0},{1,65},{65,1},{2,66},{66,2},{3,67},{67,3},{4,68},{68... | collective-permute-start | bytes 11010056 | tf_op jit(solution)/shard_map/ppermute | solution.py:478
  100.6 35.0 %collective-permute-start.20 = (bf16[512,3584]{1,0:T(8,128)(2,1)}, bf16[512,3584]{1,0:T(8,128)(2,1)}, u32[]{:S(2)}, u32[]{:S(2)}) collective-permute-start(bf16[512,3584]{1,0:T(8,128)(2,1)} %bitcast.15.refs_10_), channel_id=1, source_target_pairs={{0,64},{64,0},{1,65},{65,1},{2,66},{66,2},{3,67},{67,3},{4,68},{68... | collective-permute-start | bytes 11010056 | tf_op jit(solution)/shard_map/ppermute | solution.py:478
  100.7 73.6 %all-to-all-start = ((bf16[64,32,1152]{2,1,0:T(8,128)(2,1)}), bf16[64,32,1152]{2,1,0:T(8,128)(2,1)}, u32[]{:S(2)}, u32[]{:S(2)}) async-start(bf16[64,32,1152]{2,1,0:T(8,128)(2,1)} %copy-done), calls=%async_computation | async-start | bytes 9437184 | tf_op jit(solution)/shard_map/all_to_all | solution.py:476
  174.3 30.7 %collective-permute-start.21 = (bf16[16,16,2432]{2,1,0:T(8,128)(2,1)}, bf16[16,16,2432]{2,1,0:T(8,128)(2,1)S(1)}, u32[]{:S(2)}, u32[]{:S(2)}) collective-permute-start(bf16[16,16,2432]{2,1,0:T(8,128)(2,1)} %get-tuple-element.141), channel_id=1, source_target_pairs={{0,3},{1,0},{2,1},{3,2},{4,7},{5,4},{6,5},{7,6},{8,11},{9,8},{10,9... | collective-permute-start | bytes 3735560 | tf_op jit(solution)/shard_map/ppermute | solution.py:166
  174.3 30.7 %collective-permute-start.22 = (bf16[16,16,2432]{2,1,0:T(8,128)(2,1)}, bf16[16,16,2432]{2,1,0:T(8,128)(2,1)S(1)}, u32[]{:S(2)}, u32[]{:S(2)}) collective-permute-start(bf16[16,16,2432]{2,1,0:T(8,128)(2,1)} %get-tuple-element.142), channel_id=1, source_target_pairs={{0,1},{1,2},{2,3},{3,0},{4,5},{5,6},{6,7},{7,4},{8,9},{9,10},{10,1... | collective-permute-start | bytes 3735560 | tf_op jit(solution)/shard_map/ppermute | solution.py:166
  176.3 28.7 %collective-permute-start.23 = (bf16[16,16,2432]{2,1,0:T(8,128)(2,1)}, bf16[16,16,2432]{2,1,0:T(8,128)(2,1)}, u32[]{:S(2)}, u32[]{:S(2)}) collective-permute-start(bf16[16,16,2432]{2,1,0:T(8,128)(2,1)} %get-tuple-element.143), channel_id=1, source_target_pairs={{0,2},{1,3},{2,0},{3,1},{4,6},{5,7},{6,4},{7,5},{8,10},{9,11},{10,... | collective-permute-start | bytes 3735560 | tf_op jit(solution)/shard_map/ppermute | solution.py:166
  178.2 26.7 %collective-permute-start.25 = (bf16[16,16,1152]{2,1,0:T(8,128)(2,1)}, bf16[16,16,1152]{2,1,0:T(8,128)(2,1)}, u32[]{:S(2)}, u32[]{:S(2)}) collective-permute-start(bf16[16,16,1152]{2,1,0:T(8,128)(2,1)} %get-tuple-element.145), channel_id=1, source_target_pairs={{0,4},{1,5},{2,6},{3,7},{4,8},{5,9},{6,10},{7,11},{8,12},{9,13},{1... | collective-permute-start | bytes 1769480 | tf_op jit(solution)/shard_map/ppermute | solution.py:166
  208.6 41.4 %collective-permute-start.27 = (bf16[256,2432]{1,0:T(8,128)(2,1)S(1)}, bf16[256,2432]{1,0:T(8,128)(2,1)S(1)}, u32[]{:S(2)}, u32[]{:S(2)}) collective-permute-start(bf16[256,2432]{1,0:T(8,128)(2,1)S(1)} %get-tuple-element.151), channel_id=1, source_target_pairs={{0,12},{1,13},{2,14},{3,15},{4,0},{5,1},{6,2},{7,3},{8,4},{9,5},{1... | collective-permute-start | bytes 3735560 | tf_op jit(solution)/shard_map/ppermute | solution.py:166
  210.6 39.4 %collective-permute-start.28 = (bf16[256,2432]{1,0:T(8,128)(2,1)S(1)}, bf16[256,2432]{1,0:T(8,128)(2,1)S(1)}, u32[]{:S(2)}, u32[]{:S(2)}) collective-permute-start(bf16[256,2432]{1,0:T(8,128)(2,1)S(1)} %get-tuple-element.152), channel_id=1, source_target_pairs={{0,4},{1,5},{2,6},{3,7},{4,8},{5,9},{6,10},{7,11},{8,12},{9,13},{1... | collective-permute-start | bytes 3735560 | tf_op jit(solution)/shard_map/ppermute | solution.py:166
  210.9 39.2 %collective-permute-start.29 = (bf16[256,2432]{1,0:T(8,128)(2,1)S(1)}, bf16[256,2432]{1,0:T(8,128)(2,1)S(1)}, u32[]{:S(2)}, u32[]{:S(2)}) collective-permute-start(bf16[256,2432]{1,0:T(8,128)(2,1)S(1)} %get-tuple-element.153), channel_id=1, source_target_pairs={{0,8},{1,9},{2,10},{3,11},{4,12},{5,13},{6,14},{7,15},{8,0},{9,1},... | collective-permute-start | bytes 3735560 | tf_op jit(solution)/shard_map/ppermute | solution.py:166
  220.2 29.8 %collective-permute-start.31 = (bf16[256,1152]{1,0:T(8,128)(2,1)S(1)}, bf16[256,1152]{1,0:T(8,128)(2,1)S(1)}, u32[]{:S(2)}, u32[]{:S(2)}) collective-permute-start(bf16[256,1152]{1,0:T(8,128)(2,1)S(1)} %get-tuple-element.160), channel_id=1, source_target_pairs={{0,16},{1,17},{2,18},{3,19},{4,20},{5,21},{6,22},{7,23},{8,24},{9,... | collective-permute-start | bytes 1769480 | tf_op jit(solution)/shard_map/ppermute | solution.py:166
  231.1 18.9 %collective-permute-start.32 = (bf16[256,1152]{1,0:T(8,128)(2,1)S(1)}, bf16[256,1152]{1,0:T(8,128)(2,1)S(1)}, u32[]{:S(2)}, u32[]{:S(2)}) collective-permute-start(bf16[256,1152]{1,0:T(8,128)(2,1)S(1)} %get-tuple-element.161), channel_id=1, source_target_pairs={{0,32},{1,33},{2,34},{3,35},{4,36},{5,37},{6,38},{7,39},{8,40},{9,... | collective-permute-start | bytes 1769480 | tf_op jit(solution)/shard_map/ppermute | solution.py:166
  250.8 22.9 %collective-permute-start.33 = (bf16[64,2432]{1,0:T(8,128)(2,1)S(1)}, bf16[64,2432]{1,0:T(8,128)(2,1)S(1)}, u32[]{:S(2)}, u32[]{:S(2)}) collective-permute-start(bf16[64,2432]{1,0:T(8,128)(2,1)S(1)} %get-tuple-element.189), channel_id=1, source_target_pairs={{0,48},{1,49},{2,50},{3,51},{4,52},{5,53},{6,54},{7,55},{8,56},{9,... | collective-permute-start | bytes 933896 | tf_op jit(solution)/shard_map/ppermute | solution.py:166
  252.7 21.0 %collective-permute-start.34 = (bf16[64,2432]{1,0:T(8,128)(2,1)S(1)}, bf16[64,2432]{1,0:T(8,128)(2,1)S(1)}, u32[]{:S(2)}, u32[]{:S(2)}) collective-permute-start(bf16[64,2432]{1,0:T(8,128)(2,1)S(1)} %get-tuple-element.188), channel_id=1, source_target_pairs={{0,16},{1,17},{2,18},{3,19},{4,20},{5,21},{6,22},{7,23},{8,24},{9,... | collective-permute-start | bytes 933896 | tf_op jit(solution)/shard_map/ppermute | solution.py:166
  253.1 20.6 %collective-permute-start.35 = (bf16[64,2432]{1,0:T(8,128)(2,1)S(1)}, bf16[64,2432]{1,0:T(8,128)(2,1)S(1)}, u32[]{:S(2)}, u32[]{:S(2)}) collective-permute-start(bf16[64,2432]{1,0:T(8,128)(2,1)S(1)} %get-tuple-element.187), channel_id=1, source_target_pairs={{0,32},{1,33},{2,34},{3,35},{4,36},{5,37},{6,38},{7,39},{8,40},{9,... | collective-permute-start | bytes 933896 | tf_op jit(solution)/shard_map/ppermute | solution.py:166
  (38 other events, 369.6 us)
